TPU v7x, 128 devices: a whole 4x4x4 slice. The times are simulated.
128 devices in a mesh: lat: 16 (over z_lo, x, core), lon: 8 (over z_hi, y).
Axes of the slice: x: 4, y: 4, z: 4 (z_hi: 2, z_lo: 2; z = z_hi * 2 + z_lo), core: 2. Of those that a mesh axis runs over, the one named last changes fastest.
Arguments:
- inputs: bfloat16 [2, 192, 147456], P(None, 'lat', 'lon'), may hold values from -40 to 40
- cotangent: bfloat16 [2, 192, 147456], P(None, 'lat', 'lon'), may hold values from -4 to 4
- norm_gain: float32 [192], replicated, may hold values from 0.5 to 1.5
- norm_shift: float32 [192], replicated, may hold values from -2 to 2
- w_qkv: bfloat16 [192, 576], replicated, may hold values from -0.4375 to 0.4375
- w_proj: bfloat16 [192, 192], replicated, may hold values from -0.4375 to 0.4375
- bias_table: float32 [32, 6, 3312], P('lat'), may hold values from -4 to 284
Outputs:
- block_out: bfloat16 [2, 192, 147456], P(None, 'lat', 'lon')
- grad_in: bfloat16 [2, 192, 147456], P(None, 'lat', 'lon')
- grad_qkv: float32 [192, 576], replicated
- grad_proj: float32 [192, 192], replicated
- grad_bias: float32 [32, 6, 3312], P('lat')
All inputs are finite; a program needn't handle non-finite values.
Results may differ from a plain program's by a relative error of at most 0.0085.
Values may be sent and summed in bfloat16 or wider, within the bound.
A program may use at most 128 MiB of HBM per device.

v0:
```python
import jax
import jax.numpy as jnp
import numpy as np
from jax import lax
from jax.sharding import PartitionSpec as P

WZ = 2
WLAT = 6
WLON = 12
WIN = 144


def from_behind(value, axis, steps):
    count = lax.axis_size(axis)
    leading, last = (max(0, -steps), min(count, count - steps))
    return lax.ppermute(value, axis, [(source, source + steps) for source in range(leading, last)])


def passed_along(array, axis, by):
    peers = lax.axis_size(axis)
    return lax.ppermute(array, axis, [(i, (i + by) % peers) for i in range(peers)])


def offset_table():
    offsets = np.arange(WLON)[:, None] - np.arange(WLON)[None, :] + WLON - 1
    return offsets.reshape(-1)


def expand_bias(table_row):
    head_count = table_row.shape[0]
    shaped = table_row.reshape(head_count, WZ, WLAT, WZ, WLAT, 2 * WLON - 1)
    picked = jnp.take(shaped, jnp.asarray(offset_table(), jnp.int32), axis=5)
    picked = picked.reshape(head_count, WZ, WLAT, WZ, WLAT, WLON, WLON)
    picked = picked.transpose(0, 1, 2, 5, 3, 4, 6)
    return picked.reshape(head_count, WIN, WIN)


def collapse_bias(grid_grad):
    head_count = grid_grad.shape[0]
    shaped = grid_grad.reshape(head_count, WZ, WLAT, WLON, WZ, WLAT, WLON)
    shaped = shaped.transpose(0, 1, 2, 4, 5, 3, 6).reshape(
        head_count, WZ * WLAT * WZ * WLAT, WLON * WLON
    )
    onehot = jnp.asarray(offset_table()[:, None] == np.arange(2 * WLON - 1)[None, :], jnp.float32)
    summed = jnp.einsum("hpe,ef->hpf", shaped, onehot, precision=lax.Precision.HIGHEST)
    return summed.reshape(head_count, -1)


def window_pass(
    band_tokens, band_cotan, key_valid, table_row, norm_gain, norm_shift, w_qkv, w_proj
):
    levels, band_rows, width, channels = band_tokens.shape
    windows = width // WLON
    head_count = table_row.shape[0]
    head_dim = channels // head_count
    f32 = jnp.float32

    def to_windows(field_in):
        shaped = field_in.reshape(levels, band_rows, windows, WLON, channels).transpose(
            2, 0, 1, 3, 4
        )
        return shaped.reshape(windows * WIN, channels)

    def from_windows(field_in):
        shaped = field_in.reshape(windows, levels, band_rows, WLON, channels).transpose(
            1, 2, 0, 3, 4
        )
        return shaped.reshape(levels, band_rows, width, channels)

    tokens = to_windows(band_tokens).astype(f32)
    cotan_rows = to_windows(band_cotan)
    center = tokens - jnp.mean(tokens, axis=1, keepdims=True)
    inv_std = lax.rsqrt(jnp.mean(center * center, axis=1, keepdims=True) + 1e-05)
    normed = center * inv_std
    hidden = (normed * norm_gain + norm_shift).astype(jnp.bfloat16)
    packed = jnp.dot(hidden, w_qkv, preferred_element_type=f32).astype(jnp.bfloat16)
    packed = packed.reshape(windows, WIN, 3, head_count, head_dim)
    queries, key_block, values = (packed[:, :, 0], packed[:, :, 1], packed[:, :, 2])
    score_scale = head_dim ** (-0.5)
    key_mask = jnp.broadcast_to(key_valid[None, :, None], (levels, band_rows, WLON)).reshape(-1)
    scores = jnp.einsum("wqhd,wkhd->whqk", queries, key_block, preferred_element_type=f32)
    scores = scores * score_scale + expand_bias(table_row)[None]
    scores = jnp.where(key_mask[None, None, None, :], scores, -1000000000.0)
    row_peak = jnp.max(scores, axis=-1, keepdims=True)
    weights = jnp.exp(scores - row_peak)
    attn_probs = weights / jnp.sum(weights, axis=-1, keepdims=True)
    probs_low = attn_probs.astype(jnp.bfloat16)
    mixed_out = jnp.einsum("whqk,wkhd->wqhd", probs_low, values, preferred_element_type=f32)
    mixed_out = mixed_out.astype(jnp.bfloat16).reshape(windows * WIN, channels)
    branch = jnp.dot(mixed_out, w_proj, preferred_element_type=f32).astype(jnp.bfloat16)
    grad_two = lax.dot_general(
        mixed_out, cotan_rows, (((0,), (0,)), ((), ())), preferred_element_type=f32
    )
    d_mixed = lax.dot_general(
        cotan_rows, w_proj, (((1,), (1,)), ((), ())), preferred_element_type=f32
    )
    d_mixed = d_mixed.astype(jnp.bfloat16).reshape(windows, WIN, head_count, head_dim)
    d_probs = jnp.einsum("wqhd,wkhd->whqk", d_mixed, values, preferred_element_type=f32)
    d_values = jnp.einsum("whqk,wqhd->wkhd", probs_low, d_mixed, preferred_element_type=f32).astype(
        jnp.bfloat16
    )
    d_scores = attn_probs * (d_probs - jnp.sum(attn_probs * d_probs, axis=-1, keepdims=True))
    table_grad = collapse_bias(jnp.sum(d_scores, axis=0))
    d_scaled = (d_scores * score_scale).astype(jnp.bfloat16)
    d_query = jnp.einsum("whqk,wkhd->wqhd", d_scaled, key_block, preferred_element_type=f32)
    d_keys = jnp.einsum("whqk,wqhd->wkhd", d_scaled, queries, preferred_element_type=f32)
    d_packed = jnp.stack(
        [d_query.astype(jnp.bfloat16), d_keys.astype(jnp.bfloat16), d_values], axis=2
    )
    d_packed = d_packed.reshape(windows * WIN, 3 * channels)
    grad_one = lax.dot_general(
        hidden, d_packed, (((0,), (0,)), ((), ())), preferred_element_type=f32
    )
    d_hidden = lax.dot_general(
        d_packed, w_qkv, (((1,), (1,)), ((), ())), preferred_element_type=f32
    )
    d_normed = d_hidden * norm_gain
    d_tokens = inv_std * (
        d_normed
        - jnp.mean(d_normed, axis=1, keepdims=True)
        - normed * jnp.mean(d_normed * normed, axis=1, keepdims=True)
    )
    return (
        from_windows(branch),
        from_windows(d_tokens.astype(jnp.bfloat16)),
        table_grad,
        grad_one,
        grad_two,
    )


def on_device(inputs, cotangent, norm_gain, norm_shift, w_qkv, w_proj, bias_table):
    levels, rows_own, flat_cols = inputs.shape
    channels = norm_gain.shape[0]
    cols_own = flat_cols // channels
    half_rows = WLAT // 2
    half_cols = WLON // 2
    lat_index = lax.axis_index("lat")
    lat_count = lax.axis_size("lat")
    grid_in = inputs.reshape(levels, rows_own, cols_own, channels)
    grid_cot = cotangent.reshape(levels, rows_own, cols_own, channels)
    stacked = jnp.stack([grid_in, grid_cot])
    north_strip = from_behind(stacked[:, :, :half_rows], "lat", -1)
    extended = jnp.concatenate([stacked, north_strip], axis=2)
    east_strip = passed_along(extended[:, :, :, :half_cols], "lon", -1)
    framed = jnp.concatenate([extended[:, :, :, half_cols:], east_strip], axis=3)
    padded = jnp.pad(framed, ((0, 0), (0, 0), (half_rows, 0), (0, 0), (0, 0)))
    band_total = (rows_own + 2 * half_rows) // WLAT
    band_stack = padded.reshape(2, levels, band_total, WLAT, cols_own, channels).transpose(
        2, 0, 1, 3, 4, 5
    )
    row_index = jnp.arange(band_total * WLAT, dtype=jnp.int32).reshape(band_total, WLAT)
    key_valid = (row_index >= half_rows) & (
        (row_index < rows_own + half_rows) | (lat_index < lat_count - 1)
    )
    head_count = bias_table.shape[1]
    pos_count = bias_table.shape[2]

    def polar_band(unused):
        branch, d_branch, table_grad, grad_one, grad_two = window_pass(
            band_stack[0, 0],
            band_stack[0, 1],
            key_valid[0],
            bias_table[0],
            norm_gain,
            norm_shift,
            w_qkv,
            w_proj,
        )
        return (jnp.stack([branch, d_branch]), table_grad, grad_one, grad_two)

    def empty_band(unused):
        return (
            jnp.zeros((2, levels, WLAT, cols_own, channels), jnp.bfloat16),
            jnp.zeros((head_count, pos_count), jnp.float32),
            jnp.zeros((channels, 3 * channels), jnp.float32),
            jnp.zeros((channels, channels), jnp.float32),
        )

    first_result, first_table, first_qkv, first_proj = lax.cond(
        lat_index == 0, polar_band, empty_band, 0
    )

    def band_step(totals, band_item):
        band_pair, valid_rows, table_row = band_item
        branch, d_branch, table_grad, grad_one, grad_two = window_pass(
            band_pair[0], band_pair[1], valid_rows, table_row, norm_gain, norm_shift, w_qkv, w_proj
        )
        return (
            (totals[0] + grad_one, totals[1] + grad_two),
            (jnp.stack([branch, d_branch]), table_grad),
        )

    start = (first_qkv, first_proj)
    (raw_qkv, raw_proj), (results, table_grads) = lax.scan(
        band_step, start, (band_stack[1:], key_valid[1:], bias_table)
    )
    results = jnp.concatenate([first_result[None], results], axis=0)
    results = results.transpose(1, 2, 0, 3, 4, 5).reshape(
        2, levels, band_total * WLAT, cols_own, channels
    )
    results = results[:, :, half_rows:]
    west_strip = passed_along(results[:, :, :, cols_own - half_cols :], "lon", 1)
    unshifted = jnp.concatenate([west_strip, results[:, :, :, : cols_own - half_cols]], axis=3)
    south_strip = from_behind(unshifted[:, :, rows_own:], "lat", 1)
    leading = south_strip + unshifted[:, :, :half_rows]
    returned = jnp.concatenate([leading, unshifted[:, :, half_rows:rows_own]], axis=2)
    block_out = (grid_in.astype(jnp.float32) + returned[0].astype(jnp.float32)).astype(jnp.bfloat16)
    grad_in = (grid_cot.astype(jnp.float32) + returned[1].astype(jnp.float32)).astype(jnp.bfloat16)
    table_local = jnp.concatenate([table_grads[0:1] + first_table[None], table_grads[1:]], axis=0)
    table_total = lax.psum(table_local, "lon")
    flat_grads = jnp.concatenate([raw_qkv.reshape(-1), raw_proj.reshape(-1)]).reshape(-1, 128)
    weight_count = flat_grads.size
    table_count = table_total.size * lat_count
    table_local_squares = jnp.sum(table_total * table_total)
    summed = lax.psum(flat_grads, ("lat", "lon"))
    table_squares = lax.psum(table_local_squares, "lat")
    weight_rms = jnp.sqrt(jnp.sum(summed * summed) / weight_count + 1e-06)
    normed_flat = summed / weight_rms
    table_rms = jnp.sqrt(table_squares / table_count + 1e-06)
    flat_vector = normed_flat.reshape(-1)
    qkv_size = channels * 3 * channels
    grad_qkv = flat_vector[:qkv_size].reshape(channels, 3 * channels)
    grad_proj = flat_vector[qkv_size:].reshape(channels, channels)
    grad_bias = table_total / table_rms
    return (
        block_out.reshape(levels, rows_own, flat_cols),
        grad_in.reshape(levels, rows_own, flat_cols),
        grad_qkv,
        grad_proj,
        grad_bias,
    )


def solution(mesh):
    return jax.shard_map(
        on_device,
        mesh=mesh,
        in_specs=(
            P(None, "lat", "lon"),
            P(None, "lat", "lon"),
            P(),
            P(),
            P(),
            P(),
            P("lat", None, None),
        ),
        out_specs=(P(None, "lat", "lon"), P(None, "lat", "lon"), P(), P(), P("lat", None, None)),
        check_vma=False,
    )
```

profile of v0, /device:TPU:1, one launch (start us, length us, event | category | flops | bytes accessed | tf_op | source)
XLA Modules:
  0.0 825.7 jit_solution(11816926227388452956)
XLA Ops:
  16.7 8.7 %collective-permute-done = bf16[2,2,3,96,192]{4,3,1,2,0:T(8,128)(2,1)S(1)} collective-permute-done((bf16[2,2,3,96,192]{4,3,1,2,0:T(8,128)(2,1)S(1)}, bf16[2,2,3,96,192]{4,3,1,2,0:T(8,128)(2,1)S(1)}, u32[]{:S(2)}, u32[]{:S(2)}) %collective-permute-start) | collective-permute-done | bytes 442400 | tf_op jit(solution)/shard_map/ppermute | solution.py:16
  25.4 6.4 collective-permute-start.1
  42.3 348.7 %while.17 = (s32[]{:T(128)}, f32[192,576]{1,0:T(8,128)}, f32[192,192]{1,0:T(8,128)S(1)}, bf16[2,2,2,6,96,192]{5,4,3,0,2,1:T(8,128)(2,1)}, f32[2,6,3312]{2,0,1:T(...) while((s32[]{:T(128)}, f32[192,576]{1,0:T(8,128)}, ...), condition=%wide.region_19.21_spmd.clone, body=%wide.region_10.20_spmd.sunk.clone.sunk | while | flops 1477610880 | bytes 171159168 | solution.py:195
  73.7 19.4 %gather_fusion.1 = f32[144,6,2,6,2,6]{5,4,3,2,1,0:T(2,128)} fusion(f32[6,2,6,2,6,23]{4,3,5,2,1,0:T(2,128)S(1)} %copy.508, s32[1024]{0:T(1024)S(1)} %pad_clamp_fusion.3), kind=kCustom, calls=%fused_computation.1.clone.clone.1 | custom fusion | bytes 995904 | tf_op jit(solution)/shard_map/while/body/eval_jaxpr/jit(_take)/gather | solution.py:32
  93.0 17.8 %copy.509 = f32[6,2,6,2,6,12,12]{6,4,3,5,2,1,0:T(8,128)} copy(f32[6,2,6,2,6,12,12]{4,3,2,1,0,6,5:T(2,128)} %bitcast.282) | data formatting | bytes 995328 | tf_op jit(solution)/shard_map/while/body/eval_jaxpr/transpose | solution.py:34
  116.6 8.3 fusion.200
  131.9 11.4 %fusion.203 = bf16[8,144,1,6,32]{1,4,3,0,2:T(8,128)(2,1)} fusion(bf16[8,144,1,6,32]{1,0,4,3,2:T(8,128)(2,1)S(1)} %copy-done.6, f32[8,6,144,144]{2,3,1,0:T(8,128)} %fusion.202, f32[8,6,144,144]{2,3,1,0:T(8,128)} %copy-done.39, f32[8,6,144]{2,1,0:T(8,128)} %copy-done.41), kind=kOutput, calls=%fused_computation.95.clone.1 | convolution fusion | flops 70896528 | bytes 8875008 | tf_op jit(solution)/shard_map/while/body/eval_jaxpr/whqk,wqhd->wkhd/dot_general | solution.py:106
  143.3 12.3 %fusion.204 = bf16[8,144,1,6,32]{1,4,3,0,2:T(8,128)(2,1)} fusion(bf16[8,144,1,6,32]{1,0,4,3,2:T(8,128)(2,1)S(1)} %copy-done.4, f32[8,6,144,144]{2,3,1,0:T(8,128)} %fusion.202, f32[8,6,144,144]{2,3,1,0:T(8,128)} %copy-done.39, f32[8,6,144]{2,1,0:T(8,128)} %copy-done.41), kind=kOutput, calls=%fused_computation.94.clone.1 | convolution fusion | flops 70896528 | bytes 8875008 | tf_op jit(solution)/shard_map/while/body/eval_jaxpr/whqk,wkhd->wqhd/dot_general | solution.py:105
  182.9 11.0 %fusion.207 = f32[6,144,144]{1,2,0:T(8,128)S(1)} fusion(f32[8,6,144,144]{2,3,1,0:T(8,128)} %fusion.202, f32[8,6,144,144]{2,3,1,0:T(8,128)} %copy-done.39, f32[8,6,144]{2,1,0:T(8,128)S(1)} %copy-done.43), kind=kOutput, calls=%fused_computation.175.clone.1 | output fusion | flops 5854607 | bytes 8487936 | tf_op jit(solution)/shard_map/while/body/eval_jaxpr/sub | solution.py:102
  194.3 5.2 reshape.431
  199.6 8.4 %copy.518 = f32[6,2,6,2,6,12,12]{6,5,4,3,2,1,0:T(8,128)} copy(f32[6,2,6,2,6,12,12]{6,4,3,5,2,1,0:T(8,128)} %bitcast.281) | data formatting | bytes 995328 | tf_op jit(solution)/shard_map/while/body/eval_jaxpr/transpose | solution.py:41
  242.4 19.4 %gather_fusion.1 = f32[144,6,2,6,2,6]{5,4,3,2,1,0:T(2,128)} fusion(f32[6,2,6,2,6,23]{4,3,5,2,1,0:T(2,128)S(1)} %copy.508, s32[1024]{0:T(1024)S(1)} %pad_clamp_fusion.3), kind=kCustom, calls=%fused_computation.1.clone.clone.1 | custom fusion | bytes 995904 | tf_op jit(solution)/shard_map/while/body/eval_jaxpr/jit(_take)/gather | solution.py:32
  261.7 17.8 %copy.509 = f32[6,2,6,2,6,12,12]{6,4,3,5,2,1,0:T(8,128)} copy(f32[6,2,6,2,6,12,12]{4,3,2,1,0,6,5:T(2,128)} %bitcast.282) | data formatting | bytes 995328 | tf_op jit(solution)/shard_map/while/body/eval_jaxpr/transpose | solution.py:34
  279.6 5.1 add.240
  285.4 8.3 fusion.200
  300.7 11.4 %fusion.203 = bf16[8,144,1,6,32]{1,4,3,0,2:T(8,128)(2,1)} fusion(bf16[8,144,1,6,32]{1,0,4,3,2:T(8,128)(2,1)S(1)} %copy-done.6, f32[8,6,144,144]{2,3,1,0:T(8,128)} %fusion.202, f32[8,6,144,144]{2,3,1,0:T(8,128)} %copy-done.39, f32[8,6,144]{2,1,0:T(8,128)} %copy-done.41), kind=kOutput, calls=%fused_computation.95.clone.1 | convolution fusion | flops 70896528 | bytes 8875008 | tf_op jit(solution)/shard_map/while/body/eval_jaxpr/whqk,wqhd->wkhd/dot_general | solution.py:106
  312.1 12.3 %fusion.204 = bf16[8,144,1,6,32]{1,4,3,0,2:T(8,128)(2,1)} fusion(bf16[8,144,1,6,32]{1,0,4,3,2:T(8,128)(2,1)S(1)} %copy-done.4, f32[8,6,144,144]{2,3,1,0:T(8,128)} %fusion.202, f32[8,6,144,144]{2,3,1,0:T(8,128)} %copy-done.39, f32[8,6,144]{2,1,0:T(8,128)} %copy-done.41), kind=kOutput, calls=%fused_computation.94.clone.1 | convolution fusion | flops 70896528 | bytes 8875008 | tf_op jit(solution)/shard_map/while/body/eval_jaxpr/whqk,wkhd->wqhd/dot_general | solution.py:105
  351.8 11.0 %fusion.207 = f32[6,144,144]{1,2,0:T(8,128)S(1)} fusion(f32[8,6,144,144]{2,3,1,0:T(8,128)} %fusion.202, f32[8,6,144,144]{2,3,1,0:T(8,128)} %copy-done.39, f32[8,6,144]{2,1,0:T(8,128)S(1)} %copy-done.43), kind=kOutput, calls=%fused_computation.175.clone.1 | output fusion | flops 5854607 | bytes 8487936 | tf_op jit(solution)/shard_map/while/body/eval_jaxpr/sub | solution.py:102
  368.4 8.4 %copy.518 = f32[6,2,6,2,6,12,12]{6,5,4,3,2,1,0:T(8,128)} copy(f32[6,2,6,2,6,12,12]{6,4,3,5,2,1,0:T(8,128)} %bitcast.281) | data formatting | bytes 995328 | tf_op jit(solution)/shard_map/while/body/eval_jaxpr/transpose | solution.py:41
  405.0 233.8 %all-reduce.6.cloned.1.call-done = f32[2,6,3312]{2,0,1:T(2,128)} async-done(((f32[2,6,3312]{2,0,1:T(2,128)}), f32[2,6,3312]{2,0,1:T(2,128)}) %all-reduce.6.cloned.1.call-update) | async-done | bytes 158992 | tf_op jit(solution)/shard_map/psum | solution.py:211
  640.4 8.5 %collective-permute-start.3 = (bf16[2,2,3,96,192]{4,3,2,1,0:T(8,128)(2,1)}, bf16[2,2,3,96,192]{4,3,2,1,0:T(8,128)(2,1)}, u32[]{:S(2)}, u32[]{:S(2)}) collective-permute-start(bf16[2,2,3,96,192]{4,3,2,1,0:T(8,128)(2,1)} %pad_maximum_fusion.4), channel_id=1, source_target_pairs={{0,8},{8,16},{16,24},{24,32},{32,40},{40,48},{48,56},{56,64},{64,7... | collective-permute-start | bytes 1327112 | tf_op jit(solution)/shard_map/ppermute | solution.py:16
  648.9 27.7 %psum.23 = f32[]{:T(128)} all-reduce(f32[]{:T(128)} %multiply_reduce_fusion.7), channel_id=1, replica_groups=mesh['lat'=16,'lon'=8] {'lat'}, use_global_device_ids=true, to_apply=%region_24.26 | all-reduce | flops 1 | bytes 8 | tf_op jit(solution)/shard_map/psum | solution.py:217
  679.0 114.5 %all-reduce.4.cloned.1.call-done = f32[1152,128]{1,0:T(8,128)} async-done(((f32[1152,128]{1,0:T(8,128)}), f32[1152,128]{1,0:T(8,128)}) %all-reduce.4.cloned.1.call-update) | async-done | bytes 589840 | tf_op jit(solution)/shard_map/psum | solution.py:216
  810.4 8.2 fusion.104
  (291 shorter events, 203.7 us)
Async XLA Ops:
  7.2 631.6 %all-reduce.6.cloned.1.call-start = ((), (), s32[]{:S(2)}) async-start(), calls=%async_computation.1 | async-start | bytes 319488 | tf_op jit(solution)/shard_map/psum | solution.py:211
  13.3 12.1 %collective-permute-start = (bf16[2,2,3,96,192]{4,3,1,2,0:T(8,128)(2,1)S(1)}, bf16[2,2,3,96,192]{4,3,1,2,0:T(8,128)(2,1)S(1)}, u32[]{:S(2)}, u32[]{:S(2)}) collective-permute-start(bf16[2,2,3,96,192]{4,3,1,2,0:T(8,128)(2,1)S(1)} %slice.137), channel_id=1, source_target_pairs={{8,0},{16,8},{24,16},{32,24},{40,32},{48,40},{56,48},{64,56},{72,6... | collective-permute-start | bytes 1327112 | tf_op jit(solution)/shard_map/ppermute | solution.py:16
  25.4 9.6 %collective-permute-start.1 = (bf16[2,2,15,6,192]{4,3,1,2,0:T(8,128)(2,1)S(1)}, bf16[2,2,15,6,192]{4,3,1,2,0:T(8,128)(2,1)S(1)}, u32[]{:S(2)}, u32[]{:S(2)}) collective-permute-start(bf16[2,2,15,6,192]{4,3,1,2,0:T(8,128)(2,1)S(1)} %pad_maximum_fusion.5), channel_id=1, source_target_pairs={{0,7},{1,0},{2,1},{3,2},{4,3},{5,4},{6,5},{7,6},{8,15},{9,8},{10,9... | collective-permute-start | bytes 414728 | tf_op jit(solution)/shard_map/ppermute | solution.py:21
  116.6 8.3 %copy-start.7 = (bf16[8,144,6,32]{1,0,3,2:T(8,128)(2,1)S(1)}, bf16[8,144,6,32]{1,0,3,2:T(8,128)(2,1)}, u32[]{:S(2)}) copy-start(bf16[8,144,6,32]{1,0,3,2:T(8,128)(2,1)} %reshape.423) | copy-start | bytes 1327108 | tf_op jit(solution)/shard_map/while
  131.9 11.4 %copy-start.4 = (bf16[8,144,1,6,32]{1,0,4,3,2:T(8,128)(2,1)S(1)}, bf16[8,144,1,6,32]{1,0,4,3,2:T(8,128)(2,1)}, u32[]{:S(2)}) copy-start(bf16[8,144,1,6,32]{1,0,4,3,2:T(8,128)(2,1)} %copy-done.3) | copy-start | bytes 1327108 | tf_op jit(solution)/shard_map/while
  143.3 12.3 %copy-start.10 = (bf16[8,144,1,6,32]{1,4,3,0,2:T(8,128)(2,1)S(1)}, bf16[8,144,1,6,32]{1,4,3,0,2:T(8,128)(2,1)}, u32[]{:S(2)}) copy-start(bf16[8,144,1,6,32]{1,4,3,0,2:T(8,128)(2,1)} %fusion.203) | copy-start | bytes 1327108 | tf_op jit(solution)/shard_map/while
  157.3 7.1 copy-start.8
  160.4 6.6 copy-start.42
  166.9 7.3 copy-start.1
  178.6 4.3 copy-start.43
  208.0 6.2 copy-start.33
  208.0 7.5 copy-start.14
  285.4 8.3 %copy-start.7 = (bf16[8,144,6,32]{1,0,3,2:T(8,128)(2,1)S(1)}, bf16[8,144,6,32]{1,0,3,2:T(8,128)(2,1)}, u32[]{:S(2)}) copy-start(bf16[8,144,6,32]{1,0,3,2:T(8,128)(2,1)} %reshape.423) | copy-start | bytes 1327108 | tf_op jit(solution)/shard_map/while
  300.7 11.4 %copy-start.4 = (bf16[8,144,1,6,32]{1,0,4,3,2:T(8,128)(2,1)S(1)}, bf16[8,144,1,6,32]{1,0,4,3,2:T(8,128)(2,1)}, u32[]{:S(2)}) copy-start(bf16[8,144,1,6,32]{1,0,4,3,2:T(8,128)(2,1)} %copy-done.3) | copy-start | bytes 1327108 | tf_op jit(solution)/shard_map/while
  312.1 12.3 %copy-start.10 = (bf16[8,144,1,6,32]{1,4,3,0,2:T(8,128)(2,1)S(1)}, bf16[8,144,1,6,32]{1,4,3,0,2:T(8,128)(2,1)}, u32[]{:S(2)}) copy-start(bf16[8,144,1,6,32]{1,4,3,0,2:T(8,128)(2,1)} %fusion.203) | copy-start | bytes 1327108 | tf_op jit(solution)/shard_map/while
  326.1 7.3 copy-start.8
  329.1 6.7 copy-start.42
  335.8 7.3 copy-start.1
  347.5 4.3 copy-start.43
  376.8 6.2 copy-start.33
  376.8 7.5 copy-start.14
  394.7 9.3 %collective-permute-start.2 = (bf16[2,2,15,6,192]{4,3,2,1,0:T(8,128)(2,1)}, bf16[2,2,15,6,192]{4,3,2,1,0:T(8,128)(2,1)S(1)}, u32[]{:S(2)}, u32[]{:S(2)}) collective-permute-start(bf16[2,2,15,6,192]{4,3,2,1,0:T(8,128)(2,1)} %slice.141), channel_id=1, source_target_pairs={{0,1},{1,2},{2,3},{3,4},{4,5},{5,6},{6,7},{7,0},{8,9},{9,10},{10,1... | collective-permute-start | bytes 414728 | tf_op jit(solution)/shard_map/ppermute | solution.py:21
  398.8 394.7 %all-reduce.4.cloned.1.call-start = ((), (), s32[]{:S(2)}) async-start(), calls=%async_computation | async-start | bytes 1179648 | tf_op jit(solution)/shard_map/psum | solution.py:216
  640.4 160.2 %collective-permute-start.3 = (bf16[2,2,3,96,192]{4,3,2,1,0:T(8,128)(2,1)}, bf16[2,2,3,96,192]{4,3,2,1,0:T(8,128)(2,1)}, u32[]{:S(2)}, u32[]{:S(2)}) collective-permute-start(bf16[2,2,3,96,192]{4,3,2,1,0:T(8,128)(2,1)} %pad_maximum_fusion.4), channel_id=1, source_target_pairs={{0,8},{8,16},{16,24},{24,32},{32,40},{40,48},{48,56},{56,64},{64,7... | collective-permute-start | bytes 1327112 | tf_op jit(solution)/shard_map/ppermute | solution.py:16
  (37 other events, 88.9 us)
Sparse Core Ops, SparseCore 0:
  399.0 239.7 all-reduce.5
  644.7 148.7 all-reduce.3
where the time goes:
time: 833 us; the launch traced here: 826 us
  waiting for transfers between devices  362 us (43%)
  local copies, waits for them, and re-layouts  217 us (26%)
  matrix products  90.7 us (11%)
  other arithmetic  80 us (10%)
  blocking collectives  27.7 us (3%)
  starting transfers between devices  18.3 us (2%)
  between operations  16 us (2%)
  loops' own time  13.8 us (2%)
    psum x1, waiting for transfers between devices, on_device(): table_total = lax.psum(table_local, 'lon')  234 us
    psum x1, waiting for transfers between devices, on_device(): summed = lax.psum(flat_grads, ('lat', 'lon'))  114 us
    gather x2, local copies, waits for them, and re-layouts, expand_bias(): picked = jnp.take(shaped, jnp.asarray(offset_table(), jnp.int32), axis=5)  38.7 us
    transpose x2, local copies, waits for them, and re-layouts, expand_bias(): picked = picked.transpose(0, 1, 2, 5, 3, 4, 6)  35.7 us
    psum x1, blocking collectives, on_device(): table_squares = lax.psum(table_local_squares, 'lat')  27.7 us
    dot_general x2, matrix products, window_pass(): jnp.einsum('whqk,wkhd->wqhd', d_scaled, key_block, preferred_element_type...  24.6 us
    dot_general x2, matrix products, window_pass(): jnp.einsum('whqk,wqhd->wkhd', d_scaled, queries, preferred_element_type=f32)  22.8 us
    sub x2, other arithmetic, window_pass(): d_probs - jnp.sum(attn_probs * d_probs, axis=-1, keepdims=True)  22 us
  transfers between devices with their start and end apart: 6, of which 5 were waited for; matrix products, arithmetic and copies ran while one was open for 2% of the time, Pallas kernels for 0%

commit v1 on v0

v1 whole, which is shorter than its diff:
```python
import functools
import math

import jax
import jax.numpy as jnp
import numpy as np
from jax import lax
from jax.experimental import pallas as pl
from jax.experimental.pallas import tpu as pltpu
from jax.sharding import PartitionSpec as P

C = 192
HEADS = 6
HD = 32
WLON = 12
WIN = 144
HALF = 72
SPAN = 23
ROWLEN = 12 * SPAN
ROWPAD = 384
COLS = 96
HALO = 6 * C
WLANES = WLON * C
OWN = COLS * C
FRAME = OWN + HALO
FROWS = 24
QUART = OWN // 4
WPB = 8
POS = 3312
EPS = 1e-5
SCALE = HD**-0.5
LOG2E = math.log2(math.e)
F32 = jnp.float32
BF16 = jnp.bfloat16


def nn(a, b):
    return lax.dot_general(a, b, (((1,), (0,)), ((), ())), preferred_element_type=F32)


def nt(a, b):
    return lax.dot_general(a, b, (((1,), (1,)), ((), ())), preferred_element_type=F32)


def tn(a, b):
    return lax.dot_general(a, b, (((0,), (0,)), ((), ())), preferred_element_type=F32)


def pick_matrix():
    out = np.zeros((WIN, ROWPAD), np.float32)
    for pk in range(6):
        for zk in range(2):
            for lk in range(WLON):
                out[(pk * 2 + zk) * WLON + lk, (zk * 6 + pk) * SPAN + 11 - lk] = 1.0
    return out


def frame_in(own, halo_lat, halo_east, halo_corner, which, frame):
    def chunk(k, _):
        base = pl.multiple_of(k * HALO, HALO)
        for z in range(2):
            frame[z, 0:12, pl.ds(base, HALO)] = own[z, :, pl.ds(base, HALO)].astype(F32)
        return 0

    lax.fori_loop(0, OWN // HALO, chunk, 0)

    def strip(k, _):
        base = pl.multiple_of(k * HALO, HALO)
        rows = halo_lat[:, pl.ds(base, HALO)].astype(F32)
        for q in range(4):
            for z in range(2):
                r = q * 12 + (which * 2 + z) * 3
                frame[z, 12:15, pl.ds(pl.multiple_of(q * QUART + base, HALO), HALO)] = rows[r : r + 3]
        return 0

    lax.fori_loop(0, QUART // HALO, strip, 0)
    east = halo_east[...].astype(F32)
    corner = halo_corner[...].astype(F32)
    for z in range(2):
        r = (which * 2 + z) * 12
        frame[z, 0:12, OWN:FRAME] = east[r : r + 12]
        r = (which * 2 + z) * 3
        frame[z, 12:15, OWN:FRAME] = corner[r : r + 3]


def frame_out(frame, own, ret_lat, ret_east, ret_corner, which):
    def chunk(k, _):
        base = pl.multiple_of(k * HALO, HALO)
        for z in range(2):
            own[z, :, pl.ds(base, HALO)] = frame[z, 0:12, pl.ds(base, HALO)].astype(BF16)
        return 0

    lax.fori_loop(0, OWN // HALO, chunk, 0)


def strips_out(frames, ret_lat, ret_east, ret_corner):
    def strip(k, _):
        base = pl.multiple_of(k * HALO, HALO)
        pieces = []
        for q in range(4):
            for frame in frames:
                for z in range(2):
                    pieces.append(
                        frame[z, 12:15, pl.ds(pl.multiple_of(q * QUART + base, HALO), HALO)]
                    )
        ret_lat[:, pl.ds(base, HALO)] = jnp.concatenate(pieces, axis=0).astype(BF16)
        return 0

    lax.fori_loop(0, QUART // HALO, strip, 0)
    pieces = [frame[z, 0:12, OWN:FRAME] for frame in frames for z in range(2)]
    ret_east[...] = jnp.concatenate(pieces, axis=0).astype(BF16)
    pieces = [frame[z, 12:15, OWN:FRAME] for frame in frames for z in range(2)]
    pieces.append(jnp.zeros((4, HALO), F32))
    ret_corner[...] = jnp.concatenate(pieces, axis=0).astype(BF16)


def windows_in(frame, rows, count, tokens, first):
    def window(w, _):
        base = HALO + w * WLANES
        for z in range(2):
            for m in range(6):
                at = pl.multiple_of(base + m * 2 * C, 128)
                slab = frame[z, rows : rows + 8, pl.ds(at, 2 * C)]
                odd = pltpu.roll(slab[:, 128:384], 192, 1)
                for t in range(2):
                    lanes = slice(t * 128, t * 128 + 128)
                    slots = pl.ds(z * 12 + 2 * m, count, stride=24)
                    tokens[first + w, t, slots, :] = slab[:count, lanes]
                    slots = pl.ds(z * 12 + 2 * m + 1, count, stride=24)
                    tokens[first + w, t, slots, :] = odd[:count, lanes]
        return 0

    lax.fori_loop(0, WPB, window, 0)


def windows_out(frame, rows, count, tokens, first):
    lane = lax.broadcasted_iota(jnp.int32, (8, 128), 1)

    def window(w, _):
        base = HALO + w * WLANES
        for z in range(2):
            for m in range(6):
                at = pl.multiple_of(base + m * 2 * C, 128)
                slots = pl.ds(z * 12 + 2 * m, count, stride=24)
                even = [tokens[first + w, t, slots, :] for t in range(2)]
                slots = pl.ds(z * 12 + 2 * m + 1, count, stride=24)
                odd = [tokens[first + w, t, slots, :] for t in range(2)]
                odd.append(jnp.zeros((8 - count, 256), F32))
                odd = jnp.concatenate([jnp.concatenate(odd[:2], axis=1), odd[2]], axis=0)
                odd = pltpu.roll(odd, 64, 1)
                mid = jnp.where(lane[:count] < 64, even[1], odd[:count, :128])
                frame[z, rows : rows + count, pl.ds(at, 128)] = even[0]
                frame[z, rows : rows + count, pl.ds(at + 128, 128)] = mid
                frame[z, rows : rows + count, pl.ds(at + 256, 128)] = odd[:count, 128:]
        return 0

    lax.fori_loop(0, WPB, window, 0)


def bias_in(table, pick, rows_scratch, shifted, bias):
    for zq in range(2):
        for pq in range(6):
            at = (zq * 6 + pq) * ROWLEN
            part = table[:, at : at + ROWLEN]
            rows_scratch[pq * 2 + zq, 0:12, 0:ROWLEN] = part
    for bh in range(12):
        rows = rows_scratch[:, bh, :]
        rows = jnp.concatenate([rows, jnp.zeros((4, ROWPAD), F32)], axis=0)
        for lq in range(WLON):
            moved = pltpu.roll(rows, (ROWPAD - lq) % ROWPAD, 1) if lq else rows
            for t in range(3):
                shifted[t, pl.ds(lq, 12, stride=12), :] = moved[:12, t * 128 : t * 128 + 128]
        full = jnp.concatenate([shifted[t] for t in range(3)], axis=1)
        high = full.astype(BF16)
        rest = full - high.astype(F32)
        mid = rest.astype(BF16)
        low = (rest - mid.astype(F32)).astype(BF16)
        total = nt(pick, high) + nt(pick, mid) + nt(pick, low)
        bias[bh // HEADS, bh % HEADS] = total * LOG2E


def bias_out(grads, pick, shifted, out):
    for bh in range(12):
        full = grads[bh // HEADS, bh % HEADS].T
        high = full.astype(BF16)
        low = (full - high.astype(F32)).astype(BF16)
        full = nn(high, pick) + nn(low, pick)
        for t in range(3):
            shifted[t] = full[:, t * 128 : t * 128 + 128]
        total = jnp.zeros((16, ROWPAD), F32)
        for lq in range(WLON):
            rows = [shifted[t, pl.ds(lq, 12, stride=12), :] for t in range(3)]
            rows = jnp.concatenate(rows, axis=1)
            rows = jnp.concatenate([rows, jnp.zeros((4, ROWPAD), F32)], axis=0)
            total = total + (pltpu.roll(rows, lq, 1) if lq else rows)
        out[bh] = total


def attend(n, x_ref, g_ref, at, bias, dbias, band, gain, shift, wqkv, wqkv_t, wproj, wproj_t, eye, raw_q, raw_p):
    x = jnp.concatenate([x_ref[at, 0], x_ref[at, 1]], axis=1)[:, :C]
    g = jnp.concatenate([g_ref[at, 0], g_ref[at, 1]], axis=1)[:, :C]
    gb = g.astype(BF16)
    center = x - jnp.mean(x, axis=1, keepdims=True)
    rstd = lax.rsqrt(jnp.mean(center * center, axis=1, keepdims=True) + EPS)
    xn = center * rstd
    h = (xn * gain + shift).astype(BF16)
    qkv = nn(h, wqkv[...]).astype(BF16)
    kv_t = nt(wqkv_t[C:], h).astype(BF16)
    h_t = nt(eye[...], h).astype(BF16)
    do = nn(gb, wproj_t[...]).astype(BF16)
    o_t, dq_t, dks, dvs = [], [], [], []
    for i in range(HEADS):
        at_h = i * HD
        q = qkv[:, at_h : at_h + HD]
        k = qkv[:, C + at_h : C + at_h + HD]
        v = qkv[:, 2 * C + at_h : 2 * C + at_h + HD]
        k_t = kv_t[at_h : at_h + HD]
        v_t = kv_t[C + at_h : C + at_h + HD]
        do_h = do[:, at_h : at_h + HD]
        s = nt(k, q) * (SCALE * LOG2E) + bias[band, i]
        e = jnp.exp2(s - jnp.max(s, axis=0, keepdims=True))
        p = e * (1.0 / jnp.sum(e, axis=0, keepdims=True))
        pb = p.astype(BF16)
        o_t.append(nn(v_t, pb))
        dp = nt(v, do_h)
        dvs.append(nn(pb, do_h))
        ds = p * (dp - jnp.sum(p * dp, axis=0, keepdims=True))
        dbias[band, i] += ds
        dsb = (ds * SCALE).astype(BF16)
        dks.append(nn(dsb, q))
        dq_t.append(nn(k_t, dsb))
    o_t = jnp.concatenate(o_t, axis=0).astype(BF16)
    dq_t = jnp.concatenate(dq_t, axis=0).astype(BF16)
    o = nt(eye[:n, :n], o_t).astype(BF16)
    dq = nt(eye[:n, :n], dq_t).astype(BF16)
    a = nn(o, wproj[...]).astype(BF16)
    raw_p[...] += nn(o_t, gb)
    dk = jnp.concatenate(dks, axis=1).astype(BF16)
    dv = jnp.concatenate(dvs, axis=1).astype(BF16)
    raw_q[:, 0:C] += nn(h_t, dq)
    raw_q[:, C : 2 * C] += nn(h_t, dk)
    raw_q[:, 2 * C :] += nn(h_t, dv)
    dh = nn(dq, wqkv_t[0:C]) + nn(dk, wqkv_t[C : 2 * C]) + nn(dv, wqkv_t[2 * C :])
    dxn = dh * gain
    m1 = jnp.mean(dxn, axis=1, keepdims=True)
    m2 = jnp.mean(dxn * xn, axis=1, keepdims=True)
    dx = (rstd * (dxn - m1 - xn * m2)).astype(BF16)
    x = x + a.astype(F32)
    g = g + dx.astype(F32)
    x_ref[at, 0] = x[:, :128]
    x_ref[at, 1, :, 0:64] = x[:, 128:]
    g_ref[at, 0] = g[:, :128]
    g_ref[at, 1, :, 0:64] = g[:, 128:]


def window_kernel(
    last,
    lat_ref,
    x_own,
    g_own,
    halo_lat,
    halo_east,
    halo_corner,
    gain_ref,
    shift_ref,
    wqkv,
    wqkv_t,
    wproj,
    wproj_t,
    eye,
    pick,
    table,
    x_out,
    g_out,
    ret_lat,
    ret_east,
    ret_corner,
    raw_q,
    raw_p,
    dtable,
    fx,
    fg,
    xw,
    gw,
    xh,
    gh,
    bias,
    dbias,
    bias_h,
    dbias_h,
    rows_scratch,
    shifted,
):
    lat = lat_ref[0]
    first = lat == 0
    final = lat == last
    frame_in(x_own, halo_lat, halo_east, halo_corner, 0, fx)
    frame_in(g_own, halo_lat, halo_east, halo_corner, 1, fg)
    rows_scratch[...] = jnp.zeros_like(rows_scratch)
    bias_in(table, pick[...], rows_scratch, shifted, bias)
    dbias[...] = jnp.zeros_like(dbias)
    raw_q[...] = jnp.zeros_like(raw_q)
    raw_p[...] = jnp.zeros_like(raw_p)
    for band in range(2):
        windows_in(fx, 3 + 6 * band, 6, xw, band * WPB)
        windows_in(fg, 3 + 6 * band, 6, gw, band * WPB)
    gain = gain_ref[...]
    shift = shift_ref[...]
    rest = (gain, shift, wqkv, wqkv_t, wproj, wproj_t, eye, raw_q, raw_p)

    def full(u, _):
        attend(WIN, xw, gw, u, bias, dbias, u // WPB, *rest)
        return 0

    lax.fori_loop(0, jnp.where(final, WPB, 2 * WPB), full, 0)

    def halves(rows, band, lo):
        windows_in(fx, rows, 3, xh, 0)
        windows_in(fg, rows, 3, gh, 0)
        dbias_h[...] = jnp.zeros_like(dbias_h)
        for i in range(HEADS):
            bias_h[0, i] = bias[band, i][lo : lo + HALF, lo : lo + HALF]

        def half(u, _):
            attend(HALF, xh, gh, u, bias_h, dbias_h, 0, *rest)
            return 0

        lax.fori_loop(0, WPB, half, 0)
        zero = jnp.zeros((HALF, HALF), F32)
        for i in range(HEADS):
            part = dbias_h[0, i]
            part = jnp.concatenate([zero, part] if lo else [part, zero], axis=1)
            dbias[band, i, lo : lo + HALF, :] += part

    for band in range(2):
        windows_out(fx, 3 + 6 * band, 6, xw, band * WPB)
        windows_out(fg, 3 + 6 * band, 6, gw, band * WPB)

    @pl.when(first)
    def _():
        halves(0, 0, HALF)
        windows_out(fx, 0, 3, xh, 0)
        windows_out(fg, 0, 3, gh, 0)

    @pl.when(final)
    def _():
        halves(9, 1, 0)
        windows_out(fx, 9, 3, xh, 0)
        windows_out(fg, 9, 3, gh, 0)

    bias_out(dbias, pick[...], shifted, dtable)
    frame_out(fx, x_out, ret_lat, ret_east, ret_corner, 0)
    frame_out(fg, g_out, ret_lat, ret_east, ret_corner, 1)
    strips_out((fx, fg), ret_lat, ret_east, ret_corner)


def run_windows(last, lat, x_own, g_own, halos, gain, shift, wqkv, wproj, table):
    vmem = pl.BlockSpec(memory_space=pltpu.VMEM)
    shape = jax.ShapeDtypeStruct
    return pl.pallas_call(
        functools.partial(window_kernel, last),
        in_specs=[pl.BlockSpec(memory_space=pltpu.SMEM)] + [vmem] * 14,
        out_specs=[vmem] * 8,
        out_shape=[
            shape((2, 12, OWN), BF16),
            shape((2, 12, OWN), BF16),
            shape((48, QUART), BF16),
            shape((48, HALO), BF16),
            shape((16, HALO), BF16),
            shape((C, 3 * C), F32),
            shape((C, C), F32),
            shape((12, 16, ROWPAD), F32),
        ],
        scratch_shapes=[
            pltpu.VMEM((2, FROWS, FRAME), F32),
            pltpu.VMEM((2, FROWS, FRAME), F32),
            pltpu.VMEM((2 * WPB, 2, WIN, 128), F32),
            pltpu.VMEM((2 * WPB, 2, WIN, 128), F32),
            pltpu.VMEM((WPB, 2, HALF, 128), F32),
            pltpu.VMEM((WPB, 2, HALF, 128), F32),
            pltpu.VMEM((2, HEADS, WIN, WIN), F32),
            pltpu.VMEM((2, HEADS, WIN, WIN), F32),
            pltpu.VMEM((1, HEADS, HALF, HALF), F32),
            pltpu.VMEM((1, HEADS, HALF, HALF), F32),
            pltpu.VMEM((12, 16, ROWPAD), F32),
            pltpu.VMEM((3, WIN, 128), F32),
        ],
        compiler_params=pltpu.CompilerParams(vmem_limit_bytes=56 * 2**20),
        name="windows",
    )(
        lat.reshape(1),
        x_own,
        g_own,
        *halos,
        gain.reshape(1, C),
        shift.reshape(1, C),
        wqkv,
        wqkv.T,
        wproj,
        wproj.T,
        jnp.eye(C, dtype=BF16),
        jnp.asarray(pick_matrix(), BF16),
        table.reshape(2 * HEADS, POS),
    )


def on_device(inputs, cotangent, norm_gain, norm_shift, w_qkv, w_proj, bias_table):
    lat = lax.axis_index("lat")
    lats = lax.axis_size("lat")
    lons = lax.axis_size("lon")

    def north(v):
        return lax.ppermute(v, "lat", [(i + 1, i) for i in range(lats - 1)])

    def south(v):
        return lax.ppermute(v, "lat", [(i, i + 1) for i in range(lats - 1)])

    def along(v, by):
        return lax.ppermute(v, "lon", [(i, (i + by) % lons) for i in range(lons)])

    stacked = jnp.stack([inputs, cotangent])
    strip = stacked[:, :, :3].reshape(12, 4, QUART).transpose(1, 0, 2).reshape(48, QUART)
    halo_lat = north(strip)
    halo_east = along(stacked[:, :, :, :HALO].reshape(48, HALO), -1)
    corner = jnp.pad(strip[:12, :HALO], ((0, 4), (0, 0)))
    halo_corner = along(north(corner), -1)
    x_out, g_out, ret_lat, ret_east, ret_corner, raw_q, raw_p, dtable = run_windows(
        lats - 1,
        lat,
        inputs,
        cotangent,
        (halo_lat, halo_east, halo_corner),
        norm_gain,
        norm_shift,
        w_qkv,
        w_proj,
        bias_table,
    )
    got_lat = south(ret_lat).reshape(4, 2, 2, 3, QUART).transpose(1, 2, 3, 0, 4)
    got_lat = got_lat.reshape(2, 2, 3, OWN)
    got_east = along(ret_east, 1).reshape(2, 2, 12, HALO)
    got_corner = along(south(ret_corner), 1)[:12].reshape(2, 2, 3, HALO)
    own = jnp.stack([x_out, g_out])
    rows = jnp.where(lat == 0, own[:, :, :3], got_lat)
    corner = jnp.where(lat == 0, got_east[:, :, :3], got_corner)
    rows = jnp.concatenate([corner, rows[..., HALO:]], axis=3)
    below = jnp.concatenate([got_east[:, :, 3:], own[:, :, 3:, HALO:]], axis=3)
    own = jnp.concatenate([rows, below], axis=2)
    table = dtable[:, :12, :ROWLEN].reshape(2, HEADS, 6, 2, ROWLEN).transpose(0, 1, 3, 2, 4)
    table = lax.psum(table.reshape(2, HEADS, POS), "lon")
    raw_q, raw_p = lax.psum((raw_q, raw_p), ("lat", "lon"))
    squares = lax.psum(jnp.sum(table * table), "lat")
    rms = jnp.sqrt((jnp.sum(raw_q * raw_q) + jnp.sum(raw_p * raw_p)) / (4 * C * C) + 1e-6)
    table_rms = jnp.sqrt(squares / (table.size * lats) + 1e-6)
    return own[0], own[1], raw_q / rms, raw_p / rms, table / table_rms


def solution(mesh):
    return jax.shard_map(
        on_device,
        mesh=mesh,
        in_specs=(
            P(None, "lat", "lon"),
            P(None, "lat", "lon"),
            P(),
            P(),
            P(),
            P(),
            P("lat", None, None),
        ),
        out_specs=(P(None, "lat", "lon"), P(None, "lat", "lon"), P(), P(), P("lat", None, None)),
        check_vma=False,
    )
```

time: 833 us -> 379 us (0.45)
  local copies, waits for them, and re-layouts: 217 us -> 14.2 us
  waiting for transfers between devices: 362 us -> 208 us
  matrix products: 90.7 us -> 0 us
  Pallas kernels: 0 us -> 72.3 us
  other arithmetic: 80 us -> 14.4 us
  loops' own time: 13.8 us -> 0 us
    psum x2, waiting for transfers between devices: 348 us -> 180 us  [the longest x1 119 us: on_device(): raw_q, raw_p = lax.psum((raw_q, raw_p), ('lat', 'lon'))]
    dot_general x26 -> x0, matrix products: 90.7 us -> none  [the longest x2 24.6 us: window_pass(): jnp.einsum('whqk,wkhd->wqhd', d_scaled, key_block, preferred_element_type...]
    pallas_call x0 -> x1, Pallas kernels: none -> 72.3 us  [run_windows(): pl.pallas_call(functools.partial(window_kernel, last), in_specs=[pl.Block...]
    transpose x10 -> x1, local copies, waits for them, and re-layouts: 55.2 us -> 0.08 us  [on_device(): stacked[:, :, :3].reshape(12, 4, QUART).transpose(1, 0, 2)]
    reshape x26 -> x12, local copies, waits for them, and re-layouts: 55.3 us -> 4.43 us  [the longest x2 1.12 us: on_device(): dtable[:, :12, :ROWLEN].reshape(2, HEADS, 6, 2, ROWLEN)]
    gather x2 -> x0, local copies, waits for them, and re-layouts: 38.7 us -> none  [expand_bias(): picked = jnp.take(shaped, jnp.asarray(offset_table(), jnp.int32), axis=5)]
    sub x4 -> x0, other arithmetic: 38.5 us -> none  [the longest x2 22 us: window_pass(): d_probs - jnp.sum(attn_probs * d_probs, axis=-1, keepdims=True)]
    convert_element_type x18 -> x0, local copies, waits for them, and re-layouts: 17.6 us -> none  [the longest x6 5.93 us: window_pass(): tokens = to_windows(band_tokens).astype(f32)]
  transfers between devices with their start and end apart: 6 -> 10, of which waited for: 5 -> 4; matrix products, arithmetic and copies ran while one was open for 2% -> 4% of each run, Pallas kernels for 0% -> 0%
where the time goes in v1:
time: 379 us
  waiting for transfers between devices  208 us (55%)
  Pallas kernels  72.3 us (19%)
  blocking collectives  32.7 us (9%)
  starting transfers between devices  20.8 us (5%)
  between operations  16.4 us (4%)
  other arithmetic  14.4 us (4%)
  local copies, waits for them, and re-layouts  14.2 us (4%)
    psum x1, waiting for transfers between devices, on_device(): raw_q, raw_p = lax.psum((raw_q, raw_p), ('lat', 'lon'))  119 us
    pallas_call x1, Pallas kernels, run_windows(): pl.pallas_call(functools.partial(window_kernel, last), in_specs=[pl.Block...  72.3 us
    psum x1, waiting for transfers between devices, on_device(): table = lax.psum(table.reshape(2, HEADS, POS), 'lon')  61.2 us
    psum x1, blocking collectives, on_device(): squares = lax.psum(jnp.sum(table * table), 'lat')  32.7 us
    ppermute x2, waiting for transfers between devices, south(): return lax.ppermute(v, 'lat', [(i, i + 1) for i in range(lats - 1)])  22.7 us
    ppermute x4, starting transfers between devices, along(): return lax.ppermute(v, 'lon', [(i, (i + by) % lons) for i in range(lons)])  11.5 us
    unnamed x29, local copies, waits for them, and re-layouts  9.15 us
  transfers between devices with their start and end apart: 10, of which 4 were waited for; matrix products, arithmetic and copies ran while one was open for 4% of the time, Pallas kernels for 0%

profile of v1, /device:TPU:1, one launch (start us, length us, event | category | flops | bytes accessed | tf_op | source)
XLA Modules:
  0.0 378.6 jit_solution(13851674259674382534)
XLA Ops:
  7.2 1.7 pad_maximum_fusion.1
  10.0 3.3 collective-permute-start
  13.3 1.9 collective-permute-start.2
  15.5 6.2 %collective-permute-start.1 = (bf16[48,1152]{1,0:T(8,128)(2,1)S(1)}, bf16[48,1152]{1,0:T(8,128)(2,1)S(1)}, u32[]{:S(2)}, u32[]{:S(2)}) collective-permute-start(bf16[48,1152]{1,0:T(8,128)(2,1)S(1)} %reshape.52), channel_id=1, source_target_pairs={{0,7},{1,0},{2,1},{3,2},{4,3},{5,4},{6,5},{7,6},{8,15},{9,8},{10,9... | collective-permute-start | bytes 331784 | tf_op jit(solution)/shard_map/ppermute | solution.py:419
  21.7 5.2 %collective-permute-start.3 = (bf16[16,1152]{1,0:T(8,128)(2,1)S(1)}, bf16[16,1152]{1,0:T(8,128)(2,1)S(1)}, u32[]{:S(2)}, u32[]{:S(2)}) collective-permute-start(bf16[16,1152]{1,0:T(8,128)(2,1)S(1)} %collective-permute-done.2), channel_id=1, source_target_pairs={{0,7},{1,0},{2,1},{3,2},{4,3},{5,4},{6,5},{7,6},{8,15},{9,8},{10,9... | collective-permute-start | bytes 110600 | tf_op jit(solution)/shard_map/ppermute | solution.py:419
  27.6 1.3 copy.29.x_own
  28.9 1.3 copy.30.g_own
  33.4 72.3 %windows.1 = (bf16[2,12,18432]{2,1,0:T(8,128)(2,1)}, bf16[2,12,18432]{2,1,0:T(8,128)(2,1)}, bf16[48,4608]{1,0:T(8,128)(2,1)}, bf16[48,1152]{1,0:T(8,128)(2,1)}, ...) custom-call(s32[1]{0:T(128)} %bitcast.lat_ref, ...), custom_call_target="tpu_custom_call" | custom-call | tf_op jit(solution)/shard_map/windows/pallas_call | solution.py:360
  105.7 1.1 reshape.60
  107.9 2.0 collective-permute-start.5
  109.9 22.7 %collective-permute-done.5 = bf16[16,1152]{1,0:T(8,128)(2,1)S(1)} collective-permute-done((bf16[16,1152]{1,0:T(8,128)(2,1)}, bf16[16,1152]{1,0:T(8,128)(2,1)S(1)}, u32[]{:S(2)}, u32[]{:S(2)}) %collective-permute-start.5) | collective-permute-done | bytes 36896 | tf_op jit(solution)/shard_map/ppermute | solution.py:416
  132.7 1.9 collective-permute-start.7
  134.6 5.2 %collective-permute-done.6 = bf16[16,1152]{1,0:T(8,128)(2,1)S(1)} collective-permute-done((bf16[16,1152]{1,0:T(8,128)(2,1)S(1)}, bf16[16,1152]{1,0:T(8,128)(2,1)S(1)}, u32[]{:S(2)}, u32[]{:S(2)}) %collective-permute-start.6) | collective-permute-done | bytes 36896 | tf_op jit(solution)/shard_map/ppermute | solution.py:419
  140.5 61.2 %all-reduce.5.cloned.1.call-done = f32[2,6,3312]{2,0,1:T(2,128)} async-done(((f32[2,6,3312]{2,0,1:T(2,128)}), f32[2,6,3312]{2,0,1:T(2,128)}) %all-reduce.5.cloned.1.call-update) | async-done | bytes 158992 | tf_op jit(solution)/shard_map/psum | solution.py:450
  201.6 1.7 multiply_reduce_fusion.2
  203.3 32.7 %psum.31 = f32[]{:T(128)} all-reduce(f32[]{:T(128)} %multiply_reduce_fusion.2), channel_id=1, replica_groups=mesh['lat'=16,'lon'=8] {'lat'}, use_global_device_ids=true, to_apply=%region_6.7 | all-reduce | flops 1 | bytes 8 | tf_op jit(solution)/shard_map/psum | solution.py:452
  236.7 1.6 broadcast_divide_fusion.2
  238.3 118.8 %all-reduce.7.cloned.1.call-done = (f32[192,576]{1,0:T(8,128)}, f32[192,192]{1,0:T(8,128)}) async-done(((f32[192,576]{1,0:T(8,128)}, f32[192,192]{1,0:T(8,128)}), (f32[192,576]{1,0:T(8,128)}, f32[192,192]{1,0:T(8,128)})) %all-reduce.7.cloned.1.call-update) | async-done | bytes 589840 | tf_op jit(solution)/shard_map/psum | solution.py:451
  357.1 1.8 multiply_reduce_fusion
  358.9 1.7 multiply_reduce_fusion.1
  362.0 1.6 broadcast_divide_fusion.1
  363.6 1.8 broadcast_divide_fusion
  368.1 1.8 copy.34
  369.9 1.8 copy.35
  (60 shorter events, 9.5 us)
Async XLA Ops:
  7.2 194.5 %all-reduce.5.cloned.1.call-start = ((), (), s32[]{:S(2)}) async-start(), calls=%async_computation | async-start | bytes 319488 | tf_op jit(solution)/shard_map/psum | solution.py:450
  8.9 6.3 %copy-start = (bf16[2,12,18432]{2,0,1:T(2,128)(2,1)S(1)}, bf16[2,12,18432]{2,0,1:T(2,128)(2,1)}, u32[]{:S(2)}) copy-start(bf16[2,12,18432]{2,0,1:T(2,128)(2,1)} %param.8) | copy-start | bytes 2654212
  8.9 6.3 %copy-start.1 = (bf16[2,12,18432]{2,0,1:T(2,128)(2,1)S(1)}, bf16[2,12,18432]{2,0,1:T(2,128)(2,1)}, u32[]{:S(2)}) copy-start(bf16[2,12,18432]{2,0,1:T(2,128)(2,1)} %param.9) | copy-start | bytes 2654212
  10.0 22.6 %collective-permute-start = (bf16[48,4608]{1,0:T(8,128)(2,1)S(1)}, bf16[48,4608]{1,0:T(8,128)(2,1)S(1)}, u32[]{:S(2)}, u32[]{:S(2)}) collective-permute-start(bf16[48,4608]{1,0:T(8,128)(2,1)S(1)} %reshape.51), channel_id=1, source_target_pairs={{8,0},{16,8},{24,16},{32,24},{40,32},{48,40},{56,48},{64,56},{72,6... | collective-permute-start | bytes 1327112 | tf_op jit(solution)/shard_map/ppermute | solution.py:413
  13.3 8.3 %collective-permute-start.2 = (bf16[16,1152]{1,0:T(8,128)(2,1)S(1)}, bf16[16,1152]{1,0:T(8,128)(2,1)S(1)}, u32[]{:S(2)}, u32[]{:S(2)}) collective-permute-start(bf16[16,1152]{1,0:T(8,128)(2,1)S(1)} %pad.4), channel_id=1, source_target_pairs={{8,0},{16,8},{24,16},{32,24},{40,32},{48,40},{56,48},{64,56},{72,6... | collective-permute-start | bytes 110600 | tf_op jit(solution)/shard_map/ppermute | solution.py:413
  15.4 14.8 %copy-start.7 = (f32[2,6,3312]{2,0,1:T(2,128)S(1)}, f32[2,6,3312]{2,0,1:T(2,128)}, u32[]{:S(2)}) copy-start(f32[2,6,3312]{2,0,1:T(2,128)} %param.14) | copy-start | bytes 476932
  15.5 17.1 %collective-permute-start.1 = (bf16[48,1152]{1,0:T(8,128)(2,1)S(1)}, bf16[48,1152]{1,0:T(8,128)(2,1)S(1)}, u32[]{:S(2)}, u32[]{:S(2)}) collective-permute-start(bf16[48,1152]{1,0:T(8,128)(2,1)S(1)} %reshape.52), channel_id=1, source_target_pairs={{0,7},{1,0},{2,1},{3,2},{4,3},{5,4},{6,5},{7,6},{8,15},{9,8},{10,9... | collective-permute-start | bytes 331784 | tf_op jit(solution)/shard_map/ppermute | solution.py:419
  21.7 10.9 %collective-permute-start.3 = (bf16[16,1152]{1,0:T(8,128)(2,1)S(1)}, bf16[16,1152]{1,0:T(8,128)(2,1)S(1)}, u32[]{:S(2)}, u32[]{:S(2)}) collective-permute-start(bf16[16,1152]{1,0:T(8,128)(2,1)S(1)} %collective-permute-done.2), channel_id=1, source_target_pairs={{0,7},{1,0},{2,1},{3,2},{4,3},{5,4},{6,5},{7,6},{8,15},{9,8},{10,9... | collective-permute-start | bytes 110600 | tf_op jit(solution)/shard_map/ppermute | solution.py:419
  27.5 3.4 copy-start.4
  27.6 4.2 %copy-start.6 = (bf16[192,192]{1,0:T(8,128)(2,1)S(1)}, bf16[192,192]{1,0:T(8,128)(2,1)}, u32[]{:S(2)}) copy-start(bf16[192,192]{1,0:T(8,128)(2,1)} %wproj.1) | copy-start | bytes 221188
  32.5 0.6 copy-start.10
  32.5 0.6 copy-start.9
  32.6 0.8 copy-start.5
  107.8 249.4 %all-reduce.7.cloned.1.call-start = ((), (), s32[]{:S(2)}) async-start(), calls=%async_computation.1 | async-start | bytes 1376256 | tf_op jit(solution)/shard_map/psum | solution.py:451
  107.8 32.0 %collective-permute-start.4 = (bf16[48,1152]{1,0:T(8,128)(2,1)}, bf16[48,1152]{1,0:T(8,128)(2,1)S(1)}, u32[]{:S(2)}, u32[]{:S(2)}) collective-permute-start(bf16[48,1152]{1,0:T(8,128)(2,1)} %get-tuple-element.13), channel_id=1, source_target_pairs={{0,1},{1,2},{2,3},{3,4},{4,5},{5,6},{6,7},{7,0},{8,9},{9,10},{10,1... | collective-permute-start | bytes 331784 | tf_op jit(solution)/shard_map/ppermute | solution.py:419
  107.9 24.8 %collective-permute-start.5 = (bf16[16,1152]{1,0:T(8,128)(2,1)}, bf16[16,1152]{1,0:T(8,128)(2,1)S(1)}, u32[]{:S(2)}, u32[]{:S(2)}) collective-permute-start(bf16[16,1152]{1,0:T(8,128)(2,1)} %get-tuple-element.14), channel_id=1, source_target_pairs={{0,8},{8,16},{16,24},{24,32},{32,40},{40,48},{48,56},{56,64},{64,7... | collective-permute-start | bytes 110600 | tf_op jit(solution)/shard_map/ppermute | solution.py:416
  132.6 7.1 %collective-permute-start.6 = (bf16[16,1152]{1,0:T(8,128)(2,1)S(1)}, bf16[16,1152]{1,0:T(8,128)(2,1)S(1)}, u32[]{:S(2)}, u32[]{:S(2)}) collective-permute-start(bf16[16,1152]{1,0:T(8,128)(2,1)S(1)} %collective-permute-done.5), channel_id=1, source_target_pairs={{0,1},{1,2},{2,3},{3,4},{4,5},{5,6},{6,7},{7,0},{8,9},{9,10},{10,1... | collective-permute-start | bytes 110600 | tf_op jit(solution)/shard_map/ppermute | solution.py:419
  132.7 232.8 %collective-permute-start.7 = (bf16[48,4608]{1,0:T(8,128)(2,1)}, bf16[48,4608]{1,0:T(8,128)(2,1)S(1)}, u32[]{:S(2)}, u32[]{:S(2)}) collective-permute-start(bf16[48,4608]{1,0:T(8,128)(2,1)} %get-tuple-element.17), channel_id=1, source_target_pairs={{0,8},{8,16},{16,24},{24,32},{32,40},{40,48},{48,56},{56,64},{64,7... | collective-permute-start | bytes 1327112 | tf_op jit(solution)/shard_map/ppermute | solution.py:416
  358.9 7.5 %copy-start.2 = (bf16[2,12,18432]{2,1,0:T(8,128)(2,1)S(1)}, bf16[2,12,18432]{2,1,0:T(8,128)(2,1)}, u32[]{:S(2)}) copy-start(bf16[2,12,18432]{2,1,0:T(8,128)(2,1)} %get-tuple-element.15) | copy-start | bytes 2654212
  358.9 7.5 %copy-start.3 = (bf16[2,12,18432]{2,1,0:T(8,128)(2,1)S(1)}, bf16[2,12,18432]{2,1,0:T(8,128)(2,1)}, u32[]{:S(2)}) copy-start(bf16[2,12,18432]{2,1,0:T(8,128)(2,1)} %get-tuple-element.16) | copy-start | bytes 2654212
  366.4 0.8 copy-start.8
Sparse Core Ops, SparseCore 0:
  107.9 93.6 all-reduce.4
  207.9 149.2 all-reduce.6

commit v2 on v1

--- a/solution.py
+++ b/solution.py
@@ -27,6 +27,12 @@
 QUART = OWN // 4
 WPB = 8
 POS = 3312
+TABLE = 4096
+WCHUNK = 12 * 768 // 8
+TCHUNK = TABLE // 8
+CHUNK = WCHUNK + TCHUNK
+TILES = WCHUNK // 128
+MESH = pl.DeviceIdType.MESH
 EPS = 1e-5
 SCALE = HD**-0.5
 LOG2E = math.log2(math.e)
@@ -179,7 +185,8 @@
         bias[bh // HEADS, bh % HEADS] = total * LOG2E
 
 
-def bias_out(grads, pick, shifted, out):
+def bias_out(grads, pick, shifted, rows_scratch, out):
+    rows_scratch[...] = jnp.zeros_like(rows_scratch)
     for bh in range(12):
         full = grads[bh // HEADS, bh % HEADS].T
         high = full.astype(BF16)
@@ -193,7 +200,10 @@
             rows = jnp.concatenate(rows, axis=1)
             rows = jnp.concatenate([rows, jnp.zeros((4, ROWPAD), F32)], axis=0)
             total = total + (pltpu.roll(rows, lq, 1) if lq else rows)
-        out[bh] = total
+        rows_scratch[:, bh, :] = total[:12]
+    parts = [rows_scratch[pq * 2 + zq][:, :ROWLEN] for zq in range(2) for pq in range(6)]
+    parts.append(jnp.zeros((16, TABLE - POS), F32))
+    out[...] = jnp.concatenate(parts, axis=1)
 
 
 def attend(n, x_ref, g_ref, at, bias, dbias, band, gain, shift, wqkv, wqkv_t, wproj, wproj_t, eye, raw_q, raw_p):
@@ -348,7 +358,7 @@
         windows_out(fx, 9, 3, xh, 0)
         windows_out(fg, 9, 3, gh, 0)
 
-    bias_out(dbias, pick[...], shifted, dtable)
+    bias_out(dbias, pick[...], shifted, rows_scratch, dtable)
     frame_out(fx, x_out, ret_lat, ret_east, ret_corner, 0)
     frame_out(fg, g_out, ret_lat, ret_east, ret_corner, 1)
     strips_out((fx, fg), ret_lat, ret_east, ret_corner)
@@ -369,7 +379,7 @@
             shape((16, HALO), BF16),
             shape((C, 3 * C), F32),
             shape((C, C), F32),
-            shape((12, 16, ROWPAD), F32),
+            shape((16, TABLE), F32),
         ],
         scratch_shapes=[
             pltpu.VMEM((2, FROWS, FRAME), F32),
@@ -404,55 +414,451 @@
     )
 
 
+def copy_to(src, dst, send, recv, lat, lon):
+    return pltpu.make_async_remote_copy(
+        src_ref=src,
+        dst_ref=dst,
+        send_sem=send,
+        recv_sem=recv,
+        device_id=(lat, lon),
+        device_id_type=MESH,
+    )
+
+
+def greet(lat, lon):
+    barrier = pltpu.get_barrier_semaphore()
+    pl.semaphore_signal(barrier, inc=1, device_id=(lat, lon), device_id_type=MESH)
+
+
+def halo_kernel(
+    lats, lons, x, g, halo_lat, halo_east, halo_corner, lat_buf, east_buf, corner_buf, send, recv
+):
+    lat = lax.axis_index("lat")
+    lon = lax.axis_index("lon")
+    west = lax.rem(lon + lons - 1, lons)
+    east = lax.rem(lon + 1, lons)
+    barrier = pltpu.get_barrier_semaphore()
+    greet(lat, east)
+
+    @pl.when(lat < lats - 1)
+    def _():
+        greet(lat + 1, lon)
+        greet(lat + 1, east)
+
+    def strip(k, _):
+        base = pl.multiple_of(k * HALO, HALO)
+        pieces = []
+        for q in range(4):
+            for ref in (x, g):
+                for z in range(2):
+                    lanes = pl.ds(pl.multiple_of(q * QUART + base, HALO), HALO)
+                    pieces.append(ref[z, :, lanes].astype(F32)[:3])
+        lat_buf[:, pl.ds(base, HALO)] = jnp.concatenate(pieces, axis=0).astype(BF16)
+        return 0
+
+    lax.fori_loop(0, QUART // HALO, strip, 0)
+    sides = [ref[z, :, 0:HALO].astype(F32) for ref in (x, g) for z in range(2)]
+    east_buf[...] = jnp.concatenate(sides, axis=0).astype(BF16)
+    corners = [side[:3] for side in sides] + [jnp.zeros((4, HALO), F32)]
+    corner_buf[...] = jnp.concatenate(corners, axis=0).astype(BF16)
+
+    pl.semaphore_wait(barrier, jnp.where(lat > 0, 3, 1))
+    up = copy_to(lat_buf, halo_lat, send.at[0], recv.at[0], lat - 1, lon)
+    side = copy_to(east_buf, halo_east, send.at[1], recv.at[1], lat, west)
+    diag = copy_to(corner_buf, halo_corner, send.at[2], recv.at[2], lat - 1, west)
+
+    @pl.when(lat > 0)
+    def _():
+        up.start()
+        diag.start()
+
+    side.start()
+
+    @pl.when(lat < lats - 1)
+    def _():
+        up.wait_recv()
+        diag.wait_recv()
+
+    @pl.when(lat == lats - 1)
+    def _():
+        halo_lat[...] = jnp.zeros_like(halo_lat)
+        halo_corner[...] = jnp.zeros_like(halo_corner)
+
+    side.wait_recv()
+    side.wait_send()
+
+    @pl.when(lat > 0)
+    def _():
+        up.wait_send()
+        diag.wait_send()
+
+
+def run_halo(lats, lons, x, g):
+    vmem = pl.BlockSpec(memory_space=pltpu.VMEM)
+    shapes = ((48, QUART), (48, HALO), (16, HALO))
+    return pl.pallas_call(
+        functools.partial(halo_kernel, lats, lons),
+        in_specs=[vmem] * 2,
+        out_specs=[vmem] * 3,
+        out_shape=[jax.ShapeDtypeStruct(s, BF16) for s in shapes],
+        scratch_shapes=[pltpu.VMEM(s, BF16) for s in shapes]
+        + [pltpu.SemaphoreType.DMA((3,)), pltpu.SemaphoreType.DMA((3,))],
+        compiler_params=pltpu.CompilerParams(
+            collective_id=0, has_side_effects=True, vmem_limit_bytes=32 * 2**20
+        ),
+        name="halo",
+    )(x, g)
+
+
+def reduce_kernel(
+    lats,
+    lons,
+    ret_lat,
+    ret_east,
+    ret_corner,
+    raw_q,
+    raw_p,
+    dtable,
+    got_lat,
+    got_east,
+    got_corner,
+    summed,
+    mine,
+    parts,
+    parts_in,
+    tiles,
+    tiles_in,
+    joined,
+    ret_send,
+    ret_recv,
+    lon_send,
+    lon_recv,
+    lat_send,
+    lat_recv,
+    tile_send,
+    tile_recv,
+    back_send,
+    back_recv,
+):
+    lat = lax.axis_index("lat")
+    lon = lax.axis_index("lon")
+    west = lax.rem(lon + lons - 1, lons)
+    east = lax.rem(lon + 1, lons)
+    barrier = pltpu.get_barrier_semaphore()
+
+    def greet_lon(d, _):
+        greet(lat, lax.rem(lon + d, lons))
+        return 0
+
+    def greet_lat(d, _):
+        greet(lax.rem(lat + d, lats), lon)
+        return 0
+
+    lax.fori_loop(1, lons, greet_lon, 0)
+    lax.fori_loop(1, lats, greet_lat, 0)
+
+    @pl.when(lat > 0)
+    def _():
+        greet(lat - 1, west)
+
+    raw = jnp.concatenate([raw_q[...], raw_p[...]], axis=1)
+    for j in range(lons):
+        row = []
+        for t in range(TILES):
+            col = j * TILES + t
+            r, c = col // 6 * 16, col % 6 * 128
+            row.append(raw[r : r + 16, c : c + 128])
+        row.append(dtable[:, j * TCHUNK : (j + 1) * TCHUNK])
+        chunk = jnp.concatenate(row, axis=1)
+        mine[j] = chunk
+        parts[j] = chunk.astype(BF16)
+
+    peers = lons - 1 + lats - 1
+    pl.semaphore_wait(barrier, jnp.where(lat < lats - 1, peers + 1, peers))
+
+    down = copy_to(ret_lat, got_lat, ret_send.at[0], ret_recv.at[0], lat + 1, lon)
+    side = copy_to(ret_east, got_east, ret_send.at[1], ret_recv.at[1], lat, east)
+    diag = copy_to(ret_corner, got_corner, ret_send.at[2], ret_recv.at[2], lat + 1, east)
+
+    def to_lon(d):
+        to = lax.rem(lon + d, lons)
+        return copy_to(parts.at[to], parts_in.at[lon], lon_send.at[to], lon_recv.at[lon], lat, to)
+
+    def from_lon(d):
+        at = lax.rem(lon + d, lons)
+        return copy_to(parts.at[at], parts_in.at[at], lon_send.at[at], lon_recv.at[at], lat, at)
+
+    def start_lon(d, _):
+        to_lon(d).start()
+        return 0
+
+    lax.fori_loop(1, lons, start_lon, 0)
+    side.start()
+
+    @pl.when(lat < lats - 1)
+    def _():
+        down.start()
+        diag.start()
+
+    def add_lon(d, total):
+        from_lon(d).wait_recv()
+        return total + parts_in[lax.rem(lon + d, lons)].astype(F32)
+
+    chunk = lax.fori_loop(1, lons, add_lon, mine[lon])
+    table = chunk[:, WCHUNK:]
+    square = jnp.sum(table * table).reshape(1, 1)
+    high = square.astype(BF16).astype(F32)
+    low = (square - high).astype(BF16).astype(F32)
+    row = lax.broadcasted_iota(jnp.int32, (16, 128), 0)
+    pair = jnp.where(row < 8, high, low)
+    for t in range(lats):
+        piece = chunk[:, t * 128 : t * 128 + 128] if t < TILES else jnp.zeros((16, 128), F32)
+        tiles[t] = jnp.concatenate([piece, pair], axis=1).astype(BF16)
+
+    def to_lat(d):
+        to = lax.rem(lat + d, lats)
+        return copy_to(tiles.at[to], tiles_in.at[lat], lat_send.at[to], lat_recv.at[lat], to, lon)
+
+    def from_lat(d):
+        at = lax.rem(lat + d, lats)
+        return copy_to(tiles.at[at], tiles_in.at[at], lat_send.at[at], lat_recv.at[at], at, lon)
+
+    def start_lat(d, _):
+        to_lat(d).start()
+        return 0
+
+    lax.fori_loop(1, lats, start_lat, 0)
+
+    def add_lat(d, total):
+        from_lat(d).wait_recv()
+        return total + tiles_in[lax.rem(lat + d, lats)].astype(F32)
+
+    total = lax.fori_loop(1, lats, add_lat, tiles[lat].astype(F32))
+    square = total[0:1, 128:129] + total[8:9, 128:129]
+    high = square.astype(BF16).astype(F32)
+    low = (square - high).astype(BF16).astype(F32)
+    row = lax.broadcasted_iota(jnp.int32, (16, TCHUNK), 0)
+    table = jnp.where(row == 12, high, jnp.where(row == 13, low, table))
+
+    def to_row(d):
+        to = lax.rem(lat + d, lats)
+        return copy_to(joined.at[lat], joined.at[lat], tile_send.at[to], tile_recv.at[lat], to, lon)
+
+    def from_row(at):
+        return copy_to(joined.at[at], joined.at[at], tile_send.at[at], tile_recv.at[at], at, lon)
+
+    def start_row(d, _):
+        to_row(d).start()
+        return 0
+
+    @pl.when(lat < TILES)
+    def _():
+        joined[lat] = total[:, :128].astype(BF16)
+        lax.fori_loop(1, lats, start_row, 0)
+
+    def wait_row(at, _):
+        @pl.when(at != lat)
+        def _():
+            from_row(at).wait_recv()
+
+        return 0
+
+    lax.fori_loop(0, TILES, wait_row, 0)
+    pieces = [joined[t] for t in range(TILES)] + [table.astype(BF16)]
+    summed[lon] = jnp.concatenate(pieces, axis=1)
+
+    def to_back(d):
+        to = lax.rem(lon + d, lons)
+        return copy_to(summed.at[lon], summed.at[lon], back_send.at[to], back_recv.at[lon], lat, to)
+
+    def from_back(d):
+        at = lax.rem(lon + d, lons)
+        return copy_to(summed.at[at], summed.at[at], back_send.at[at], back_recv.at[at], lat, at)
+
+    def start_back(d, _):
+        to_back(d).start()
+        return 0
+
+    lax.fori_loop(1, lons, start_back, 0)
+
+    def done_lon(d, _):
+        to_lon(d).wait_send()
+        from_back(d).wait_recv()
+        to_back(d).wait_send()
+        return 0
+
+    def done_lat(d, _):
+        to_lat(d).wait_send()
+        return 0
+
+    def done_row(d, _):
+        to_row(d).wait_send()
+        return 0
+
+    lax.fori_loop(1, lons, done_lon, 0)
+    lax.fori_loop(1, lats, done_lat, 0)
+
+    @pl.when(lat < TILES)
+    def _():
+        lax.fori_loop(1, lats, done_row, 0)
+
+    side.wait_send()
+    side.wait_recv()
+
+    @pl.when(lat < lats - 1)
+    def _():
+        down.wait_send()
+        diag.wait_send()
+
+    @pl.when(lat > 0)
+    def _():
+        down.wait_recv()
+        diag.wait_recv()
+
+    @pl.when(lat == 0)
+    def _():
+        got_lat[...] = jnp.zeros_like(got_lat)
+        got_corner[...] = jnp.zeros_like(got_corner)
+
+
+def run_reduce(lats, lons, ret_lat, ret_east, ret_corner, raw_q, raw_p, dtable):
+    vmem = pl.BlockSpec(memory_space=pltpu.VMEM)
+    shapes = ((48, QUART), (48, HALO), (16, HALO), (lons, 16, CHUNK))
+    sems = pltpu.SemaphoreType.DMA
+    return pl.pallas_call(
+        functools.partial(reduce_kernel, lats, lons),
+        in_specs=[vmem] * 6,
+        out_specs=[vmem] * 4,
+        out_shape=[jax.ShapeDtypeStruct(s, BF16) for s in shapes],
+        scratch_shapes=[
+            pltpu.VMEM((lons, 16, CHUNK), F32),
+            pltpu.VMEM((lons, 16, CHUNK), BF16),
+            pltpu.VMEM((lons, 16, CHUNK), BF16),
+            pltpu.VMEM((lats, 16, 256), BF16),
+            pltpu.VMEM((lats, 16, 256), BF16),
+            pltpu.VMEM((TILES, 16, 128), BF16),
+            sems((3,)),
+            sems((3,)),
+            sems((lons,)),
+            sems((lons,)),
+            sems((lats,)),
+            sems((lats,)),
+            sems((lats,)),
+            sems((TILES,)),
+            sems((lons,)),
+            sems((lons,)),
+        ],
+        compiler_params=pltpu.CompilerParams(
+            collective_id=1, has_side_effects=True, vmem_limit_bytes=32 * 2**20
+        ),
+        name="reduce",
+    )(ret_lat, ret_east, ret_corner, raw_q, raw_p, dtable)
+
+
+def finish_kernel(
+    lats,
+    lons,
+    lat_ref,
+    x_own,
+    g_own,
+    got_lat,
+    got_east,
+    got_corner,
+    summed,
+    x_out,
+    g_out,
+    grad_q,
+    grad_p,
+    grad_bias,
+):
+    first = lat_ref[0] == 0
+    east = got_east[...].astype(F32)
+    corner = got_corner[...].astype(F32)
+    for n, (own, out) in enumerate(((x_own, x_out), (g_own, g_out))):
+        for z in range(2):
+            at = n * 2 + z
+            side = east[at * 12 : at * 12 + 12]
+            top = jnp.where(first, side[:3], corner[at * 3 : at * 3 + 3])
+            out[z, :, 0:HALO] = jnp.concatenate([top, side[3:]], axis=0).astype(BF16)
+
+    def strip(k, _):
+        base = pl.multiple_of(k * HALO, HALO)
+        rows = got_lat[:, pl.ds(base, HALO)].astype(F32)
+        for q in range(4):
+            lanes = pl.ds(pl.multiple_of(q * QUART + base, HALO), HALO)
+
+            @pl.when((k > 0) | (q > 0))
+            def _():
+                for n, (own, out) in enumerate(((x_own, x_out), (g_own, g_out))):
+                    for z in range(2):
+                        r = q * 12 + (n * 2 + z) * 3
+                        mine = own[z, :, lanes].astype(F32)
+                        top = jnp.where(first, mine[:3], rows[r : r + 3])
+                        out[z, :, lanes] = jnp.concatenate([top, mine[3:]], axis=0).astype(BF16)
+
+        return 0
+
+    lax.fori_loop(0, QUART // HALO, strip, 0)
+    whole = [summed[j].astype(F32) for j in range(lons)]
+    squares = jnp.zeros((16, 128), F32)
+    table_squares = jnp.zeros((1, 1), F32)
+    cols = []
+    for j in range(lons):
+        for t in range(TILES):
+            piece = whole[j][:, t * 128 : t * 128 + 128]
+            squares = squares + piece * piece
+            cols.append(piece)
+        table_squares = table_squares + whole[j][12:13, WCHUNK : WCHUNK + 1]
+        table_squares = table_squares + whole[j][13:14, WCHUNK : WCHUNK + 1]
+    rms = jnp.sqrt(jnp.sum(squares).reshape(1, 1) / (4 * C * C) + 1e-6)
+    for r in range(12):
+        row = jnp.concatenate(cols[r * 6 : r * 6 + 6], axis=1) / rms
+        grad_q[r * 16 : r * 16 + 16] = row[:, : 3 * C]
+        grad_p[r * 16 : r * 16 + 16] = row[:, 3 * C :]
+    table = jnp.concatenate([part[:12, WCHUNK:] for part in whole], axis=1)
+    table_rms = jnp.sqrt(table_squares / (lats * 2 * HEADS * POS) + 1e-6)
+    grad_bias[...] = table[:, :POS] / table_rms
+
+
+def run_finish(lats, lons, lat, *args):
+    vmem = pl.BlockSpec(memory_space=pltpu.VMEM)
+    shape = jax.ShapeDtypeStruct
+    return pl.pallas_call(
+        functools.partial(finish_kernel, lats, lons),
+        in_specs=[pl.BlockSpec(memory_space=pltpu.SMEM)] + [vmem] * 6,
+        out_specs=[vmem] * 5,
+        out_shape=[
+            shape((2, 12, OWN), BF16),
+            shape((2, 12, OWN), BF16),
+            shape((C, 3 * C), F32),
+            shape((C, C), F32),
+            shape((2 * HEADS, POS), F32),
+        ],
+        compiler_params=pltpu.CompilerParams(vmem_limit_bytes=32 * 2**20),
+        name="finish",
+    )(lat.reshape(1), *args)
+
+
 def on_device(inputs, cotangent, norm_gain, norm_shift, w_qkv, w_proj, bias_table):
     lat = lax.axis_index("lat")
     lats = lax.axis_size("lat")
     lons = lax.axis_size("lon")
-
-    def north(v):
-        return lax.ppermute(v, "lat", [(i + 1, i) for i in range(lats - 1)])
-
-    def south(v):
-        return lax.ppermute(v, "lat", [(i, i + 1) for i in range(lats - 1)])
-
-    def along(v, by):
-        return lax.ppermute(v, "lon", [(i, (i + by) % lons) for i in range(lons)])
-
-    stacked = jnp.stack([inputs, cotangent])
-    strip = stacked[:, :, :3].reshape(12, 4, QUART).transpose(1, 0, 2).reshape(48, QUART)
-    halo_lat = north(strip)
-    halo_east = along(stacked[:, :, :, :HALO].reshape(48, HALO), -1)
-    corner = jnp.pad(strip[:12, :HALO], ((0, 4), (0, 0)))
-    halo_corner = along(north(corner), -1)
-    x_out, g_out, ret_lat, ret_east, ret_corner, raw_q, raw_p, dtable = run_windows(
+    halos = run_halo(lats, lons, inputs, cotangent)
+    x_own, g_own, *sent = run_windows(
         lats - 1,
         lat,
         inputs,
         cotangent,
-        (halo_lat, halo_east, halo_corner),
+        halos,
         norm_gain,
         norm_shift,
         w_qkv,
         w_proj,
         bias_table,
     )
-    got_lat = south(ret_lat).reshape(4, 2, 2, 3, QUART).transpose(1, 2, 3, 0, 4)
-    got_lat = got_lat.reshape(2, 2, 3, OWN)
-    got_east = along(ret_east, 1).reshape(2, 2, 12, HALO)
-    got_corner = along(south(ret_corner), 1)[:12].reshape(2, 2, 3, HALO)
-    own = jnp.stack([x_out, g_out])
-    rows = jnp.where(lat == 0, own[:, :, :3], got_lat)
-    corner = jnp.where(lat == 0, got_east[:, :, :3], got_corner)
-    rows = jnp.concatenate([corner, rows[..., HALO:]], axis=3)
-    below = jnp.concatenate([got_east[:, :, 3:], own[:, :, 3:, HALO:]], axis=3)
-    own = jnp.concatenate([rows, below], axis=2)
-    table = dtable[:, :12, :ROWLEN].reshape(2, HEADS, 6, 2, ROWLEN).transpose(0, 1, 3, 2, 4)
-    table = lax.psum(table.reshape(2, HEADS, POS), "lon")
-    raw_q, raw_p = lax.psum((raw_q, raw_p), ("lat", "lon"))
-    squares = lax.psum(jnp.sum(table * table), "lat")
-    rms = jnp.sqrt((jnp.sum(raw_q * raw_q) + jnp.sum(raw_p * raw_p)) / (4 * C * C) + 1e-6)
-    table_rms = jnp.sqrt(squares / (table.size * lats) + 1e-6)
-    return own[0], own[1], raw_q / rms, raw_p / rms, table / table_rms
+    got = run_reduce(lats, lons, *sent)
+    x_out, g_out, grad_q, grad_p, grad_bias = run_finish(lats, lons, lat, x_own, g_own, *got)
+    return x_out, g_out, grad_q, grad_p, grad_bias.reshape(2, HEADS, POS)
 
 
 def solution(mesh):

time: 379 us -> 163 us (0.43)
  waiting for transfers between devices: 208 us -> 0 us
  Pallas kernels: 72.3 us -> 141 us
  blocking collectives: 32.7 us -> 0 us
  starting transfers between devices: 20.8 us -> 0 us
  between operations: 16.4 us -> 0.75 us
  other arithmetic: 14.4 us -> 0.65 us
  local copies, waits for them, and re-layouts: 14.2 us -> 18.3 us
    psum x2 -> x0, waiting for transfers between devices: 180 us -> none  [the longest x1 119 us: on_device(): raw_q, raw_p = lax.psum((raw_q, raw_p), ('lat', 'lon'))]
    pallas_call x0 -> x3, Pallas kernels: none -> 68.9 us  [the longest x1 52.3 us: run_reduce(): pl.pallas_call(functools.partial(reduce_kernel, lats, lons), in_specs=[vm...]
    psum x1 -> x0, blocking collectives: 32.7 us -> none  [on_device(): squares = lax.psum(jnp.sum(table * table), 'lat')]
    ppermute x8 -> x0, waiting for transfers between devices: 27.9 us -> none  [the longest x2 22.7 us: south(): return lax.ppermute(v, 'lat', [(i, i + 1) for i in range(lats - 1)])]
    ppermute x8 -> x0, starting transfers between devices: 20.7 us -> none  [the longest x4 11.5 us: along(): return lax.ppermute(v, 'lon', [(i, (i + by) % lons) for i in range(lons)])]
    unnamed x29 -> x40, local copies, waits for them, and re-layouts: 9.15 us -> 17.6 us
    reduce_sum x3 -> x0, other arithmetic: 5.17 us -> none  [the longest x1 1.76 us: on_device(): jnp.sum(raw_q * raw_q) + jnp.sum(raw_p * raw_p)]
    div x3 -> x0, other arithmetic: 5.11 us -> none  [on_device(): return (own[0], own[1], raw_q / rms, raw_p / rms, table / table_rms)]
  transfers between devices with their start and end apart: 10 -> 0, of which waited for: 4 -> 0; matrix products, arithmetic and copies ran while one was open for 4% -> 0% of each run, Pallas kernels for 0% -> 0%
where the time goes in v2:
time: 163 us; the launch traced here: 161 us
  Pallas kernels  141 us (87%)
  local copies, waits for them, and re-layouts  18.3 us (11%)
    pallas_call x1, Pallas kernels, run_windows(): pl.pallas_call(functools.partial(window_kernel, last), in_specs=[pl.Block...  72.2 us
    pallas_call x1, Pallas kernels, run_reduce(): pl.pallas_call(functools.partial(reduce_kernel, lats, lons), in_specs=[vm...  52.3 us
    unnamed x40, local copies, waits for them, and re-layouts  17.6 us
    pallas_call x1, Pallas kernels, run_halo(): pl.pallas_call(functools.partial(halo_kernel, lats, lons), in_specs=[vmem...  15.1 us

profile of v2, /device:TPU:1, one launch (start us, length us, event | category | flops | bytes accessed | tf_op | source)
XLA Modules:
  0.0 160.9 jit_solution(9600324529315013143)
XLA Ops:
  0.7 1.7 %copy.26 = bf16[192,192]{0,1:T(8,128)(2,1)} copy(bf16[192,192]{1,0:T(8,128)(2,1)} %wproj.1) | data formatting | bytes 147456 | tf_op args[5]
  2.4 0.7 fusion.eye
  3.0 0.9 copy.27
  4.0 0.7 reshape.29.table
  4.7 0.9 copy.25
  5.6 0.3 copy.28.x.x_own
  6.0 0.3 copy.29.g.g_own
  6.3 15.1 %halo.1 = (bf16[48,4608]{1,0:T(8,128)(2,1)S(1)}, bf16[48,1152]{1,0:T(8,128)(2,1)S(1)}, bf16[16,1152]{1,0:T(8,128)(2,1)S(1)}) custom-call(bf16[2,12,18432]{2,1,0:T(8,128)(2,1)S(1)} %copy.28.x.x_own, bf16[2,12,18432]{2,1,0:T(8,128)(2,1)S(1)} %copy.29.g.g_own), custom_call_target="tpu_custom_call" | custom-call | tf_op jit(solution)/shard_map/halo/pallas_call | solution.py:499
  21.4 0.8 copy-done.5
  22.1 0.6 copy-done.9
  22.8 0.6 copy-done.11
  23.4 72.2 %windows.1 = (bf16[2,12,18432]{2,1,0:T(8,128)(2,1)}, bf16[2,12,18432]{2,1,0:T(8,128)(2,1)}, bf16[48,4608]{1,0:T(8,128)(2,1)}, bf16[48,1152]{1,0:T(8,128)(2,1)}, ...) custom-call(s32[1]{0:T(128)} %bitcast.lat_ref, ...), custom_call_target="tpu_custom_call" | custom-call | tf_op jit(solution)/shard_map/windows/pallas_call | solution.py:370
  95.6 1.1 copy-done.4
  96.8 1.0 copy-done.6
  97.8 0.9 copy-done.7
  98.7 0.9 copy-done.8
  99.6 0.9 copy-done.10
  100.5 0.8 copy-done.12
  101.3 52.3 %reduce.1 = (bf16[48,4608]{1,0:T(8,128)(2,1)S(1)}, bf16[48,1152]{1,0:T(8,128)(2,1)S(1)}, bf16[16,1152]{1,0:T(8,128)(2,1)S(1)}, bf16[8,16,1664]{2,1,0:T(8,128)(2,1)S(1)}) custom-call(bf16[48,4608]{1,0:T(8,128)(2,1)S(1)} %copy-done.6, bf16[48,1152]{1,0:T(8,128)(2,1)S(1)} %copy-done.10, bf16[16,1152]{1,0:T(8,128)(2,1)S(1)} %copy-done.12, ...), custom_call_target="tpu_custom_call" | custom-call | tf_op jit(solution)/shard_map/reduce/pallas_call | solution.py:728
  153.6 1.3 copy-done.3
  154.9 1.6 finish.1
  156.4 1.8 %copy.30 = bf16[2,12,18432]{2,0,1:T(2,128)(2,1)} copy(bf16[2,12,18432]{2,1,0:T(8,128)(2,1)S(1)} %get-tuple-element.50) | data formatting | bytes 1769472
  158.3 0.7 copy.32
  159.0 1.8 %copy.31 = bf16[2,12,18432]{2,0,1:T(2,128)(2,1)} copy(bf16[2,12,18432]{2,1,0:T(8,128)(2,1)S(1)} %get-tuple-element.51) | data formatting | bytes 1769472
  (23 shorter events, 0.2 us)
Async XLA Ops:
  0.6 4.1 %copy-start.13 = (bf16[192,576]{1,0:T(8,128)(2,1)S(1)}, bf16[192,576]{1,0:T(8,128)(2,1)}, u32[]{:S(2)}) copy-start(bf16[192,576]{1,0:T(8,128)(2,1)} %wqkv.1) | copy-start | bytes 663556
  0.6 5.0 %copy-start.14 = (bf16[2,12,18432]{2,0,1:T(2,128)(2,1)S(1)}, bf16[2,12,18432]{2,0,1:T(2,128)(2,1)}, u32[]{:S(2)}) copy-start(bf16[2,12,18432]{2,0,1:T(2,128)(2,1)} %param.8) | copy-start | bytes 2654212
  4.7 1.3 copy-start.15
  6.0 15.4 %copy-start = (bf16[2,12,18432]{2,1,0:T(8,128)(2,1)}, bf16[2,12,18432]{2,1,0:T(8,128)(2,1)S(1)}, u32[]{:S(2)}) copy-start(bf16[2,12,18432]{2,1,0:T(8,128)(2,1)S(1)} %copy.28.x.x_own) | copy-start | bytes 2654212
  6.3 17.1 %copy-start.1 = (bf16[2,12,18432]{2,1,0:T(8,128)(2,1)}, bf16[2,12,18432]{2,1,0:T(8,128)(2,1)S(1)}, u32[]{:S(2)}) copy-start(bf16[2,12,18432]{2,1,0:T(8,128)(2,1)S(1)} %copy.29.g.g_own) | copy-start | bytes 2654212
  21.3 0.8 copy-start.5
  22.1 0.6 copy-start.9
  22.8 0.6 copy-start.11
  95.6 58.0 %copy-start.2 = (bf16[2,12,18432]{2,1,0:T(8,128)(2,1)S(1)}, bf16[2,12,18432]{2,1,0:T(8,128)(2,1)}, u32[]{:S(2)}) copy-start(bf16[2,12,18432]{2,1,0:T(8,128)(2,1)} %get-tuple-element.28.x_own) | copy-start | bytes 2654212
  95.6 1.1 copy-start.4
  96.8 1.0 copy-start.6
  97.8 0.9 copy-start.7
  98.7 0.9 copy-start.8
  99.6 0.9 copy-start.10
  100.5 0.8 copy-start.12
  153.6 1.3 copy-start.3

commit v3 on v2

--- a/solution.py
+++ b/solution.py
@@ -206,61 +206,83 @@
     out[...] = jnp.concatenate(parts, axis=1)
 
 
-def attend(n, x_ref, g_ref, at, bias, dbias, band, gain, shift, wqkv, wqkv_t, wproj, wproj_t, eye, raw_q, raw_p):
-    x = jnp.concatenate([x_ref[at, 0], x_ref[at, 1]], axis=1)[:, :C]
-    g = jnp.concatenate([g_ref[at, 0], g_ref[at, 1]], axis=1)[:, :C]
+def attend(n, x_ref, g_ref, us, bias, dbias, band, gain, shift, wqkv, wqkv_t, wproj, wproj_t, eye, raw_q, raw_p):
+    ws = range(len(us))
+    pairs = [(w, i) for w in ws for i in range(HEADS)]
+
+    def tokens(ref):
+        rows = [jnp.concatenate([ref[u, 0], ref[u, 1]], axis=1) for u in us]
+        return jnp.concatenate(rows, axis=0)[:, :C]
+
+    def split(a):
+        return [a[w * n : (w + 1) * n] for w in ws]
+
+    x = tokens(x_ref)
+    g = tokens(g_ref)
     gb = g.astype(BF16)
     center = x - jnp.mean(x, axis=1, keepdims=True)
     rstd = lax.rsqrt(jnp.mean(center * center, axis=1, keepdims=True) + EPS)
     xn = center * rstd
     h = (xn * gain + shift).astype(BF16)
-    qkv = nn(h, wqkv[...]).astype(BF16)
-    kv_t = nt(wqkv_t[C:], h).astype(BF16)
+    qkv = split(nn(h, wqkv[...]).astype(BF16))
+    kv_t = [nt(wqkv_t[C:], part).astype(BF16) for part in split(h)]
     h_t = nt(eye[...], h).astype(BF16)
-    do = nn(gb, wproj_t[...]).astype(BF16)
-    o_t, dq_t, dks, dvs = [], [], [], []
-    for i in range(HEADS):
-        at_h = i * HD
-        q = qkv[:, at_h : at_h + HD]
-        k = qkv[:, C + at_h : C + at_h + HD]
-        v = qkv[:, 2 * C + at_h : 2 * C + at_h + HD]
-        k_t = kv_t[at_h : at_h + HD]
-        v_t = kv_t[C + at_h : C + at_h + HD]
-        do_h = do[:, at_h : at_h + HD]
-        s = nt(k, q) * (SCALE * LOG2E) + bias[band, i]
-        e = jnp.exp2(s - jnp.max(s, axis=0, keepdims=True))
-        p = e * (1.0 / jnp.sum(e, axis=0, keepdims=True))
-        pb = p.astype(BF16)
-        o_t.append(nn(v_t, pb))
-        dp = nt(v, do_h)
-        dvs.append(nn(pb, do_h))
-        ds = p * (dp - jnp.sum(p * dp, axis=0, keepdims=True))
-        dbias[band, i] += ds
-        dsb = (ds * SCALE).astype(BF16)
-        dks.append(nn(dsb, q))
-        dq_t.append(nn(k_t, dsb))
-    o_t = jnp.concatenate(o_t, axis=0).astype(BF16)
-    dq_t = jnp.concatenate(dq_t, axis=0).astype(BF16)
-    o = nt(eye[:n, :n], o_t).astype(BF16)
-    dq = nt(eye[:n, :n], dq_t).astype(BF16)
+    do = split(nn(gb, wproj_t[...]).astype(BF16))
+
+    def cut(a, base):
+        return [a[w][:, base + i * HD : base + (i + 1) * HD] for w, i in pairs]
+
+    q, k, v = cut(qkv, 0), cut(qkv, C), cut(qkv, 2 * C)
+    k_t = [kv_t[w][i * HD : (i + 1) * HD] for w, i in pairs]
+    v_t = [kv_t[w][C + i * HD : C + (i + 1) * HD] for w, i in pairs]
+    do_h = cut(do, 0)
+    hs = range(len(pairs))
+    o_t, dvs, dks, dq_t = {}, {}, {}, {}
+    for b0 in range(0, len(pairs), 6):
+        grp = range(b0, b0 + 6)
+        s = {i: nt(k[i], q[i]) * (SCALE * LOG2E) + bias[band, pairs[i][1]] for i in grp}
+        dp = {i: nt(v[i], do_h[i]) for i in grp}
+        e = {i: jnp.exp2(s[i] - jnp.max(s[i], axis=0, keepdims=True)) for i in grp}
+        p = {i: e[i] * (1.0 / jnp.sum(e[i], axis=0, keepdims=True)) for i in grp}
+        pb = {i: p[i].astype(BF16) for i in grp}
+        for i in grp:
+            o_t[i] = nn(v_t[i], pb[i])
+        for i in grp:
+            dvs[i] = nn(pb[i], do_h[i])
+        ds = {i: p[i] * (dp[i] - jnp.sum(p[i] * dp[i], axis=0, keepdims=True)) for i in grp}
+        for i in grp:
+            dbias[band, pairs[i][1]] += ds[i]
+        dsb = {i: (ds[i] * SCALE).astype(BF16) for i in grp}
+        for i in grp:
+            dks[i] = nn(dsb[i], q[i])
+        for i in grp:
+            dq_t[i] = nn(k_t[i], dsb[i])
+
+    def join(parts, axis):
+        parts = [[parts[w * HEADS + i] for i in range(HEADS)] for w in ws]
+        return [jnp.concatenate(part, axis=axis).astype(BF16) for part in parts]
+
+    o_t, dq_t = join(o_t, 0), join(dq_t, 0)
+    dk, dv = (jnp.concatenate(join(part, 1), axis=0) for part in (dks, dvs))
+    o = jnp.concatenate([nt(eye[:n, :n], o_t[w]).astype(BF16) for w in ws], axis=0)
+    dq = jnp.concatenate([nt(eye[:n, :n], dq_t[w]).astype(BF16) for w in ws], axis=0)
     a = nn(o, wproj[...]).astype(BF16)
-    raw_p[...] += nn(o_t, gb)
-    dk = jnp.concatenate(dks, axis=1).astype(BF16)
-    dv = jnp.concatenate(dvs, axis=1).astype(BF16)
+    dh = nn(dq, wqkv_t[0:C]) + nn(dk, wqkv_t[C : 2 * C]) + nn(dv, wqkv_t[2 * C :])
+    raw_p[...] += sum(nn(o_t[w], gb[w * n : (w + 1) * n]) for w in ws)
     raw_q[:, 0:C] += nn(h_t, dq)
     raw_q[:, C : 2 * C] += nn(h_t, dk)
     raw_q[:, 2 * C :] += nn(h_t, dv)
-    dh = nn(dq, wqkv_t[0:C]) + nn(dk, wqkv_t[C : 2 * C]) + nn(dv, wqkv_t[2 * C :])
     dxn = dh * gain
     m1 = jnp.mean(dxn, axis=1, keepdims=True)
     m2 = jnp.mean(dxn * xn, axis=1, keepdims=True)
     dx = (rstd * (dxn - m1 - xn * m2)).astype(BF16)
-    x = x + a.astype(F32)
-    g = g + dx.astype(F32)
-    x_ref[at, 0] = x[:, :128]
-    x_ref[at, 1, :, 0:64] = x[:, 128:]
-    g_ref[at, 0] = g[:, :128]
-    g_ref[at, 1, :, 0:64] = g[:, 128:]
+    x = split(x + a.astype(F32))
+    g = split(g + dx.astype(F32))
+    for w, u in enumerate(us):
+        x_ref[u, 0] = x[w][:, :128]
+        x_ref[u, 1, :, 0:64] = x[w][:, 128:]
+        g_ref[u, 0] = g[w][:, :128]
+        g_ref[u, 1, :, 0:64] = g[w][:, 128:]
 
 
 def window_kernel(
@@ -319,10 +341,10 @@
     rest = (gain, shift, wqkv, wqkv_t, wproj, wproj_t, eye, raw_q, raw_p)
 
     def full(u, _):
-        attend(WIN, xw, gw, u, bias, dbias, u // WPB, *rest)
-        return 0
-
-    lax.fori_loop(0, jnp.where(final, WPB, 2 * WPB), full, 0)
+        attend(WIN, xw, gw, [4 * u + r for r in range(4)], bias, dbias, u // (WPB // 4), *rest)
+        return 0
+
+    lax.fori_loop(0, jnp.where(final, WPB // 4, 2 * WPB // 4), full, 0)
 
     def halves(rows, band, lo):
         windows_in(fx, rows, 3, xh, 0)
@@ -332,10 +354,10 @@
             bias_h[0, i] = bias[band, i][lo : lo + HALF, lo : lo + HALF]
 
         def half(u, _):
-            attend(HALF, xh, gh, u, bias_h, dbias_h, 0, *rest)
+            attend(HALF, xh, gh, [4 * u + r for r in range(4)], bias_h, dbias_h, 0, *rest)
             return 0
 
-        lax.fori_loop(0, WPB, half, 0)
+        lax.fori_loop(0, WPB // 4, half, 0)
         zero = jnp.zeros((HALF, HALF), F32)
         for i in range(HEADS):
             part = dbias_h[0, i]

time: 163 us -> 113 us (0.69)
  Pallas kernels: 141 us -> 91.6 us
    pallas_call x1, Pallas kernels: 72.2 us -> 38.8 us  [run_windows(): pl.pallas_call(functools.partial(window_kernel, last), in_specs=[pl.Block...]
    pallas_call x1, Pallas kernels: 52.3 us -> 36.1 us  [run_reduce(): pl.pallas_call(functools.partial(reduce_kernel, lats, lons), in_specs=[vm...]
where the time goes in v3:
time: 113 us; the launch traced here: 111 us
  Pallas kernels  91.6 us (81%)
  local copies, waits for them, and re-layouts  18.3 us (16%)
    pallas_call x1, Pallas kernels, run_windows(): pl.pallas_call(functools.partial(window_kernel, last), in_specs=[pl.Block...  38.8 us
    pallas_call x1, Pallas kernels, run_reduce(): pl.pallas_call(functools.partial(reduce_kernel, lats, lons), in_specs=[vm...  36.1 us
    unnamed x40, local copies, waits for them, and re-layouts  17.6 us
    pallas_call x1, Pallas kernels, run_halo(): pl.pallas_call(functools.partial(halo_kernel, lats, lons), in_specs=[vmem...  15.1 us

profile of v3, /device:TPU:1, one launch (start us, length us, event | category | flops | bytes accessed | tf_op | source)
XLA Modules:
  0.0 111.3 jit_solution(7455932002439755377)
XLA Ops:
  0.7 1.7 %copy.26 = bf16[192,192]{0,1:T(8,128)(2,1)} copy(bf16[192,192]{1,0:T(8,128)(2,1)} %wproj.1) | data formatting | bytes 147456 | tf_op args[5]
  2.4 0.7 fusion.eye
  3.0 0.9 copy.27
  4.0 0.7 reshape.29.table
  4.7 0.9 copy.25
  5.6 0.3 copy.28.x.x_own
  6.0 0.3 copy.29.g.g_own
  6.3 15.1 %halo.1 = (bf16[48,4608]{1,0:T(8,128)(2,1)S(1)}, bf16[48,1152]{1,0:T(8,128)(2,1)S(1)}, bf16[16,1152]{1,0:T(8,128)(2,1)S(1)}) custom-call(bf16[2,12,18432]{2,1,0:T(8,128)(2,1)S(1)} %copy.28.x.x_own, bf16[2,12,18432]{2,1,0:T(8,128)(2,1)S(1)} %copy.29.g.g_own), custom_call_target="tpu_custom_call" | custom-call | tf_op jit(solution)/shard_map/halo/pallas_call | solution.py:521
  21.4 0.8 copy-done.5
  22.1 0.6 copy-done.9
  22.8 0.6 copy-done.11
  23.4 38.8 %windows.1 = (bf16[2,12,18432]{2,1,0:T(8,128)(2,1)}, bf16[2,12,18432]{2,1,0:T(8,128)(2,1)}, bf16[48,4608]{1,0:T(8,128)(2,1)}, bf16[48,1152]{1,0:T(8,128)(2,1)}, ...) custom-call(s32[1]{0:T(128)} %bitcast.lat_ref, ...), custom_call_target="tpu_custom_call" | custom-call | tf_op jit(solution)/shard_map/windows/pallas_call | solution.py:392
  62.2 1.1 %copy-done.4 = f32[192,576]{1,0:T(8,128)S(1)} copy-done((f32[192,576]{1,0:T(8,128)S(1)}, f32[192,576]{1,0:T(8,128)}, u32[]{:S(2)}) %copy-start.4) | copy-done | bytes 442392
  63.3 1.0 copy-done.6
  64.3 0.9 copy-done.7
  65.3 0.9 copy-done.8
  66.2 0.9 copy-done.10
  67.1 0.8 copy-done.12
  67.9 36.1 %reduce.1 = (bf16[48,4608]{1,0:T(8,128)(2,1)S(1)}, bf16[48,1152]{1,0:T(8,128)(2,1)S(1)}, bf16[16,1152]{1,0:T(8,128)(2,1)S(1)}, bf16[8,16,1664]{2,1,0:T(8,128)(2,1)S(1)}) custom-call(bf16[48,4608]{1,0:T(8,128)(2,1)S(1)} %copy-done.6, bf16[48,1152]{1,0:T(8,128)(2,1)S(1)} %copy-done.10, bf16[16,1152]{1,0:T(8,128)(2,1)S(1)} %copy-done.12, ...), custom_call_target="tpu_custom_call" | custom-call | tf_op jit(solution)/shard_map/reduce/pallas_call | solution.py:750
  104.0 1.3 %copy-done.3 = bf16[2,12,18432]{2,1,0:T(8,128)(2,1)S(1)} copy-done((bf16[2,12,18432]{2,1,0:T(8,128)(2,1)S(1)}, bf16[2,12,18432]{2,1,0:T(8,128)(2,1)}, u32[]{:S(2)}) %copy-start.3) | copy-done | bytes 884760
  105.3 1.6 %finish.1 = (bf16[2,12,18432]{2,1,0:T(8,128)(2,1)S(1)}, bf16[2,12,18432]{2,1,0:T(8,128)(2,1)S(1)}, f32[192,576]{1,0:T(8,128)}, f32[192,192]{1,0:T(8,128)}, f32[12,3312]{1,0:T(8,128)S(1)}) custom-call(s32[1]{0:T(128)} %bitcast.lat_ref, bf16[2,12,18432]{2,1,0:T(8,128)(2,1)S(1)} %copy-done.2, bf16[2,12,18432]{2,1,0:T(8,128)(2,1)S(1)} %copy-done.3, ...), custom_call_target="tpu_custom_call" | custom-call | tf_op jit(solution)/shard_map/finish/pallas_call | solution.py:848
  106.9 1.8 %copy.30 = bf16[2,12,18432]{2,0,1:T(2,128)(2,1)} copy(bf16[2,12,18432]{2,1,0:T(8,128)(2,1)S(1)} %get-tuple-element.50) | data formatting | bytes 1769472
  108.7 0.7 copy.32
  109.5 1.8 %copy.31 = bf16[2,12,18432]{2,0,1:T(2,128)(2,1)} copy(bf16[2,12,18432]{2,1,0:T(8,128)(2,1)S(1)} %get-tuple-element.51) | data formatting | bytes 1769472
  (23 shorter events, 0.2 us)
Async XLA Ops:
  0.6 4.1 %copy-start.13 = (bf16[192,576]{1,0:T(8,128)(2,1)S(1)}, bf16[192,576]{1,0:T(8,128)(2,1)}, u32[]{:S(2)}) copy-start(bf16[192,576]{1,0:T(8,128)(2,1)} %wqkv.1) | copy-start | bytes 663556
  0.6 5.0 %copy-start.14 = (bf16[2,12,18432]{2,0,1:T(2,128)(2,1)S(1)}, bf16[2,12,18432]{2,0,1:T(2,128)(2,1)}, u32[]{:S(2)}) copy-start(bf16[2,12,18432]{2,0,1:T(2,128)(2,1)} %param.8) | copy-start | bytes 2654212
  4.7 1.3 %copy-start.15 = (bf16[2,12,18432]{2,0,1:T(2,128)(2,1)S(1)}, bf16[2,12,18432]{2,0,1:T(2,128)(2,1)}, u32[]{:S(2)}) copy-start(bf16[2,12,18432]{2,0,1:T(2,128)(2,1)} %param.9) | copy-start | bytes 2654212
  6.0 15.4 %copy-start = (bf16[2,12,18432]{2,1,0:T(8,128)(2,1)}, bf16[2,12,18432]{2,1,0:T(8,128)(2,1)S(1)}, u32[]{:S(2)}) copy-start(bf16[2,12,18432]{2,1,0:T(8,128)(2,1)S(1)} %copy.28.x.x_own) | copy-start | bytes 2654212
  6.3 17.1 %copy-start.1 = (bf16[2,12,18432]{2,1,0:T(8,128)(2,1)}, bf16[2,12,18432]{2,1,0:T(8,128)(2,1)S(1)}, u32[]{:S(2)}) copy-start(bf16[2,12,18432]{2,1,0:T(8,128)(2,1)S(1)} %copy.29.g.g_own) | copy-start | bytes 2654212
  21.3 0.8 copy-start.5
  22.1 0.6 copy-start.9
  22.8 0.6 copy-start.11
  62.2 41.9 %copy-start.2 = (bf16[2,12,18432]{2,1,0:T(8,128)(2,1)S(1)}, bf16[2,12,18432]{2,1,0:T(8,128)(2,1)}, u32[]{:S(2)}) copy-start(bf16[2,12,18432]{2,1,0:T(8,128)(2,1)} %get-tuple-element.28.x_own) | copy-start | bytes 2654212
  62.2 1.1 %copy-start.4 = (f32[192,576]{1,0:T(8,128)S(1)}, f32[192,576]{1,0:T(8,128)}, u32[]{:S(2)}) copy-start(f32[192,576]{1,0:T(8,128)} %get-tuple-element.33.raw_q) | copy-start | bytes 1327108
  63.3 1.0 copy-start.6
  64.3 0.9 copy-start.7
  65.3 0.9 copy-start.8
  66.2 0.9 copy-start.10
  67.1 0.8 copy-start.12
  104.0 1.3 %copy-start.3 = (bf16[2,12,18432]{2,1,0:T(8,128)(2,1)S(1)}, bf16[2,12,18432]{2,1,0:T(8,128)(2,1)}, u32[]{:S(2)}) copy-start(bf16[2,12,18432]{2,1,0:T(8,128)(2,1)} %get-tuple-element.29.g_own) | copy-start | bytes 2654212

commit v4 on v0

v4 whole, which is shorter than its diff:
```python
import functools
import math

import jax
import jax.numpy as jnp
import numpy as np
from jax import lax
from jax.experimental import pallas as pl
from jax.experimental.pallas import tpu as pltpu
from jax.sharding import PartitionSpec as P

C = 192
HEADS = 6
HD = 32
WLON = 12
WIN = 144
HALF = 72
SPAN = 23
ROWLEN = 12 * SPAN
ROWPAD = 384
COLS = 96
HALO = 6 * C
WLANES = WLON * C
OWN = COLS * C
FRAME = OWN + HALO
FROWS = 15
GROUP = 4
WPB = 8
POS = 3312
TABLE = 4096
WCHUNK = 12 * 768 // 8
TCHUNK = TABLE // 8
TILES = WCHUNK // 128
MESH = pl.DeviceIdType.MESH
EPS = 1e-5
SCALE = HD**-0.5
LOG2E = math.log2(math.e)
F32 = jnp.float32
BF16 = jnp.bfloat16


def nn(a, b):
    return lax.dot_general(a, b, (((1,), (0,)), ((), ())), preferred_element_type=F32)


def nt(a, b):
    return lax.dot_general(a, b, (((1,), (1,)), ((), ())), preferred_element_type=F32)


def tn(a, b):
    return lax.dot_general(a, b, (((0,), (0,)), ((), ())), preferred_element_type=F32)


def pick_matrix():
    row = lax.broadcasted_iota(jnp.int32, (WIN, 1), 0)
    lk = lax.rem(row, WLON)
    block = lax.div(row, WLON)
    kb = lax.rem(block, 2) * 6 + lax.div(block, 2)
    col = lax.broadcasted_iota(jnp.int32, (WIN, ROWPAD), 1)
    return jnp.where(col == kb * SPAN + 11 - lk, 1.0, 0.0).astype(BF16)


def windows_in(frame, row, count, tokens, first, half=0):
    def window(w, _):
        base = HALO + (2 * w + half // HALF if count == 3 else w) * WLANES
        for m in range(6):
            at = pl.multiple_of(base + m * 2 * C, 128)
            slab = frame[row : row + count, :, pl.ds(at, 2 * C)].astype(F32).reshape(2 * count, 2 * C)
            even = slab[:, :C]
            odd = slab[:, C:]
            for n, part in ((2 * m, even), (2 * m + 1, odd)):
                slots = pl.ds(half + n, 2 * count, stride=WLON)
                tokens[first + w, 0, slots, :] = part[:, :128]
                tokens[first + w, 1, slots, :] = jnp.concatenate([part[:, 128:], part[:, 128:]], axis=1)
        return 0

    lax.fori_loop(0, WPB // 2 if count == 3 else WPB, window, 0)


def windows_out(frame, row, count, tokens, first, half=0):
    def window(w, _):
        base = HALO + (2 * w + half // HALF if count == 3 else w) * WLANES
        for m in range(6):
            at = pl.multiple_of(base + m * 2 * C, 128)
            parts = []
            for n in (2 * m, 2 * m + 1):
                slots = pl.ds(half + n, 2 * count, stride=WLON)
                parts.append(tokens[first + w, 0, slots, :])
                parts.append(tokens[first + w, 1, slots, :][:, : C - 128])
            slab = jnp.concatenate(parts, axis=1).reshape(count, 2, 2 * C)
            frame[row : row + count, :, pl.ds(at, 2 * C)] = slab.astype(BF16)
        return 0

    lax.fori_loop(0, WPB // 2 if count == 3 else WPB, window, 0)


def halves(frame, row, tokens, first, out):
    move = windows_out if out else windows_in
    move(frame, row, 3, tokens, first, 0)
    move(frame, row, 3, tokens, first, HALF)


def put_head(ref, slot, i, value):
    ref[slot, :, i * 128 : i * 128 + 128] = value[:, :128]
    ref[slot, :, 768 + i * 16 : 768 + i * 16 + 16] = value[:, 128:]


def get_head(ref, slot, i):
    tail = ref[slot, :, 768 + i * 16 : 768 + i * 16 + 16]
    return jnp.concatenate([ref[slot, :, i * 128 : i * 128 + 128], tail], axis=1)


def bias_in(table, flat, pick, rows_scratch, shifted, bias):
    for i in range(HEADS):
        flat[2 * i : 2 * i + 2, 0:POS] = table[i]
    for zq in range(2):
        for pq in range(6):
            at = (zq * 6 + pq) * ROWLEN
            rows_scratch[pq * 2 + zq, 0:12, 0:ROWLEN] = flat[0:12, at : at + ROWLEN]
    for n in range(12):
        rows = rows_scratch[:, n, :]
        rows = jnp.concatenate([rows, jnp.zeros((4, ROWPAD), F32)], axis=0)
        for lq in range(WLON):
            moved = pltpu.roll(rows, (ROWPAD - lq) % ROWPAD, 1) if lq else rows
            for t in range(3):
                shifted[t, pl.ds(lq, 12, stride=12), :] = moved[:12, t * 128 : t * 128 + 128]
        full = jnp.concatenate([shifted[t] for t in range(3)], axis=1)
        high = full.astype(BF16)
        rest = full - high.astype(F32)
        mid = rest.astype(BF16)
        low = (rest - mid.astype(F32)).astype(BF16)
        total = nt(pick, high) + nt(pick, mid) + nt(pick, low)
        put_head(bias, n % 2, n // 2, total * LOG2E)


def bias_out(grads, pick, shifted, rows_scratch):
    for n in range(12):
        full = nn(get_head(grads, n % 2, n // 2).astype(BF16).T, pick)
        for t in range(3):
            shifted[t] = full[:, t * 128 : t * 128 + 128]
        total = jnp.zeros((16, ROWPAD), F32)
        for lq in range(WLON):
            rows = [shifted[t, pl.ds(lq, 12, stride=12), :] for t in range(3)]
            rows = jnp.concatenate(rows, axis=1)
            rows = jnp.concatenate([rows, jnp.zeros((4, ROWPAD), F32)], axis=0)
            total = total + (pltpu.roll(rows, lq, 1) if lq else rows)
        rows_scratch[:, n, :] = total[:12]
    parts = [rows_scratch[pq * 2 + zq][:, :ROWLEN] for zq in range(2) for pq in range(6)]
    parts.append(jnp.zeros((16, TABLE - POS), F32))
    return jnp.concatenate(parts, axis=1)


def head_rows(a):
    lane = lax.broadcasted_iota(jnp.int32, (1, 128), 1) // HD
    zero = jnp.zeros((), BF16)

    def only(part, i):
        return jnp.where(lane[:, : part.shape[1]] == i % 4, part, zero)

    wide, slim = a[:, :128], a[:, 128:C]
    first = jnp.concatenate([only(wide[:128], i) for i in range(4)], axis=0)
    second = jnp.concatenate([only(slim[:128], i) for i in range(4, HEADS)], axis=0)
    tail = [only(wide[128:], i) for i in range(4)]
    left = jnp.concatenate(tail + [jnp.zeros((64, 128), BF16)], axis=0)
    tail = [only(slim[128:], i) for i in range(4, HEADS)]
    right = jnp.concatenate([jnp.zeros((64, 64), BF16)] + tail + [jnp.zeros((32, 64), BF16)], axis=0)
    return first, second, left, right


def across(a, rows):
    first, second, left, right = rows
    return jnp.concatenate(
        [nt(a[:, :128], first), nt(a[:, 128:C], second), nt(a, jnp.concatenate([left, right], axis=1))],
        axis=1,
    )


def gathered(a, rows):
    first, second, left, right = rows
    tail = nn(a[:, 768:], jnp.concatenate([left, right], axis=1))
    return jnp.concatenate(
        [nn(a[:, :512], first) + tail[:, :128], nn(a[:, 512:768], second) + tail[:, 128:]], axis=1
    )


def by_head(t, a):
    tail = nn(t, a[:, 768:])
    out = []
    for j in range(HEADS // 2):
        pair = nn(t[64 * j : 64 * j + 64], a[:, 256 * j : 256 * j + 256])
        for i in (2 * j, 2 * j + 1):
            r = (i % 2) * HD
            main = pair[r : r + HD, r * 4 : r * 4 + 128]
            out.append(jnp.concatenate([main, tail[i * HD : i * HD + HD, 16 * i : 16 * i + 16]], axis=1))
    return jnp.concatenate(out, axis=0)


def attend(x_ref, g_ref, us, bias, dbias, slot, gain, shift, wqkv, wqkv_t, wproj, wproj_t, raw_q, raw_p):
    n = WIN
    ws = range(len(us))

    def tokens(ref):
        rows = [jnp.concatenate([ref[u, 0], ref[u, 1]], axis=1) for u in us]
        return jnp.concatenate(rows, axis=0)[:, :C]

    def split(a):
        return [a[w * n : (w + 1) * n] for w in ws]

    x = tokens(x_ref)
    g = tokens(g_ref)
    gb = g.astype(BF16)
    center = x - jnp.mean(x, axis=1, keepdims=True)
    rstd = lax.rsqrt(jnp.mean(center * center, axis=1, keepdims=True) + EPS)
    xn = center * rstd
    h = (xn * gain + shift).astype(BF16)
    q = split(nn(h, wqkv[:, :C]).astype(BF16))
    kv = split(nn(h, wqkv[:, C:]).astype(BF16))
    k = [a[:, :C] for a in kv]
    v = [a[:, C:] for a in kv]
    do = split(nn(gb, wproj_t[...]).astype(BF16))
    k_t = [a.T for a in k]
    v_t = [a.T for a in v]
    h_t = h.T
    qr = [head_rows(a) for a in q]
    dor = [head_rows(a) for a in do]
    s = [across(k[w], qr[w]) for w in ws]
    dp = [across(v[w], dor[w]) for w in ws]
    pb, dsb = [], []
    for w in ws:
        ps, dss = [], []
        for b in range(7):
            lanes = slice(b * 128, b * 128 + 128)
            t = s[w][:, lanes] * (SCALE * LOG2E) + bias[slot, :, lanes]
            e = jnp.exp2(t - jnp.max(t, axis=0, keepdims=True))
            p = e * (1.0 / jnp.sum(e, axis=0, keepdims=True))
            d = dp[w][:, lanes]
            ds = p * (d - jnp.sum(p * d, axis=0, keepdims=True))
            dbias[slot, :, lanes] += ds
            ps.append(p.astype(BF16))
            dss.append((ds * SCALE).astype(BF16))
        pb.append(jnp.concatenate(ps, axis=1))
        dsb.append(jnp.concatenate(dss, axis=1))
    o_t = [by_head(v_t[w], pb[w]).astype(BF16) for w in ws]
    dq_t = [by_head(k_t[w], dsb[w]).astype(BF16) for w in ws]
    dv = jnp.concatenate([gathered(pb[w], dor[w]).astype(BF16) for w in ws], axis=0)
    dk = jnp.concatenate([gathered(dsb[w], qr[w]).astype(BF16) for w in ws], axis=0)
    o = jnp.concatenate([o_t[w].T for w in ws], axis=0)
    dq = jnp.concatenate([dq_t[w].T for w in ws], axis=0)
    a = nn(o, wproj[...]).astype(BF16)
    dh = nn(dq, wqkv_t[0:C]) + nn(dk, wqkv_t[C : 2 * C]) + nn(dv, wqkv_t[2 * C :])
    raw_p[...] += sum(nn(o_t[w], gb[w * n : (w + 1) * n]) for w in ws)
    raw_q[:, 0:C] += nn(h_t, dq)
    raw_q[:, C : 2 * C] += nn(h_t, dk)
    raw_q[:, 2 * C :] += nn(h_t, dv)
    dxn = dh * gain
    m1 = jnp.mean(dxn, axis=1, keepdims=True)
    m2 = jnp.mean(dxn * xn, axis=1, keepdims=True)
    dx = (rstd * (dxn - m1 - xn * m2)).astype(BF16)
    x = split(x + a.astype(F32))
    g = split(g + dx.astype(F32))
    for w, u in enumerate(us):
        x_ref[u, 0] = x[w][:, :128]
        x_ref[u, 1, :, 0:64] = x[w][:, 128:]
        g_ref[u, 0] = g[w][:, :128]
        g_ref[u, 1, :, 0:64] = g[w][:, 128:]


def copy_to(src, dst, send, recv, lat, lon):
    return pltpu.make_async_remote_copy(
        src_ref=src,
        dst_ref=dst,
        send_sem=send,
        recv_sem=recv,
        device_id=(lat, lon),
        device_id_type=MESH,
    )


def greet(lat, lon):
    barrier = pltpu.get_barrier_semaphore()
    pl.semaphore_signal(barrier, inc=1, device_id=(lat, lon), device_id_type=MESH)


def each(lo, hi, skip, act):
    def step(i, _):
        @pl.when(i != skip)
        def _():
            act(i)

        return 0

    lax.fori_loop(lo, hi, step, 0)


def kernel(
    lats,
    lons,
    x,
    g,
    gain_ref,
    shift_ref,
    wqkv,
    wproj,
    table,
    x_out,
    g_out,
    grad_q,
    grad_p,
    grad_bias,
    fx,
    fg,
    xw,
    gw,
    bias,
    dbias,
    rows_scratch,
    shifted,
    flat,
    wqkv_t,
    wproj_t,
    raw_q,
    raw_p,
    mine_w,
    part_w,
    part_w_in,
    tiles,
    tiles_in,
    joined,
    sum_w,
    mine_t,
    part_t,
    part_t_in,
    sum_t,
    squares,
    own_sem,
    halo_send,
    halo_recv,
    ret_send,
    ret_recv,
    w_send,
    w_recv,
    t_send,
    t_recv,
    tile_send,
    tile_recv,
    join_send,
    join_recv,
    wb_send,
    wb_recv,
    tb_send,
    tb_recv,
    sq_send,
    sq_recv,
):
    lat = lax.axis_index("lat")
    lon = lax.axis_index("lon")
    west = lax.rem(lon + lons - 1, lons)
    east = lax.rem(lon + 1, lons)
    first = lat == 0
    final = lat == lats - 1
    barrier = pltpu.get_barrier_semaphore()
    each(0, lons, lon, lambda o: greet(lat, o))
    each(0, lats, lat, lambda a: greet(a, lon))

    @pl.when(lat > 0)
    def _():
        greet(lat - 1, west)

    @pl.when(lat < lats - 1)
    def _():
        greet(lat + 1, east)

    pairs = ((x, fx), (g, fg))
    local = []
    for n, (src, frame) in enumerate(pairs):
        local.append(
            pltpu.make_async_copy(
                src.at[3:12, :, HALO:OWN], frame.at[3:12, :, HALO:OWN], own_sem.at[n]
            )
        )
    polar = []
    for n, (src, frame) in enumerate(pairs):
        polar.append(
            pltpu.make_async_copy(
                src.at[0:3, :, HALO:OWN], frame.at[0:3, :, HALO:OWN], own_sem.at[2 + n]
            )
        )
    for copy in local:
        copy.start()

    @pl.when(first)
    def _():
        for copy in polar:
            copy.start()

    wqkv_t[...] = wqkv[...].T
    wproj_t[...] = wproj[...].T

    ups, sides, diags = [], [], []
    for n, (src, frame) in enumerate(pairs):
        ups.append(
            copy_to(
                src.at[0:3, :, HALO:OWN],
                frame.at[12:15, :, HALO:OWN],
                halo_send.at[n],
                halo_recv.at[n],
                lat - 1,
                lon,
            )
        )
        sides.append(
            copy_to(
                src.at[:, :, 0:HALO],
                frame.at[0:12, :, OWN:FRAME],
                halo_send.at[2 + n],
                halo_recv.at[2 + n],
                lat,
                west,
            )
        )
        diags.append(
            copy_to(
                src.at[0:3, :, 0:HALO],
                frame.at[12:15, :, OWN:FRAME],
                halo_send.at[4 + n],
                halo_recv.at[4 + n],
                lat - 1,
                west,
            )
        )
    peers = lons - 1 + lats - 1
    pl.semaphore_wait(barrier, peers + jnp.where(lat > 0, 1, 0) + jnp.where(lat < lats - 1, 1, 0))
    for copy in sides:
        copy.start()

    @pl.when(lat > 0)
    def _():
        for copy in ups + diags:
            copy.start()

    pick = pick_matrix()
    rows_scratch[...] = jnp.zeros_like(rows_scratch)
    bias[:, :, 768:] = jnp.zeros((3, WIN, 128), F32)
    bias_in(table, flat, pick, rows_scratch, shifted, bias)
    dbias[...] = jnp.zeros_like(dbias)
    raw_q[...] = jnp.zeros_like(raw_q)
    raw_p[...] = jnp.zeros_like(raw_p)

    for copy in local:
        copy.wait()
    for copy in sides:
        copy.wait_recv()
    windows_in(fx, 3, 6, xw, 0)
    windows_in(fg, 3, 6, gw, 0)

    def halves_in(row, unit, slot, source, lo):
        halves(fx, row, xw, unit, False)
        halves(fg, row, gw, unit, False)
        for i in range(HEADS):
            part = get_head(bias, source, i)[lo : lo + HALF, lo : lo + HALF]
            away = jnp.full((HALF, HALF), -1e9, F32)
            top = jnp.concatenate([part, away], axis=1)
            low = jnp.concatenate([away, part], axis=1)
            put_head(bias, slot, i, jnp.concatenate([top, low], axis=0))

    def halves_out(row, unit, slot, target, lo):
        halves(fx, row, xw, unit, True)
        halves(fg, row, gw, unit, True)
        zero = jnp.zeros((HALF, HALF), F32)
        for i in range(HEADS):
            both = get_head(dbias, slot, i)
            part = both[:HALF, :HALF] + both[HALF:, HALF:]
            part = jnp.concatenate([zero, part] if lo else [part, zero], axis=1)
            none = jnp.zeros((HALF, WIN), F32)
            part = jnp.concatenate([none, part] if lo else [part, none], axis=0)
            old = get_head(dbias, target, i) if target != slot else 0.0
            put_head(dbias, target, i, old + part)

    @pl.when(first)
    def _():
        for copy in polar:
            copy.wait()
        halves_in(0, 2 * WPB, 2, 0, HALF)

    @pl.when(final)
    def _():
        halves_in(9, WPB, 1, 1, 0)

    rest = (gain_ref[...], shift_ref[...], wqkv, wqkv_t, wproj, wproj_t, raw_q, raw_p)
    full = 2 * WPB // GROUP
    half = WPB // 2 // GROUP

    def group(u, _):
        @pl.when((u == full // 2) & (lat < lats - 1))
        def _():
            for copy in ups + diags:
                copy.wait_recv()
            windows_in(fx, 9, 6, xw, WPB)
            windows_in(fg, 9, 6, gw, WPB)

        slot = jnp.minimum(u // (WPB // GROUP), 2)
        attend(xw, gw, [GROUP * u + r for r in range(GROUP)], bias, dbias, slot, *rest)
        return 0

    lax.fori_loop(0, jnp.where(first, full + half, jnp.where(final, full // 2 + half, full)), group, 0)

    raw = jnp.concatenate([raw_q[...], raw_p[...]], axis=1)
    for j in range(lons):
        row = []
        for t in range(TILES):
            col = j * TILES + t
            r, c = col // 6 * 16, col % 6 * 128
            row.append(raw[r : r + 16, c : c + 128])
        chunk = jnp.concatenate(row, axis=1)
        mine_w[j] = chunk
        part_w[j] = chunk.astype(BF16)

    def w_out(o):
        return copy_to(part_w.at[o], part_w_in.at[lon], w_send.at[o], w_recv.at[lon], lat, o)

    def w_in(o):
        return copy_to(part_w.at[o], part_w_in.at[o], w_send.at[o], w_recv.at[o], lat, o)

    each(0, lons, lon, lambda o: w_out(o).start())

    @pl.when(lat < lats - 1)
    def _():
        windows_out(fx, 9, 6, xw, WPB)
        windows_out(fg, 9, 6, gw, WPB)

    downs, crosses = [], []
    for n, frame in enumerate((fx, fg)):
        downs.append(
            copy_to(
                frame.at[12:15, :, HALO:OWN],
                frame.at[0:3, :, HALO:OWN],
                ret_send.at[n],
                ret_recv.at[n],
                lat + 1,
                lon,
            )
        )
        crosses.append(
            copy_to(
                frame.at[12:15, :, OWN:FRAME],
                frame.at[0:3, :, 0:HALO],
                ret_send.at[4 + n],
                ret_recv.at[4 + n],
                lat + 1,
                east,
            )
        )

    @pl.when(lat < lats - 1)
    def _():
        for copy in downs + crosses:
            copy.start()

    windows_out(fx, 3, 6, xw, 0)
    windows_out(fg, 3, 6, gw, 0)

    @pl.when(first)
    def _():
        halves_out(0, 2 * WPB, 2, 0, HALF)

    @pl.when(final)
    def _():
        halves_out(9, WPB, 1, 1, 0)

    backs, tops = [], []
    for n, frame in enumerate((fx, fg)):
        backs.append(
            copy_to(
                frame.at[3:12, :, OWN:FRAME],
                frame.at[3:12, :, 0:HALO],
                ret_send.at[2 + n],
                ret_recv.at[2 + n],
                lat,
                east,
            )
        )
        tops.append(
            copy_to(
                frame.at[0:3, :, OWN:FRAME],
                frame.at[0:3, :, 0:HALO],
                ret_send.at[6 + n],
                ret_recv.at[6 + n],
                lat,
                east,
            )
        )
    for copy in backs:
        copy.start()

    @pl.when(first)
    def _():
        for copy in tops:
            copy.start()

    grads = bias_out(dbias, pick, shifted, rows_scratch)
    for j in range(lons):
        chunk = grads[:, j * TCHUNK : (j + 1) * TCHUNK]
        mine_t[j] = chunk
        part_t[j] = chunk.astype(BF16)

    def t_out(o):
        return copy_to(part_t.at[o], part_t_in.at[lon], t_send.at[o], t_recv.at[lon], lat, o)

    def t_in(o):
        return copy_to(part_t.at[o], part_t_in.at[o], t_send.at[o], t_recv.at[o], lat, o)

    each(0, lons, lon, lambda o: t_out(o).start())

    def add_w(d, total):
        o = lax.rem(lon + d, lons)
        w_in(o).wait_recv()
        return total + part_w_in[o].astype(F32)

    total = lax.fori_loop(1, lons, add_w, mine_w[lon])
    for t in range(TILES):
        tiles[t] = total[:, t * 128 : t * 128 + 128].astype(BF16)

    def tile_out(a):
        return copy_to(tiles.at[a], tiles_in.at[lat], tile_send.at[a], tile_recv.at[lat], a, lon)

    def tile_in(a):
        return copy_to(tiles.at[0], tiles_in.at[a], tile_send.at[0], tile_recv.at[a], a, lon)

    each(0, TILES, lat, lambda a: tile_out(a).start())

    def add_t(d, total):
        o = lax.rem(lon + d, lons)
        t_in(o).wait_recv()
        return total + part_t_in[o].astype(F32)

    sum_t[lon] = lax.fori_loop(1, lons, add_t, mine_t[lon]).astype(BF16)

    def tb_out(o):
        return copy_to(sum_t.at[lon], sum_t.at[lon], tb_send.at[o], tb_recv.at[lon], lat, o)

    def tb_in(o):
        return copy_to(sum_t.at[o], sum_t.at[o], tb_send.at[o], tb_recv.at[o], lat, o)

    each(0, lons, lon, lambda o: tb_out(o).start())

    def join_out(a):
        return copy_to(joined.at[lat], joined.at[lat], join_send.at[a], join_recv.at[lat], a, lon)

    def join_in(a):
        return copy_to(joined.at[a], joined.at[a], join_send.at[a], join_recv.at[a], a, lon)

    @pl.when(lat < TILES)
    def _():
        def add_tile(d, total):
            a = lax.rem(lat + d, lats)
            tile_in(a).wait_recv()
            return total + tiles_in[a].astype(F32)

        total = lax.fori_loop(1, lats, add_tile, tiles[lat].astype(F32))
        joined[lat] = total.astype(BF16)
        each(0, lats, lat, lambda a: join_out(a).start())

    each(0, lons, lon, lambda o: tb_in(o).wait_recv())
    whole = jnp.concatenate([sum_t[j].astype(F32) for j in range(lons)], axis=1)
    square = jnp.sum(whole * whole).reshape(1, 1)
    squares[lat] = jnp.broadcast_to(square, (8, 128))

    def sq_out(a):
        return copy_to(squares.at[lat], squares.at[lat], sq_send.at[a], sq_recv.at[lat], a, lon)

    def sq_in(a):
        return copy_to(squares.at[a], squares.at[a], sq_send.at[a], sq_recv.at[a], a, lon)

    each(0, lats, lat, lambda a: sq_out(a).start())

    each(0, TILES, lat, lambda a: join_in(a).wait_recv())
    sum_w[lon] = jnp.concatenate([joined[t] for t in range(TILES)], axis=1)

    def wb_out(o):
        return copy_to(sum_w.at[lon], sum_w.at[lon], wb_send.at[o], wb_recv.at[lon], lat, o)

    def wb_in(o):
        return copy_to(sum_w.at[o], sum_w.at[o], wb_send.at[o], wb_recv.at[o], lat, o)

    each(0, lons, lon, lambda o: wb_out(o).start())

    for copy in backs:
        copy.wait()

    @pl.when(lat > 0)
    def _():
        for copy in downs + crosses:
            copy.wait_recv()

    @pl.when(lat < lats - 1)
    def _():
        for copy in downs + crosses:
            copy.wait_send()

    @pl.when(first)
    def _():
        for copy in tops:
            copy.wait()

    leave = [
        pltpu.make_async_copy(frame.at[0:12, :, 0:OWN], out, own_sem.at[n])
        for n, (frame, out) in enumerate(((fx, x_out), (fg, g_out)))
    ]
    for copy in leave:
        copy.start()

    each(0, lats, lat, lambda a: sq_in(a).wait_recv())
    table_squares = jnp.zeros((1, 1), F32)
    for a in range(lats):
        table_squares = table_squares + squares[a][0:1, 0:1]
    table_rms = jnp.sqrt(table_squares / (lats * 2 * HEADS * POS) + 1e-6)
    whole = whole[:, :POS] / table_rms
    for i in range(HEADS):
        grad_bias[i] = whole[2 * i : 2 * i + 2]

    each(0, lons, lon, lambda o: wb_in(o).wait_recv())
    cols = []
    square = jnp.zeros((16, 128), F32)
    for j in range(lons):
        for t in range(TILES):
            piece = sum_w[j, :, t * 128 : t * 128 + 128].astype(F32)
            square = square + piece * piece
            cols.append(piece)
    rms = jnp.sqrt(jnp.sum(square).reshape(1, 1) / (4 * C * C) + 1e-6)
    inverse = 1.0 / rms
    for r in range(12):
        row = jnp.concatenate(cols[r * 6 : r * 6 + 6], axis=1) * inverse
        grad_q[r * 16 : r * 16 + 16] = row[:, : 3 * C]
        grad_p[r * 16 : r * 16 + 16] = row[:, 3 * C :]

    def sent(o):
        w_out(o).wait_send()
        t_out(o).wait_send()
        tb_out(o).wait_send()
        wb_out(o).wait_send()

    each(0, lons, lon, sent)
    each(0, TILES, lat, lambda a: tile_out(a).wait_send())
    each(0, lats, lat, lambda a: sq_out(a).wait_send())

    @pl.when(lat < TILES)
    def _():
        each(0, lats, lat, lambda a: join_out(a).wait_send())

    for copy in sides:
        copy.wait_send()

    @pl.when(lat > 0)
    def _():
        for copy in ups + diags:
            copy.wait_send()

    for copy in leave:
        copy.wait()


def on_device(inputs, cotangent, norm_gain, norm_shift, w_qkv, w_proj, bias_table):
    lats = lax.axis_size("lat")
    lons = lax.axis_size("lon")
    vmem = pl.BlockSpec(memory_space=pltpu.VMEM)
    hbm = pl.BlockSpec(memory_space=pl.ANY)
    shape = jax.ShapeDtypeStruct
    units = 2 * WPB + WPB // 2
    sems = pltpu.SemaphoreType.DMA
    counts = [4, 6, 6, 8, 8] + [lons] * 4 + [lats] * 4 + [lons] * 4 + [lats] * 2
    x_out, g_out, grad_q, grad_p, grad_bias = pl.pallas_call(
        functools.partial(kernel, lats, lons),
        in_specs=[hbm, hbm] + [vmem] * 5,
        out_specs=[hbm, hbm] + [vmem] * 3,
        out_shape=[
            shape((12, 2, OWN), BF16),
            shape((12, 2, OWN), BF16),
            shape((C, 3 * C), F32),
            shape((C, C), F32),
            shape((HEADS, 2, POS), F32),
        ],
        scratch_shapes=[
            pltpu.VMEM((FROWS, 2, FRAME), BF16),
            pltpu.VMEM((FROWS, 2, FRAME), BF16),
            pltpu.VMEM((units, 2, WIN, 128), F32),
            pltpu.VMEM((units, 2, WIN, 128), F32),
            pltpu.VMEM((3, WIN, 896), F32),
            pltpu.VMEM((3, WIN, 896), F32),
            pltpu.VMEM((12, 16, ROWPAD), F32),
            pltpu.VMEM((3, WIN, 128), F32),
            pltpu.VMEM((16, 3328), F32),
            pltpu.VMEM((3 * C, C), BF16),
            pltpu.VMEM((C, C), BF16),
            pltpu.VMEM((C, 3 * C), F32),
            pltpu.VMEM((C, C), F32),
            pltpu.VMEM((lons, 16, WCHUNK), F32),
            pltpu.VMEM((lons, 16, WCHUNK), BF16),
            pltpu.VMEM((lons, 16, WCHUNK), BF16),
            pltpu.VMEM((TILES, 16, 128), BF16),
            pltpu.VMEM((lats, 16, 128), BF16),
            pltpu.VMEM((TILES, 16, 128), BF16),
            pltpu.VMEM((lons, 16, WCHUNK), BF16),
            pltpu.VMEM((lons, 16, TCHUNK), F32),
            pltpu.VMEM((lons, 16, TCHUNK), BF16),
            pltpu.VMEM((lons, 16, TCHUNK), BF16),
            pltpu.VMEM((lons, 16, TCHUNK), BF16),
            pltpu.VMEM((lats, 8, 128), F32),
        ]
        + [sems((n,)) for n in counts],
        compiler_params=pltpu.CompilerParams(
            collective_id=0, has_side_effects=True, vmem_limit_bytes=56 * 2**20
        ),
        name="windows",
    )(
        inputs.transpose(1, 0, 2),
        cotangent.transpose(1, 0, 2),
        norm_gain.reshape(1, C),
        norm_shift.reshape(1, C),
        w_qkv,
        w_proj,
        bias_table.transpose(1, 0, 2),
    )
    x_out, g_out, grad_bias = (a.transpose(1, 0, 2) for a in (x_out, g_out, grad_bias))
    return x_out, g_out, grad_q, grad_p, grad_bias


def solution(mesh):
    return jax.shard_map(
        on_device,
        mesh=mesh,
        in_specs=(
            P(None, "lat", "lon"),
            P(None, "lat", "lon"),
            P(),
            P(),
            P(),
            P(),
            P("lat", None, None),
        ),
        out_specs=(P(None, "lat", "lon"), P(None, "lat", "lon"), P(), P(), P("lat", None, None)),
        check_vma=False,
    )
```

time: 833 us -> 78.1 us (0.09)
  the two profiles are of different devices: /device:TPU:1 before, /device:TPU:0 now
where the time goes in v4:
time: 78.1 us; the launch traced here: 77.8 us
  Pallas kernels  70.3 us (90%)
  local copies, waits for them, and re-layouts  6.87 us (9%)
    pallas_call x1, Pallas kernels, on_device(): pl.pallas_call(functools.partial(kernel, lats, lons), in_specs=[hbm, hbm]...  70.3 us
    unnamed x13, local copies, waits for them, and re-layouts  6.87 us

profile of v4, /device:TPU:0, one launch (start us, length us, event | category | flops | bytes accessed | tf_op | source)
XLA Modules:
  0.0 77.8 jit_solution(37335537973540498)
XLA Ops:
  0.6 70.3 %windows.1 = (bf16[12,2,18432]{2,1,0:T(2,128)(2,1)}, bf16[12,2,18432]{2,1,0:T(2,128)(2,1)}, f32[192,576]{1,0:T(8,128)}, f32[192,192]{1,0:T(8,128)}, f32[6,2,3312]{2,1,0:T(2,128)}) custom-call(bf16[12,2,18432]{2,1,0:T(2,128)(2,1)} %bitcast.10, bf16[12,2,18432]{2,1,0:T(2,128)(2,1)} %bitcast.11, f32[1,192]{1,0:T(1,128)} %bitcast.14, f32[1,192]{1,0:T(1,128)} %bitcast.15, ...), custom_call_target="tpu_custom_call" | custom-call | tf_op jit(solution)/shard_map/windows/pallas_call | solution.py:771
  70.9 0.0 copy-start
  70.9 2.8 %copy.17 = bf16[2,12,18432]{2,0,1:T(2,128)(2,1)} copy(bf16[2,12,18432]{2,0,1:T(2,128)(2,1)} %bitcast.9) | data formatting | bytes 1769472
  73.7 0.0 copy-done
  73.7 0.0 copy-start.1
  73.7 0.9 %copy.18 = bf16[2,12,18432]{2,0,1:T(2,128)(2,1)} copy(bf16[2,12,18432]{2,0,1:T(2,128)(2,1)S(1)} %bitcast.8) | data formatting | bytes 1769472
  74.6 0.4 copy-done.1
  75.0 0.0 copy-start.2
  75.0 0.8 copy.19
  75.8 0.3 copy-done.2
  76.2 0.0 copy-start.3
  76.2 0.7 copy.20
  76.8 0.3 copy-done.3
  77.1 0.7 copy.21
Async XLA Ops:
  70.9 2.8 %copy-start = (bf16[12,2,18432]{2,1,0:T(2,128)(2,1)S(1)}, bf16[12,2,18432]{2,1,0:T(2,128)(2,1)}, u32[]{:S(2)}) copy-start(bf16[12,2,18432]{2,1,0:T(2,128)(2,1)} %get-tuple-element.11) | copy-start | bytes 2654212
  73.7 1.4 %copy-start.1 = (f32[192,576]{1,0:T(8,128)S(1)}, f32[192,576]{1,0:T(8,128)}, u32[]{:S(2)}) copy-start(f32[192,576]{1,0:T(8,128)} %get-tuple-element.22) | copy-start | bytes 1327108
  75.0 1.1 %copy-start.2 = (f32[192,192]{1,0:T(8,128)S(1)}, f32[192,192]{1,0:T(8,128)}, u32[]{:S(2)}) copy-start(f32[192,192]{1,0:T(8,128)} %get-tuple-element.23) | copy-start | bytes 442372
  76.2 1.0 %copy-start.3 = (f32[6,2,3312]{2,1,0:T(2,128)S(1)}, f32[6,2,3312]{2,1,0:T(2,128)}, u32[]{:S(2)}) copy-start(f32[6,2,3312]{2,1,0:T(2,128)} %get-tuple-element.14) | copy-start | bytes 476932

commit v5 on v4

--- a/solution.py
+++ b/solution.py
@@ -60,7 +60,7 @@
     return jnp.where(col == kb * SPAN + 11 - lk, 1.0, 0.0).astype(BF16)
 
 
-def windows_in(frame, row, count, tokens, first, half=0):
+def windows_in(frame, row, count, tokens, first, half=0, lo=0, hi=WPB):
     def window(w, _):
         base = HALO + (2 * w + half // HALF if count == 3 else w) * WLANES
         for m in range(6):
@@ -74,21 +74,21 @@
                 tokens[first + w, 1, slots, :] = jnp.concatenate([part[:, 128:], part[:, 128:]], axis=1)
         return 0
 
-    lax.fori_loop(0, WPB // 2 if count == 3 else WPB, window, 0)
+    lax.fori_loop(lo, WPB // 2 if count == 3 else hi, window, 0)
 
 
 def windows_out(frame, row, count, tokens, first, half=0):
     def window(w, _):
         base = HALO + (2 * w + half // HALF if count == 3 else w) * WLANES
-        for m in range(6):
-            at = pl.multiple_of(base + m * 2 * C, 128)
-            parts = []
-            for n in (2 * m, 2 * m + 1):
-                slots = pl.ds(half + n, 2 * count, stride=WLON)
-                parts.append(tokens[first + w, 0, slots, :])
-                parts.append(tokens[first + w, 1, slots, :][:, : C - 128])
-            slab = jnp.concatenate(parts, axis=1).reshape(count, 2, 2 * C)
-            frame[row : row + count, :, pl.ds(at, 2 * C)] = slab.astype(BF16)
+        for p in range(count):
+            for m in range(6):
+                at = pl.multiple_of(base + m * 2 * C, 128)
+                parts = []
+                for n in (2 * m, 2 * m + 1):
+                    slots = pl.ds(half + p * 24 + n, 2, stride=WLON)
+                    parts.append(tokens[first + w, 0, slots, :])
+                    parts.append(tokens[first + w, 1, slots, :][:, : C - 128])
+                frame[row + p, :, pl.ds(at, 2 * C)] = jnp.concatenate(parts, axis=1).astype(BF16)
         return 0
 
     lax.fori_loop(0, WPB // 2 if count == 3 else WPB, window, 0)
@@ -110,14 +110,18 @@
     return jnp.concatenate([ref[slot, :, i * 128 : i * 128 + 128], tail], axis=1)
 
 
-def bias_in(table, flat, pick, rows_scratch, shifted, bias):
+def bias_rows(table, flat, rows_scratch):
+    rows_scratch[...] = jnp.zeros_like(rows_scratch)
     for i in range(HEADS):
         flat[2 * i : 2 * i + 2, 0:POS] = table[i]
     for zq in range(2):
         for pq in range(6):
             at = (zq * 6 + pq) * ROWLEN
             rows_scratch[pq * 2 + zq, 0:12, 0:ROWLEN] = flat[0:12, at : at + ROWLEN]
-    for n in range(12):
+
+
+def bias_in(lo, hi, pick, rows_scratch, shifted, bias):
+    for n in range(lo, hi):
         rows = rows_scratch[:, n, :]
         rows = jnp.concatenate([rows, jnp.zeros((4, ROWPAD), F32)], axis=0)
         for lq in range(WLON):
@@ -126,10 +130,8 @@
                 shifted[t, pl.ds(lq, 12, stride=12), :] = moved[:12, t * 128 : t * 128 + 128]
         full = jnp.concatenate([shifted[t] for t in range(3)], axis=1)
         high = full.astype(BF16)
-        rest = full - high.astype(F32)
-        mid = rest.astype(BF16)
-        low = (rest - mid.astype(F32)).astype(BF16)
-        total = nt(pick, high) + nt(pick, mid) + nt(pick, low)
+        low = (full - high.astype(F32)).astype(BF16)
+        total = nt(pick, high) + nt(pick, low)
         put_head(bias, n % 2, n // 2, total * LOG2E)
 
 
@@ -428,6 +430,10 @@
                 west,
             )
         )
+    pick = pick_matrix()
+    bias[:, :, 768:] = jnp.zeros((3, WIN, 128), F32)
+    bias_rows(table, flat, rows_scratch)
+    bias_in(0, 6, pick, rows_scratch, shifted, bias)
     peers = lons - 1 + lats - 1
     pl.semaphore_wait(barrier, peers + jnp.where(lat > 0, 1, 0) + jnp.where(lat < lats - 1, 1, 0))
     for copy in sides:
@@ -438,20 +444,19 @@
         for copy in ups + diags:
             copy.start()
 
-    pick = pick_matrix()
-    rows_scratch[...] = jnp.zeros_like(rows_scratch)
-    bias[:, :, 768:] = jnp.zeros((3, WIN, 128), F32)
-    bias_in(table, flat, pick, rows_scratch, shifted, bias)
+    bias_in(6, 12, pick, rows_scratch, shifted, bias)
     dbias[...] = jnp.zeros_like(dbias)
     raw_q[...] = jnp.zeros_like(raw_q)
     raw_p[...] = jnp.zeros_like(raw_p)
 
     for copy in local:
         copy.wait()
+    windows_in(fx, 3, 6, xw, 0, 0, 0, WPB - 1)
+    windows_in(fg, 3, 6, gw, 0, 0, 0, WPB - 1)
     for copy in sides:
         copy.wait_recv()
-    windows_in(fx, 3, 6, xw, 0)
-    windows_in(fg, 3, 6, gw, 0)
+    windows_in(fx, 3, 6, xw, 0, 0, WPB - 1)
+    windows_in(fg, 3, 6, gw, 0, 0, WPB - 1)
 
     def halves_in(row, unit, slot, source, lo):
         halves(fx, row, xw, unit, False)
@@ -463,9 +468,7 @@
             low = jnp.concatenate([away, part], axis=1)
             put_head(bias, slot, i, jnp.concatenate([top, low], axis=0))
 
-    def halves_out(row, unit, slot, target, lo):
-        halves(fx, row, xw, unit, True)
-        halves(fg, row, gw, unit, True)
+    def halves_grad(slot, target, lo):
         zero = jnp.zeros((HALF, HALF), F32)
         for i in range(HEADS):
             both = get_head(dbias, slot, i)
@@ -523,79 +526,13 @@
 
     each(0, lons, lon, lambda o: w_out(o).start())
 
-    @pl.when(lat < lats - 1)
-    def _():
-        windows_out(fx, 9, 6, xw, WPB)
-        windows_out(fg, 9, 6, gw, WPB)
-
-    downs, crosses = [], []
-    for n, frame in enumerate((fx, fg)):
-        downs.append(
-            copy_to(
-                frame.at[12:15, :, HALO:OWN],
-                frame.at[0:3, :, HALO:OWN],
-                ret_send.at[n],
-                ret_recv.at[n],
-                lat + 1,
-                lon,
-            )
-        )
-        crosses.append(
-            copy_to(
-                frame.at[12:15, :, OWN:FRAME],
-                frame.at[0:3, :, 0:HALO],
-                ret_send.at[4 + n],
-                ret_recv.at[4 + n],
-                lat + 1,
-                east,
-            )
-        )
-
-    @pl.when(lat < lats - 1)
-    def _():
-        for copy in downs + crosses:
-            copy.start()
-
-    windows_out(fx, 3, 6, xw, 0)
-    windows_out(fg, 3, 6, gw, 0)
-
     @pl.when(first)
     def _():
-        halves_out(0, 2 * WPB, 2, 0, HALF)
+        halves_grad(2, 0, HALF)
 
     @pl.when(final)
     def _():
-        halves_out(9, WPB, 1, 1, 0)
-
-    backs, tops = [], []
-    for n, frame in enumerate((fx, fg)):
-        backs.append(
-            copy_to(
-                frame.at[3:12, :, OWN:FRAME],
-                frame.at[3:12, :, 0:HALO],
-                ret_send.at[2 + n],
-                ret_recv.at[2 + n],
-                lat,
-                east,
-            )
-        )
-        tops.append(
-            copy_to(
-                frame.at[0:3, :, OWN:FRAME],
-                frame.at[0:3, :, 0:HALO],
-                ret_send.at[6 + n],
-                ret_recv.at[6 + n],
-                lat,
-                east,
-            )
-        )
-    for copy in backs:
-        copy.start()
-
-    @pl.when(first)
-    def _():
-        for copy in tops:
-            copy.start()
+        halves_grad(1, 1, 0)
 
     grads = bias_out(dbias, pick, shifted, rows_scratch)
     for j in range(lons):
@@ -611,6 +548,24 @@
 
     each(0, lons, lon, lambda o: t_out(o).start())
 
+    downs, crosses, backs, tops = [], [], [], []
+    for n, frame in enumerate((fx, fg)):
+        rows = frame.at[0:3, :, HALO:OWN]
+        side = frame.at[3:12, :, 0:HALO]
+        corner = frame.at[0:3, :, 0:HALO]
+        sems = [(ret_send.at[2 * r + n], ret_recv.at[2 * r + n]) for r in range(4)]
+        downs.append(copy_to(frame.at[12:15, :, HALO:OWN], rows, *sems[0], lat + 1, lon))
+        crosses.append(copy_to(frame.at[12:15, :, OWN:FRAME], corner, *sems[1], lat + 1, east))
+        backs.append(copy_to(frame.at[3:12, :, OWN:FRAME], side, *sems[2], lat, east))
+        tops.append(copy_to(frame.at[0:3, :, OWN:FRAME], corner, *sems[3], lat, east))
+
+    @pl.when(lat < lats - 1)
+    def _():
+        windows_out(fx, 9, 6, xw, WPB)
+        windows_out(fg, 9, 6, gw, WPB)
+        for copy in downs + crosses:
+            copy.start()
+
     def add_w(d, total):
         o = lax.rem(lon + d, lons)
         w_in(o).wait_recv()
@@ -628,6 +583,24 @@
 
     each(0, TILES, lat, lambda a: tile_out(a).start())
 
+    windows_out(fx, 3, 6, xw, 0)
+    windows_out(fg, 3, 6, gw, 0)
+
+    @pl.when(first)
+    def _():
+        halves(fx, 0, xw, 2 * WPB, True)
+        halves(fg, 0, gw, 2 * WPB, True)
+        for copy in tops:
+            copy.start()
+
+    @pl.when(final)
+    def _():
+        halves(fx, 9, xw, WPB, True)
+        halves(fg, 9, gw, WPB, True)
+
+    for copy in backs:
+        copy.start()
+
     def add_t(d, total):
         o = lax.rem(lon + d, lons)
         t_in(o).wait_recv()
@@ -660,6 +633,17 @@
         joined[lat] = total.astype(BF16)
         each(0, lats, lat, lambda a: join_out(a).start())
 
+    each(0, TILES, lat, lambda a: join_in(a).wait_recv())
+    sum_w[lon] = jnp.concatenate([joined[t] for t in range(TILES)], axis=1)
+
+    def wb_out(o):
+        return copy_to(sum_w.at[lon], sum_w.at[lon], wb_send.at[o], wb_recv.at[lon], lat, o)
+
+    def wb_in(o):
+        return copy_to(sum_w.at[o], sum_w.at[o], wb_send.at[o], wb_recv.at[o], lat, o)
+
+    each(0, lons, lon, lambda o: wb_out(o).start())
+
     each(0, lons, lon, lambda o: tb_in(o).wait_recv())
     whole = jnp.concatenate([sum_t[j].astype(F32) for j in range(lons)], axis=1)
     square = jnp.sum(whole * whole).reshape(1, 1)
@@ -672,17 +656,6 @@
         return copy_to(squares.at[a], squares.at[a], sq_send.at[a], sq_recv.at[a], a, lon)
 
     each(0, lats, lat, lambda a: sq_out(a).start())
-
-    each(0, TILES, lat, lambda a: join_in(a).wait_recv())
-    sum_w[lon] = jnp.concatenate([joined[t] for t in range(TILES)], axis=1)
-
-    def wb_out(o):
-        return copy_to(sum_w.at[lon], sum_w.at[lon], wb_send.at[o], wb_recv.at[lon], lat, o)
-
-    def wb_in(o):
-        return copy_to(sum_w.at[o], sum_w.at[o], wb_send.at[o], wb_recv.at[o], lat, o)
-
-    each(0, lons, lon, lambda o: wb_out(o).start())
 
     for copy in backs:
         copy.wait()
@@ -759,6 +732,32 @@
         copy.wait()
 
 
+def finish_kernel(x, g, q, p, b, x_out, g_out, q_out, p_out, b_out, sems):
+    copies = []
+    for src, dst in ((x, x_out), (g, g_out)):
+        for r in range(0, 12, 3):
+            copies.append((src.at[r : r + 3], dst.at[r : r + 3]))
+    copies += [(q, q_out), (p, p_out), (b, b_out)]
+    copies = [pltpu.make_async_copy(*pair, sems.at[n]) for n, pair in enumerate(copies)]
+    for copy in copies:
+        copy.start()
+    for copy in copies:
+        copy.wait()
+
+
+def finish(*results):
+    hbm = pl.BlockSpec(memory_space=pl.ANY)
+    return pl.pallas_call(
+        finish_kernel,
+        in_specs=[hbm] * 5,
+        out_specs=[hbm] * 5,
+        out_shape=[jax.ShapeDtypeStruct(a.shape, a.dtype) for a in results],
+        scratch_shapes=[pltpu.SemaphoreType.DMA((11,))],
+        compiler_params=pltpu.CompilerParams(vmem_limit_bytes=56 * 2**20),
+        name="finish",
+    )(*results)
+
+
 def on_device(inputs, cotangent, norm_gain, norm_shift, w_qkv, w_proj, bias_table):
     lats = lax.axis_size("lat")
     lons = lax.axis_size("lon")
@@ -768,7 +767,7 @@
     units = 2 * WPB + WPB // 2
     sems = pltpu.SemaphoreType.DMA
     counts = [4, 6, 6, 8, 8] + [lons] * 4 + [lats] * 4 + [lons] * 4 + [lats] * 2
-    x_out, g_out, grad_q, grad_p, grad_bias = pl.pallas_call(
+    results = pl.pallas_call(
         functools.partial(kernel, lats, lons),
         in_specs=[hbm, hbm] + [vmem] * 5,
         out_specs=[hbm, hbm] + [vmem] * 3,
@@ -820,6 +819,7 @@
         w_proj,
         bias_table.transpose(1, 0, 2),
     )
+    x_out, g_out, grad_q, grad_p, grad_bias = finish(*results)
     x_out, g_out, grad_bias = (a.transpose(1, 0, 2) for a in (x_out, g_out, grad_bias))
     return x_out, g_out, grad_q, grad_p, grad_bias
 

time: 78.1 us -> 146 us (1.87)
  the two profiles are of different devices: /device:TPU:0 before, /device:TPU:1 now
where the time goes in v5:
time: 146 us
  Pallas kernels  146 us (100%)
    pallas_call x1, Pallas kernels, finish(): pl.pallas_call(finish_kernel, in_specs=[hbm] * 5, out_specs=[hbm] * 5, ou...  80.5 us
    pallas_call x1, Pallas kernels, on_device(): pl.pallas_call(functools.partial(kernel, lats, lons), in_specs=[hbm, hbm]...  65.1 us

profile of v5, /device:TPU:1, one launch (start us, length us, event | category | flops | bytes accessed | tf_op | source)
XLA Modules:
  0.0 146.3 jit_solution(18402847423514113070)
XLA Ops:
  0.6 65.1 %windows.1 = (bf16[12,2,18432]{2,1,0:T(2,128)(2,1)}, bf16[12,2,18432]{2,1,0:T(2,128)(2,1)}, f32[192,576]{1,0:T(8,128)}, f32[192,192]{1,0:T(8,128)}, f32[6,2,3312]{2,1,0:T(2,128)}) custom-call(bf16[12,2,18432]{2,1,0:T(2,128)(2,1)} %bitcast.8, bf16[12,2,18432]{2,1,0:T(2,128)(2,1)} %bitcast.9, f32[1,192]{1,0:T(1,128)} %bitcast.11, f32[1,192]{1,0:T(1,128)} %bitcast.12, ...), custom_call_target="tpu_custom_call" | custom-call | tf_op jit(solution)/shard_map/windows/pallas_call | solution.py:770
  65.8 80.5 %finish.1 = (bf16[12,2,18432]{2,1,0:T(2,128)(2,1)}, bf16[12,2,18432]{2,1,0:T(2,128)(2,1)}, f32[192,576]{1,0:T(8,128)}, f32[192,192]{1,0:T(8,128)}, f32[6,2,3312]{2,1,0:T(2,128)}) custom-call(bf16[12,2,18432]{2,1,0:T(2,128)(2,1)} %get-tuple-element.15.x, bf16[12,2,18432]{2,1,0:T(2,128)(2,1)} %get-tuple-element.16.g, f32[192,576]{1,0:T(8,128)} %get-tuple-element.17.q, ...), custom_call_target="tpu_custom_call" | custom-call | tf_op jit(solution)/shard_map/finish/pallas_call | solution.py:750

commit v6 on v5

--- a/solution.py
+++ b/solution.py
@@ -60,44 +60,36 @@
     return jnp.where(col == kb * SPAN + 11 - lk, 1.0, 0.0).astype(BF16)
 
 
-def windows_in(frame, row, count, tokens, first, half=0, lo=0, hi=WPB):
-    def window(w, _):
-        base = HALO + (2 * w + half // HALF if count == 3 else w) * WLANES
-        for m in range(6):
-            at = pl.multiple_of(base + m * 2 * C, 128)
-            slab = frame[row : row + count, :, pl.ds(at, 2 * C)].astype(F32).reshape(2 * count, 2 * C)
-            even = slab[:, :C]
-            odd = slab[:, C:]
-            for n, part in ((2 * m, even), (2 * m + 1, odd)):
-                slots = pl.ds(half + n, 2 * count, stride=WLON)
-                tokens[first + w, 0, slots, :] = part[:, :128]
-                tokens[first + w, 1, slots, :] = jnp.concatenate([part[:, 128:], part[:, 128:]], axis=1)
-        return 0
-
-    lax.fori_loop(lo, WPB // 2 if count == 3 else hi, window, 0)
-
-
-def windows_out(frame, row, count, tokens, first, half=0):
-    def window(w, _):
-        base = HALO + (2 * w + half // HALF if count == 3 else w) * WLANES
-        for p in range(count):
-            for m in range(6):
-                at = pl.multiple_of(base + m * 2 * C, 128)
-                parts = []
-                for n in (2 * m, 2 * m + 1):
-                    slots = pl.ds(half + p * 24 + n, 2, stride=WLON)
-                    parts.append(tokens[first + w, 0, slots, :])
-                    parts.append(tokens[first + w, 1, slots, :][:, : C - 128])
-                frame[row + p, :, pl.ds(at, 2 * C)] = jnp.concatenate(parts, axis=1).astype(BF16)
-        return 0
-
-    lax.fori_loop(0, WPB // 2 if count == 3 else WPB, window, 0)
-
-
-def halves(frame, row, tokens, first, out):
-    move = windows_out if out else windows_in
-    move(frame, row, 3, tokens, first, 0)
-    move(frame, row, 3, tokens, first, HALF)
+def pieces_in(frame, tokens, place, unit, count=GROUP):
+    def piece(r, side, m):
+        row, base = place(r, side)
+        slab = frame[pl.ds(row, 3), :, pl.ds(pl.multiple_of(base + m * 2 * C, 128), 2 * C)]
+        slab = slab.astype(F32).reshape(6, 2 * C)
+        for n, part in ((2 * m, slab[:, :C]), (2 * m + 1, slab[:, C:])):
+            slots = pl.ds(side * HALF + n, 6, stride=WLON)
+            tokens[unit + r, 0, slots, :] = part[:, :128]
+            tokens[unit + r, 1, slots, :] = jnp.concatenate([part[:, 128:], part[:, 128:]], axis=1)
+
+    return [
+        functools.partial(piece, r, side, m) for r in range(count) for side in range(2) for m in range(6)
+    ]
+
+
+def pieces_out(frame, tokens, place, unit, count=GROUP):
+    def piece(r, side, m):
+        row, base = place(r, side)
+        for p in range(3):
+            parts = []
+            for n in (2 * m, 2 * m + 1):
+                slots = pl.ds(side * HALF + p * 24 + n, 2, stride=WLON)
+                parts.append(tokens[unit + r, 0, slots, :])
+                parts.append(tokens[unit + r, 1, slots, :][:, : C - 128])
+            lanes = pl.ds(pl.multiple_of(base + m * 2 * C, 128), 2 * C)
+            frame[row + p, :, lanes] = jnp.concatenate(parts, axis=1).astype(BF16)
+
+    return [
+        functools.partial(piece, r, side, m) for r in range(count) for side in range(2) for m in range(6)
+    ]
 
 
 def put_head(ref, slot, i, value):
@@ -197,9 +189,23 @@
     return jnp.concatenate(out, axis=0)
 
 
-def attend(x_ref, g_ref, us, bias, dbias, slot, gain, shift, wqkv, wqkv_t, wproj, wproj_t, raw_q, raw_p):
+def weight_sums(raw_q, h_t, dqkv):
+    for j in range(3):
+        raw_q[:, j * C : j * C + C] += nn(h_t, dqkv[:, j * C : j * C + C])
+
+
+def attend(
+    x_ref, g_ref, us, bias, dbias, slot, gain, shift, wqkv, wqkv_t, wproj, wproj_t, raw_q, raw_p, held_h, held_d, early, late
+):
     n = WIN
     ws = range(len(us))
+    early, late = iter(early), iter(late)
+
+    def emit(queue, count):
+        for _ in range(count):
+            step = next(queue, None)
+            if step is not None:
+                step()
 
     def tokens(ref):
         rows = [jnp.concatenate([ref[u, 0], ref[u, 1]], axis=1) for u in us]
@@ -211,24 +217,46 @@
     x = tokens(x_ref)
     g = tokens(g_ref)
     gb = g.astype(BF16)
+    do = split(nn(gb, wproj_t[...]).astype(BF16))
+    weight_sums(raw_q, held_h[...], held_d[...])
     center = x - jnp.mean(x, axis=1, keepdims=True)
     rstd = lax.rsqrt(jnp.mean(center * center, axis=1, keepdims=True) + EPS)
     xn = center * rstd
     h = (xn * gain + shift).astype(BF16)
-    q = split(nn(h, wqkv[:, :C]).astype(BF16))
-    kv = split(nn(h, wqkv[:, C:]).astype(BF16))
-    k = [a[:, :C] for a in kv]
-    v = [a[:, C:] for a in kv]
-    do = split(nn(gb, wproj_t[...]).astype(BF16))
+    held_h[...] = h.T
+    qkv = split(nn(h, wqkv[...]).astype(BF16))
+    q = [a[:, :C] for a in qkv]
+    k = [a[:, C : 2 * C] for a in qkv]
+    v = [a[:, 2 * C :] for a in qkv]
     k_t = [a.T for a in k]
     v_t = [a.T for a in v]
-    h_t = h.T
     qr = [head_rows(a) for a in q]
     dor = [head_rows(a) for a in do]
-    s = [across(k[w], qr[w]) for w in ws]
-    dp = [across(v[w], dor[w]) for w in ws]
-    pb, dsb = [], []
+    s, dp, pb, dsb, o_t, dq_t, dv, dk = {}, {}, {}, {}, {}, {}, {}, {}
+
+    def scores(w):
+        def one(out, a, rows):
+            out[w] = across(a[w], rows[w])
+
+        return [functools.partial(one, s, k, qr), functools.partial(one, dp, v, dor)]
+
+    def products(w):
+        def one(out, act, *args):
+            out[w] = act(*args).astype(BF16)
+
+        return [
+            functools.partial(one, dq_t, by_head, k_t[w], dsb[w]),
+            functools.partial(one, dk, gathered, dsb[w], qr[w]),
+            functools.partial(one, dv, gathered, pb[w], dor[w]),
+            functools.partial(one, o_t, by_head, v_t[w], pb[w]),
+        ]
+
+    for step in scores(0):
+        step()
     for w in ws:
+        ready = scores(w + 1) if w + 1 < len(us) else []
+        done = products(w - 1) if w else []
+        ready = done + ready
         ps, dss = [], []
         for b in range(7):
             lanes = slice(b * 128, b * 128 + 128)
@@ -240,26 +268,36 @@
             dbias[slot, :, lanes] += ds
             ps.append(p.astype(BF16))
             dss.append((ds * SCALE).astype(BF16))
-        pb.append(jnp.concatenate(ps, axis=1))
-        dsb.append(jnp.concatenate(dss, axis=1))
-    o_t = [by_head(v_t[w], pb[w]).astype(BF16) for w in ws]
-    dq_t = [by_head(k_t[w], dsb[w]).astype(BF16) for w in ws]
-    dv = jnp.concatenate([gathered(pb[w], dor[w]).astype(BF16) for w in ws], axis=0)
-    dk = jnp.concatenate([gathered(dsb[w], qr[w]).astype(BF16) for w in ws], axis=0)
+            if ready:
+                ready.pop(0)()
+            emit(early, 0)
+            emit(late, 0)
+        for step in ready:
+            step()
+        pb[w] = jnp.concatenate(ps, axis=1)
+        dsb[w] = jnp.concatenate(dss, axis=1)
+    for step in products(len(us) - 1):
+        step()
+    dk = [dk[w] for w in ws]
+    dv = [dv[w] for w in ws]
+    dk = jnp.concatenate(dk, axis=0)
+    dv = jnp.concatenate(dv, axis=0)
+    dq = jnp.concatenate([dq_t[w].T for w in ws], axis=0)
+    dqkv = jnp.concatenate([dq, dk, dv], axis=1)
+    held_d[...] = dqkv
+    dh = nn(dqkv, wqkv_t[...])
+    emit(late, 0)
     o = jnp.concatenate([o_t[w].T for w in ws], axis=0)
-    dq = jnp.concatenate([dq_t[w].T for w in ws], axis=0)
-    a = nn(o, wproj[...]).astype(BF16)
-    dh = nn(dq, wqkv_t[0:C]) + nn(dk, wqkv_t[C : 2 * C]) + nn(dv, wqkv_t[2 * C :])
-    raw_p[...] += sum(nn(o_t[w], gb[w * n : (w + 1) * n]) for w in ws)
-    raw_q[:, 0:C] += nn(h_t, dq)
-    raw_q[:, C : 2 * C] += nn(h_t, dk)
-    raw_q[:, 2 * C :] += nn(h_t, dv)
     dxn = dh * gain
     m1 = jnp.mean(dxn, axis=1, keepdims=True)
     m2 = jnp.mean(dxn * xn, axis=1, keepdims=True)
     dx = (rstd * (dxn - m1 - xn * m2)).astype(BF16)
+    g = split(g + dx.astype(F32))
+    a = nn(o, wproj[...]).astype(BF16)
+    raw_p[...] += sum(nn(o_t[w], gb[w * n : (w + 1) * n]) for w in ws)
     x = split(x + a.astype(F32))
-    g = split(g + dx.astype(F32))
+    emit(early, 10**6)
+    emit(late, 10**6)
     for w, u in enumerate(us):
         x_ref[u, 0] = x[w][:, :128]
         x_ref[u, 1, :, 0:64] = x[w][:, 128:]
@@ -322,6 +360,8 @@
     wproj_t,
     raw_q,
     raw_p,
+    held_h,
+    held_d,
     mine_w,
     part_w,
     part_w_in,
@@ -451,16 +491,7 @@
 
     for copy in local:
         copy.wait()
-    windows_in(fx, 3, 6, xw, 0, 0, 0, WPB - 1)
-    windows_in(fg, 3, 6, gw, 0, 0, 0, WPB - 1)
-    for copy in sides:
-        copy.wait_recv()
-    windows_in(fx, 3, 6, xw, 0, 0, WPB - 1)
-    windows_in(fg, 3, 6, gw, 0, 0, WPB - 1)
-
-    def halves_in(row, unit, slot, source, lo):
-        halves(fx, row, xw, unit, False)
-        halves(fg, row, gw, unit, False)
+    def halves_in(slot, source, lo):
         for i in range(HEADS):
             part = get_head(bias, source, i)[lo : lo + HALF, lo : lo + HALF]
             away = jnp.full((HALF, HALF), -1e9, F32)
@@ -483,29 +514,58 @@
     def _():
         for copy in polar:
             copy.wait()
-        halves_in(0, 2 * WPB, 2, 0, HALF)
+        halves_in(2, 0, HALF)
 
     @pl.when(final)
     def _():
-        halves_in(9, WPB, 1, 1, 0)
-
-    rest = (gain_ref[...], shift_ref[...], wqkv, wqkv_t, wproj, wproj_t, raw_q, raw_p)
+        halves_in(1, 1, 0)
+
+    rest = (gain_ref[...], shift_ref[...], wqkv, wqkv_t, wproj, wproj_t, raw_q, raw_p, held_h, held_d)
     full = 2 * WPB // GROUP
     half = WPB // 2 // GROUP
+    steps = jnp.where(first, full + half, jnp.where(final, full // 2 + half, full))
+
+    def place(v, r, side, spare):
+        halved = (first & (v == full)) | (final & (v == full // 2))
+        row = jnp.where(halved, jnp.where(first, 0, 9), 3 + 6 * (v // (full // 2)) + 3 * side)
+        window = jnp.where(halved, 2 * r + side, lax.rem(v, full // 2) * GROUP + r)
+        return jnp.where(spare, FROWS + 3 * side, row), HALO + window * WLANES
+
+    def laying(v, unit, out, spare=False):
+        move = pieces_out if out else pieces_in
+        at = functools.partial(lambda r, side: place(v, r, side, spare))
+        both = zip(move(fx, xw, at, unit), move(fg, gw, at, unit))
+        return [step for pair in both for step in pair]
+
+    held_h[...] = jnp.zeros_like(held_h)
+    held_d[...] = jnp.zeros_like(held_d)
+
+    def start(r, _):
+        for frame, tokens in ((fx, xw), (fg, gw)):
+            for step in pieces_in(frame, tokens, lambda _, side: place(0, r, side, False), r, 1):
+                step()
+        return 0
+
+    lax.fori_loop(0, GROUP, start, 0)
+    for copy in sides:
+        copy.wait_recv()
 
     def group(u, _):
-        @pl.when((u == full // 2) & (lat < lats - 1))
+        @pl.when((u == full // 2 - 1) & (lat < lats - 1))
         def _():
             for copy in ups + diags:
                 copy.wait_recv()
-            windows_in(fx, 9, 6, xw, WPB)
-            windows_in(fg, 9, 6, gw, WPB)
 
         slot = jnp.minimum(u // (WPB // GROUP), 2)
-        attend(xw, gw, [GROUP * u + r for r in range(GROUP)], bias, dbias, slot, *rest)
+        us = [GROUP * u + r for r in range(GROUP)]
+        behind = jnp.maximum(u - 1, 0)
+        early = laying(behind, GROUP * behind, True, u == 0)
+        late = laying(jnp.minimum(u + 1, steps - 1), GROUP * (u + 1), False)
+        attend(xw, gw, us, bias, dbias, slot, *rest, early, late)
         return 0
 
-    lax.fori_loop(0, jnp.where(first, full + half, jnp.where(final, full // 2 + half, full)), group, 0)
+    lax.fori_loop(0, steps, group, 0)
+    weight_sums(raw_q, held_h[...], held_d[...])
 
     raw = jnp.concatenate([raw_q[...], raw_p[...]], axis=1)
     for j in range(lons):
@@ -559,12 +619,27 @@
         backs.append(copy_to(frame.at[3:12, :, OWN:FRAME], side, *sems[2], lat, east))
         tops.append(copy_to(frame.at[0:3, :, OWN:FRAME], corner, *sems[3], lat, east))
 
+    def finish_out(r, _):
+        for frame, tokens in ((fx, xw), (fg, gw)):
+            at = lambda _, side: place(steps - 1, r, side, False)
+            for step in pieces_out(frame, tokens, at, GROUP * (steps - 1) + r, 1):
+                step()
+        return 0
+
+    lax.fori_loop(0, GROUP, finish_out, 0)
+
     @pl.when(lat < lats - 1)
     def _():
-        windows_out(fx, 9, 6, xw, WPB)
-        windows_out(fg, 9, 6, gw, WPB)
         for copy in downs + crosses:
             copy.start()
+
+    @pl.when(first)
+    def _():
+        for copy in tops:
+            copy.start()
+
+    for copy in backs:
+        copy.start()
 
     def add_w(d, total):
         o = lax.rem(lon + d, lons)
@@ -582,24 +657,6 @@
         return copy_to(tiles.at[0], tiles_in.at[a], tile_send.at[0], tile_recv.at[a], a, lon)
 
     each(0, TILES, lat, lambda a: tile_out(a).start())
-
-    windows_out(fx, 3, 6, xw, 0)
-    windows_out(fg, 3, 6, gw, 0)
-
-    @pl.when(first)
-    def _():
-        halves(fx, 0, xw, 2 * WPB, True)
-        halves(fg, 0, gw, 2 * WPB, True)
-        for copy in tops:
-            copy.start()
-
-    @pl.when(final)
-    def _():
-        halves(fx, 9, xw, WPB, True)
-        halves(fg, 9, gw, WPB, True)
-
-    for copy in backs:
-        copy.start()
 
     def add_t(d, total):
         o = lax.rem(lon + d, lons)
@@ -732,16 +789,21 @@
         copy.wait()
 
 
-def finish_kernel(x, g, q, p, b, x_out, g_out, q_out, p_out, b_out, sems):
-    copies = []
-    for src, dst in ((x, x_out), (g, g_out)):
+def finish_kernel(x, g, q, p, b, x_out, g_out, q_out, p_out, b_out, xs, gs, qs, ps, bs, sems):
+    moves = []
+    for src, mid, dst in ((x, xs, x_out), (g, gs, g_out)):
         for r in range(0, 12, 3):
-            copies.append((src.at[r : r + 3], dst.at[r : r + 3]))
-    copies += [(q, q_out), (p, p_out), (b, b_out)]
-    copies = [pltpu.make_async_copy(*pair, sems.at[n]) for n, pair in enumerate(copies)]
-    for copy in copies:
+            part = slice(r, r + 3)
+            moves.append((src.at[part], mid.at[part], dst.at[part]))
+    moves += [(q, qs, q_out), (p, ps, p_out), (b, bs, b_out)]
+    into = [pltpu.make_async_copy(m[0], m[1], sems.at[n]) for n, m in enumerate(moves)]
+    away = [pltpu.make_async_copy(m[1], m[2], sems.at[len(moves) + n]) for n, m in enumerate(moves)]
+    for copy in into:
         copy.start()
-    for copy in copies:
+    for first, second in zip(into, away):
+        first.wait()
+        second.start()
+    for copy in away:
         copy.wait()
 
 
@@ -752,7 +814,8 @@
         in_specs=[hbm] * 5,
         out_specs=[hbm] * 5,
         out_shape=[jax.ShapeDtypeStruct(a.shape, a.dtype) for a in results],
-        scratch_shapes=[pltpu.SemaphoreType.DMA((11,))],
+        scratch_shapes=[pltpu.VMEM(a.shape, a.dtype) for a in results]
+        + [pltpu.SemaphoreType.DMA((22,))],
         compiler_params=pltpu.CompilerParams(vmem_limit_bytes=56 * 2**20),
         name="finish",
     )(*results)
@@ -764,7 +827,7 @@
     vmem = pl.BlockSpec(memory_space=pltpu.VMEM)
     hbm = pl.BlockSpec(memory_space=pl.ANY)
     shape = jax.ShapeDtypeStruct
-    units = 2 * WPB + WPB // 2
+    units = 2 * WPB + WPB // 2 + GROUP
     sems = pltpu.SemaphoreType.DMA
     counts = [4, 6, 6, 8, 8] + [lons] * 4 + [lats] * 4 + [lons] * 4 + [lats] * 2
     results = pl.pallas_call(
@@ -779,8 +842,8 @@
             shape((HEADS, 2, POS), F32),
         ],
         scratch_shapes=[
-            pltpu.VMEM((FROWS, 2, FRAME), BF16),
-            pltpu.VMEM((FROWS, 2, FRAME), BF16),
+            pltpu.VMEM((FROWS + 6, 2, FRAME), BF16),
+            pltpu.VMEM((FROWS + 6, 2, FRAME), BF16),
             pltpu.VMEM((units, 2, WIN, 128), F32),
             pltpu.VMEM((units, 2, WIN, 128), F32),
             pltpu.VMEM((3, WIN, 896), F32),
@@ -792,6 +855,8 @@
             pltpu.VMEM((C, C), BF16),
             pltpu.VMEM((C, 3 * C), F32),
             pltpu.VMEM((C, C), F32),
+            pltpu.VMEM((C, GROUP * WIN), BF16),
+            pltpu.VMEM((GROUP * WIN, 3 * C), BF16),
             pltpu.VMEM((lons, 16, WCHUNK), F32),
             pltpu.VMEM((lons, 16, WCHUNK), BF16),
             pltpu.VMEM((lons, 16, WCHUNK), BF16),

time: 146 us -> 68.9 us (0.47)
  Pallas kernels: 146 us -> 68.1 us
    pallas_call x1, Pallas kernels: 80.5 us -> 2.78 us  [finish(): pl.pallas_call(finish_kernel, in_specs=[hbm] * 5, out_specs=[hbm] * 5, ou...]
where the time goes in v6:
time: 68.9 us; the launch traced here: 68.7 us
  Pallas kernels  68.1 us (99%)
    pallas_call x1, Pallas kernels, on_device(): pl.pallas_call(functools.partial(kernel, lats, lons), in_specs=[hbm, hbm]...  65.3 us
    pallas_call x1, Pallas kernels, finish(): pl.pallas_call(finish_kernel, in_specs=[hbm] * 5, out_specs=[hbm] * 5, ou...  2.78 us

profile of v6, /device:TPU:1, one launch (start us, length us, event | category | flops | bytes accessed | tf_op | source)
XLA Modules:
  0.0 68.7 jit_solution(3540583494831929679)
XLA Ops:
  0.6 65.3 %windows.1 = (bf16[12,2,18432]{2,1,0:T(2,128)(2,1)}, bf16[12,2,18432]{2,1,0:T(2,128)(2,1)}, f32[192,576]{1,0:T(8,128)}, f32[192,192]{1,0:T(8,128)}, f32[6,2,3312]{2,1,0:T(2,128)}) custom-call(bf16[12,2,18432]{2,1,0:T(2,128)(2,1)} %bitcast.8, bf16[12,2,18432]{2,1,0:T(2,128)(2,1)} %bitcast.9, f32[1,192]{1,0:T(1,128)} %bitcast.11, f32[1,192]{1,0:T(1,128)} %bitcast.12, ...), custom_call_target="tpu_custom_call" | custom-call | tf_op jit(solution)/shard_map/windows/pallas_call | solution.py:833
  65.9 2.8 %finish.1 = (bf16[12,2,18432]{2,1,0:T(2,128)(2,1)}, bf16[12,2,18432]{2,1,0:T(2,128)(2,1)}, f32[192,576]{1,0:T(8,128)}, f32[192,192]{1,0:T(8,128)}, f32[6,2,3312]{2,1,0:T(2,128)}) custom-call(bf16[12,2,18432]{2,1,0:T(2,128)(2,1)} %get-tuple-element.15.x, bf16[12,2,18432]{2,1,0:T(2,128)(2,1)} %get-tuple-element.16.g, f32[192,576]{1,0:T(8,128)} %get-tuple-element.17.q, ...), custom_call_target="tpu_custom_call" | custom-call | tf_op jit(solution)/shard_map/finish/pallas_call | solution.py:812

commit v7 on v6

--- a/solution.py
+++ b/solution.py
@@ -28,9 +28,10 @@
 WPB = 8
 POS = 3312
 TABLE = 4096
-WCHUNK = 12 * 768 // 8
+WTILES = 72
+PARTS = 16
+PTILES = 5
 TCHUNK = TABLE // 8
-TILES = WCHUNK // 128
 MESH = pl.DeviceIdType.MESH
 EPS = 1e-5
 SCALE = HD**-0.5
@@ -251,33 +252,39 @@
             functools.partial(one, o_t, by_head, v_t[w], pb[w]),
         ]
 
-    for step in scores(0):
-        step()
-    for w in ws:
-        ready = scores(w + 1) if w + 1 < len(us) else []
-        done = products(w - 1) if w else []
-        ready = done + ready
-        ps, dss = [], []
+    halves = [ws[n : n + 2] for n in range(0, len(us), 2)]
+    for w in halves[0]:
+        for step in scores(w):
+            step()
+    for at, duo in enumerate(halves):
+        ready = [step for w in halves[at - 1] for step in products(w)] if at else []
+        if at + 1 < len(halves):
+            ready += [step for w in halves[at + 1] for step in scores(w)]
+        ps, dss = {w: [] for w in duo}, {w: [] for w in duo}
         for b in range(7):
             lanes = slice(b * 128, b * 128 + 128)
-            t = s[w][:, lanes] * (SCALE * LOG2E) + bias[slot, :, lanes]
-            e = jnp.exp2(t - jnp.max(t, axis=0, keepdims=True))
-            p = e * (1.0 / jnp.sum(e, axis=0, keepdims=True))
-            d = dp[w][:, lanes]
-            ds = p * (d - jnp.sum(p * d, axis=0, keepdims=True))
-            dbias[slot, :, lanes] += ds
-            ps.append(p.astype(BF16))
-            dss.append((ds * SCALE).astype(BF16))
-            if ready:
-                ready.pop(0)()
-            emit(early, 0)
-            emit(late, 0)
+            add = bias[slot, :, lanes]
+            change = 0.0
+            for w in duo:
+                t = s[w][:, lanes] * (SCALE * LOG2E) + add
+                e = jnp.exp2(t - jnp.max(t, axis=0, keepdims=True))
+                p = e * (1.0 / jnp.sum(e, axis=0, keepdims=True))
+                d = dp[w][:, lanes]
+                ds = p * (d - jnp.sum(p * d, axis=0, keepdims=True))
+                change = change + ds
+                ps[w].append(p.astype(BF16))
+                dss[w].append((ds * SCALE).astype(BF16))
+                if ready:
+                    ready.pop(0)()
+            dbias[slot, :, lanes] += change
         for step in ready:
             step()
-        pb[w] = jnp.concatenate(ps, axis=1)
-        dsb[w] = jnp.concatenate(dss, axis=1)
-    for step in products(len(us) - 1):
-        step()
+        for w in duo:
+            pb[w] = jnp.concatenate(ps[w], axis=1)
+            dsb[w] = jnp.concatenate(dss[w], axis=1)
+    for w in halves[-1]:
+        for step in products(w):
+            step()
     dk = [dk[w] for w in ws]
     dv = [dv[w] for w in ws]
     dk = jnp.concatenate(dk, axis=0)
@@ -344,9 +351,9 @@
     table,
     x_out,
     g_out,
-    grad_q,
-    grad_p,
-    grad_bias,
+    sum_w,
+    sum_t,
+    squares,
     fx,
     fg,
     xw,
@@ -365,15 +372,10 @@
     mine_w,
     part_w,
     part_w_in,
-    tiles,
-    tiles_in,
-    joined,
-    sum_w,
+    cross,
     mine_t,
     part_t,
     part_t_in,
-    sum_t,
-    squares,
     own_sem,
     halo_send,
     halo_recv,
@@ -385,8 +387,6 @@
     t_recv,
     tile_send,
     tile_recv,
-    join_send,
-    join_recv,
     wb_send,
     wb_recv,
     tb_send,
@@ -401,8 +401,12 @@
     first = lat == 0
     final = lat == lats - 1
     barrier = pltpu.get_barrier_semaphore()
-    each(0, lons, lon, lambda o: greet(lat, o))
-    each(0, lats, lat, lambda a: greet(a, lon))
+    core = lax.rem(lat, 2)
+    base = lat - core
+    own = 2 * lon + core
+    each(0, PARTS, own, lambda m: greet(base + lax.rem(m, 2), m // 2))
+    each(0, lats // 2, lat // 2, lambda a: greet(2 * a, lon))
+    each(0, lats // 2, lat // 2, lambda a: greet(2 * a + 1, lon))
 
     @pl.when(lat > 0)
     def _():
@@ -474,7 +478,7 @@
     bias[:, :, 768:] = jnp.zeros((3, WIN, 128), F32)
     bias_rows(table, flat, rows_scratch)
     bias_in(0, 6, pick, rows_scratch, shifted, bias)
-    peers = lons - 1 + lats - 1
+    peers = PARTS - 1 + lats - 2
     pl.semaphore_wait(barrier, peers + jnp.where(lat > 0, 1, 0) + jnp.where(lat < lats - 1, 1, 0))
     for copy in sides:
         copy.start()
@@ -568,45 +572,25 @@
     weight_sums(raw_q, held_h[...], held_d[...])
 
     raw = jnp.concatenate([raw_q[...], raw_p[...]], axis=1)
-    for j in range(lons):
+    for m in range(PARTS):
         row = []
-        for t in range(TILES):
-            col = j * TILES + t
+        for col in range(m * PTILES, m * PTILES + PTILES):
             r, c = col // 6 * 16, col % 6 * 128
-            row.append(raw[r : r + 16, c : c + 128])
+            row.append(raw[r : r + 16, c : c + 128] if col < WTILES else jnp.zeros((16, 128), F32))
         chunk = jnp.concatenate(row, axis=1)
-        mine_w[j] = chunk
-        part_w[j] = chunk.astype(BF16)
-
-    def w_out(o):
-        return copy_to(part_w.at[o], part_w_in.at[lon], w_send.at[o], w_recv.at[lon], lat, o)
-
-    def w_in(o):
-        return copy_to(part_w.at[o], part_w_in.at[o], w_send.at[o], w_recv.at[o], lat, o)
-
-    each(0, lons, lon, lambda o: w_out(o).start())
-
-    @pl.when(first)
-    def _():
-        halves_grad(2, 0, HALF)
-
-    @pl.when(final)
-    def _():
-        halves_grad(1, 1, 0)
-
-    grads = bias_out(dbias, pick, shifted, rows_scratch)
-    for j in range(lons):
-        chunk = grads[:, j * TCHUNK : (j + 1) * TCHUNK]
-        mine_t[j] = chunk
-        part_t[j] = chunk.astype(BF16)
-
-    def t_out(o):
-        return copy_to(part_t.at[o], part_t_in.at[lon], t_send.at[o], t_recv.at[lon], lat, o)
-
-    def t_in(o):
-        return copy_to(part_t.at[o], part_t_in.at[o], t_send.at[o], t_recv.at[o], lat, o)
-
-    each(0, lons, lon, lambda o: t_out(o).start())
+        mine_w[m] = chunk
+        part_w[m] = chunk.astype(BF16)
+
+    def member(m):
+        return base + lax.rem(m, 2), m // 2
+
+    def w_out(m):
+        return copy_to(part_w.at[m], part_w_in.at[own], w_send.at[m], w_recv.at[own], *member(m))
+
+    def w_in(m):
+        return copy_to(part_w.at[m], part_w_in.at[m], w_send.at[m], w_recv.at[m], *member(m))
+
+    each(0, PARTS, own, lambda m: w_out(m).start())
 
     downs, crosses, backs, tops = [], [], [], []
     for n, frame in enumerate((fx, fg)):
@@ -641,22 +625,45 @@
     for copy in backs:
         copy.start()
 
+    @pl.when(first)
+    def _():
+        halves_grad(2, 0, HALF)
+
+    @pl.when(final)
+    def _():
+        halves_grad(1, 1, 0)
+
+    grads = bias_out(dbias, pick, shifted, rows_scratch)
+    for j in range(lons):
+        chunk = grads[:, j * TCHUNK : (j + 1) * TCHUNK]
+        mine_t[j] = chunk
+        part_t[j] = chunk.astype(BF16)
+
+    def t_out(o):
+        return copy_to(part_t.at[o], part_t_in.at[lon], t_send.at[o], t_recv.at[lon], lat, o)
+
+    def t_in(o):
+        return copy_to(part_t.at[o], part_t_in.at[o], t_send.at[o], t_recv.at[o], lat, o)
+
+    each(0, lons, lon, lambda o: t_out(o).start())
+
     def add_w(d, total):
-        o = lax.rem(lon + d, lons)
-        w_in(o).wait_recv()
-        return total + part_w_in[o].astype(F32)
-
-    total = lax.fori_loop(1, lons, add_w, mine_w[lon])
-    for t in range(TILES):
-        tiles[t] = total[:, t * 128 : t * 128 + 128].astype(BF16)
-
-    def tile_out(a):
-        return copy_to(tiles.at[a], tiles_in.at[lat], tile_send.at[a], tile_recv.at[lat], a, lon)
-
-    def tile_in(a):
-        return copy_to(tiles.at[0], tiles_in.at[a], tile_send.at[0], tile_recv.at[a], a, lon)
-
-    each(0, TILES, lat, lambda a: tile_out(a).start())
+        m = lax.rem(own + d, PARTS)
+        w_in(m).wait_recv()
+        return total + part_w_in[m].astype(F32)
+
+    chip = lat // 2
+    cross[chip] = lax.fori_loop(1, PARTS, add_w, mine_w[own]).astype(BF16)
+
+    def cross_out(a):
+        at = cross.at[chip]
+        return copy_to(at, at, tile_send.at[a], tile_recv.at[chip], 2 * a + core, lon)
+
+    def cross_in(a):
+        at = cross.at[a]
+        return copy_to(at, at, tile_send.at[a], tile_recv.at[a], 2 * a + core, lon)
+
+    each(0, lats // 2, chip, lambda a: cross_out(a).start())
 
     def add_t(d, total):
         o = lax.rem(lon + d, lons)
@@ -673,33 +680,19 @@
 
     each(0, lons, lon, lambda o: tb_out(o).start())
 
-    def join_out(a):
-        return copy_to(joined.at[lat], joined.at[lat], join_send.at[a], join_recv.at[lat], a, lon)
-
-    def join_in(a):
-        return copy_to(joined.at[a], joined.at[a], join_send.at[a], join_recv.at[a], a, lon)
-
-    @pl.when(lat < TILES)
-    def _():
-        def add_tile(d, total):
-            a = lax.rem(lat + d, lats)
-            tile_in(a).wait_recv()
-            return total + tiles_in[a].astype(F32)
-
-        total = lax.fori_loop(1, lats, add_tile, tiles[lat].astype(F32))
-        joined[lat] = total.astype(BF16)
-        each(0, lats, lat, lambda a: join_out(a).start())
-
-    each(0, TILES, lat, lambda a: join_in(a).wait_recv())
-    sum_w[lon] = jnp.concatenate([joined[t] for t in range(TILES)], axis=1)
-
-    def wb_out(o):
-        return copy_to(sum_w.at[lon], sum_w.at[lon], wb_send.at[o], wb_recv.at[lon], lat, o)
-
-    def wb_in(o):
-        return copy_to(sum_w.at[o], sum_w.at[o], wb_send.at[o], wb_recv.at[o], lat, o)
-
-    each(0, lons, lon, lambda o: wb_out(o).start())
+    each(0, lats // 2, chip, lambda a: cross_in(a).wait_recv())
+    total = cross[0].astype(F32)
+    for a in range(1, lats // 2):
+        total = total + cross[a].astype(F32)
+    sum_w[own] = total.astype(BF16)
+
+    def wb_out(m):
+        return copy_to(sum_w.at[own], sum_w.at[own], wb_send.at[m], wb_recv.at[own], *member(m))
+
+    def wb_in(m):
+        return copy_to(sum_w.at[m], sum_w.at[m], wb_send.at[m], wb_recv.at[m], *member(m))
+
+    each(0, PARTS, own, lambda m: wb_out(m).start())
 
     each(0, lons, lon, lambda o: tb_in(o).wait_recv())
     whole = jnp.concatenate([sum_t[j].astype(F32) for j in range(lons)], axis=1)
@@ -740,81 +733,95 @@
         copy.start()
 
     each(0, lats, lat, lambda a: sq_in(a).wait_recv())
-    table_squares = jnp.zeros((1, 1), F32)
-    for a in range(lats):
-        table_squares = table_squares + squares[a][0:1, 0:1]
-    table_rms = jnp.sqrt(table_squares / (lats * 2 * HEADS * POS) + 1e-6)
-    whole = whole[:, :POS] / table_rms
-    for i in range(HEADS):
-        grad_bias[i] = whole[2 * i : 2 * i + 2]
-
-    each(0, lons, lon, lambda o: wb_in(o).wait_recv())
+    each(0, PARTS, own, lambda m: wb_in(m).wait_recv())
+
+    def sent_w(m):
+        w_out(m).wait_send()
+        wb_out(m).wait_send()
+
+    def sent_t(o):
+        t_out(o).wait_send()
+        tb_out(o).wait_send()
+
+    each(0, PARTS, own, sent_w)
+    each(0, lons, lon, sent_t)
+    each(0, lats // 2, chip, lambda a: cross_out(a).wait_send())
+    each(0, lats, lat, lambda a: sq_out(a).wait_send())
+
+    for copy in sides:
+        copy.wait_send()
+
+    @pl.when(lat > 0)
+    def _():
+        for copy in ups + diags:
+            copy.wait_send()
+
+    for copy in leave:
+        copy.wait()
+
+
+def finish_kernel(lats, lons, x, g, sum_w, sum_t, squares, x_out, g_out, q_out, p_out, b_out, xs, gs, ws, ts, ss, grad_q, grad_p, grad_bias, sems):
+    small = [(sum_w, ws), (sum_t, ts), (squares, ss)]
+    moves = []
+    for src, mid, dst in ((x, xs, x_out), (g, gs, g_out)):
+        for r in range(0, 12, 3):
+            part = slice(r, r + 3)
+            moves.append((src.at[part], mid.at[part], dst.at[part]))
+    into = [pltpu.make_async_copy(m[0], m[1], sems.at[n]) for n, m in enumerate(moves)]
+    away = [pltpu.make_async_copy(m[1], m[2], sems.at[8 + n]) for n, m in enumerate(moves)]
+    small = [pltpu.make_async_copy(*pair, sems.at[16 + n]) for n, pair in enumerate(small)]
+    ends = ((grad_q, q_out), (grad_p, p_out), (grad_bias, b_out))
+    ends = [pltpu.make_async_copy(*pair, sems.at[19 + n]) for n, pair in enumerate(ends)]
+    for copy in small + into:
+        copy.start()
+    for copy in small:
+        copy.wait()
     cols = []
     square = jnp.zeros((16, 128), F32)
-    for j in range(lons):
-        for t in range(TILES):
-            piece = sum_w[j, :, t * 128 : t * 128 + 128].astype(F32)
-            square = square + piece * piece
-            cols.append(piece)
+    for col in range(WTILES):
+        m, t = col // PTILES, col % PTILES
+        piece = ws[m, :, t * 128 : t * 128 + 128].astype(F32)
+        square = square + piece * piece
+        cols.append(piece)
     rms = jnp.sqrt(jnp.sum(square).reshape(1, 1) / (4 * C * C) + 1e-6)
     inverse = 1.0 / rms
     for r in range(12):
         row = jnp.concatenate(cols[r * 6 : r * 6 + 6], axis=1) * inverse
         grad_q[r * 16 : r * 16 + 16] = row[:, : 3 * C]
         grad_p[r * 16 : r * 16 + 16] = row[:, 3 * C :]
-
-    def sent(o):
-        w_out(o).wait_send()
-        t_out(o).wait_send()
-        tb_out(o).wait_send()
-        wb_out(o).wait_send()
-
-    each(0, lons, lon, sent)
-    each(0, TILES, lat, lambda a: tile_out(a).wait_send())
-    each(0, lats, lat, lambda a: sq_out(a).wait_send())
-
-    @pl.when(lat < TILES)
-    def _():
-        each(0, lats, lat, lambda a: join_out(a).wait_send())
-
-    for copy in sides:
-        copy.wait_send()
-
-    @pl.when(lat > 0)
-    def _():
-        for copy in ups + diags:
-            copy.wait_send()
-
-    for copy in leave:
-        copy.wait()
-
-
-def finish_kernel(x, g, q, p, b, x_out, g_out, q_out, p_out, b_out, xs, gs, qs, ps, bs, sems):
-    moves = []
-    for src, mid, dst in ((x, xs, x_out), (g, gs, g_out)):
-        for r in range(0, 12, 3):
-            part = slice(r, r + 3)
-            moves.append((src.at[part], mid.at[part], dst.at[part]))
-    moves += [(q, qs, q_out), (p, ps, p_out), (b, bs, b_out)]
-    into = [pltpu.make_async_copy(m[0], m[1], sems.at[n]) for n, m in enumerate(moves)]
-    away = [pltpu.make_async_copy(m[1], m[2], sems.at[len(moves) + n]) for n, m in enumerate(moves)]
-    for copy in into:
-        copy.start()
+    ends[0].start()
+    ends[1].start()
     for first, second in zip(into, away):
         first.wait()
         second.start()
-    for copy in away:
+    table_squares = jnp.zeros((1, 1), F32)
+    for a in range(lats):
+        table_squares = table_squares + ss[a][0:1, 0:1]
+    table_rms = jnp.sqrt(table_squares / (lats * 2 * HEADS * POS) + 1e-6)
+    whole = jnp.concatenate([ts[j].astype(F32) for j in range(lons)], axis=1)
+    whole = whole[:, :POS] * (1.0 / table_rms)
+    for i in range(HEADS):
+        grad_bias[i] = whole[2 * i : 2 * i + 2]
+    ends[2].start()
+    for copy in away + ends:
         copy.wait()
 
 
-def finish(*results):
+def finish(lats, lons, *results):
     hbm = pl.BlockSpec(memory_space=pl.ANY)
+    shapes = [
+        jax.ShapeDtypeStruct((12, 2, OWN), BF16),
+        jax.ShapeDtypeStruct((12, 2, OWN), BF16),
+        jax.ShapeDtypeStruct((C, 3 * C), F32),
+        jax.ShapeDtypeStruct((C, C), F32),
+        jax.ShapeDtypeStruct((HEADS, 2, POS), F32),
+    ]
     return pl.pallas_call(
-        finish_kernel,
+        functools.partial(finish_kernel, lats, lons),
         in_specs=[hbm] * 5,
         out_specs=[hbm] * 5,
-        out_shape=[jax.ShapeDtypeStruct(a.shape, a.dtype) for a in results],
-        scratch_shapes=[pltpu.VMEM(a.shape, a.dtype) for a in results]
+        out_shape=shapes,
+        scratch_shapes=[pltpu.VMEM(a.shape, a.dtype) for a in list(results) + shapes[2:]]
         + [pltpu.SemaphoreType.DMA((22,))],
         compiler_params=pltpu.CompilerParams(vmem_limit_bytes=56 * 2**20),
         name="finish",
@@ -829,7 +836,7 @@
     shape = jax.ShapeDtypeStruct
     units = 2 * WPB + WPB // 2 + GROUP
     sems = pltpu.SemaphoreType.DMA
-    counts = [4, 6, 6, 8, 8] + [lons] * 4 + [lats] * 4 + [lons] * 4 + [lats] * 2
+    counts = [4, 6, 6, 8, 8] + [PARTS] * 2 + [lons] * 2 + [lats // 2] * 2 + [PARTS] * 2 + [lons] * 2 + [lats] * 2
     results = pl.pallas_call(
         functools.partial(kernel, lats, lons),
         in_specs=[hbm, hbm] + [vmem] * 5,
@@ -837,9 +844,9 @@
         out_shape=[
             shape((12, 2, OWN), BF16),
             shape((12, 2, OWN), BF16),
-            shape((C, 3 * C), F32),
-            shape((C, C), F32),
-            shape((HEADS, 2, POS), F32),
+            shape((PARTS, 16, PTILES * 128), BF16),
+            shape((lons, 16, TCHUNK), BF16),
+            shape((lats, 8, 128), F32),
         ],
         scratch_shapes=[
             pltpu.VMEM((FROWS + 6, 2, FRAME), BF16),
@@ -857,18 +864,13 @@
             pltpu.VMEM((C, C), F32),
             pltpu.VMEM((C, GROUP * WIN), BF16),
             pltpu.VMEM((GROUP * WIN, 3 * C), BF16),
-            pltpu.VMEM((lons, 16, WCHUNK), F32),
-            pltpu.VMEM((lons, 16, WCHUNK), BF16),
-            pltpu.VMEM((lons, 16, WCHUNK), BF16),
-            pltpu.VMEM((TILES, 16, 128), BF16),
-            pltpu.VMEM((lats, 16, 128), BF16),
-            pltpu.VMEM((TILES, 16, 128), BF16),
-            pltpu.VMEM((lons, 16, WCHUNK), BF16),
+            pltpu.VMEM((PARTS, 16, PTILES * 128), F32),
+            pltpu.VMEM((PARTS, 16, PTILES * 128), BF16),
+            pltpu.VMEM((PARTS, 16, PTILES * 128), BF16),
+            pltpu.VMEM((lats // 2, 16, PTILES * 128), BF16),
             pltpu.VMEM((lons, 16, TCHUNK), F32),
             pltpu.VMEM((lons, 16, TCHUNK), BF16),
             pltpu.VMEM((lons, 16, TCHUNK), BF16),
-            pltpu.VMEM((lons, 16, TCHUNK), BF16),
-            pltpu.VMEM((lats, 8, 128), F32),
         ]
         + [sems((n,)) for n in counts],
         compiler_params=pltpu.CompilerParams(
@@ -884,7 +886,7 @@
         w_proj,
         bias_table.transpose(1, 0, 2),
     )
-    x_out, g_out, grad_q, grad_p, grad_bias = finish(*results)
+    x_out, g_out, grad_q, grad_p, grad_bias = finish(lats, lons, *results)
     x_out, g_out, grad_bias = (a.transpose(1, 0, 2) for a in (x_out, g_out, grad_bias))
     return x_out, g_out, grad_q, grad_p, grad_bias
 

time: 68.9 us -> 64 us (0.929)
  Pallas kernels: 68.1 us -> 63.1 us
    pallas_call x1, Pallas kernels: 65.3 us -> 60.2 us  [on_device(): pl.pallas_call(functools.partial(kernel, lats, lons), in_specs=[hbm, hbm]...]
where the time goes in v7:
time: 64 us; the launch traced here: 63.8 us
  Pallas kernels  63.1 us (99%)
  between operations  0.64 us (1%)
    pallas_call x1, Pallas kernels, on_device(): pl.pallas_call(functools.partial(kernel, lats, lons), in_specs=[hbm, hbm]...  60.2 us
    pallas_call x1, Pallas kernels, finish(): pl.pallas_call(functools.partial(finish_kernel, lats, lons), in_specs=[hb...  2.91 us

profile of v7, /device:TPU:1, one launch (start us, length us, event | category | flops | bytes accessed | tf_op | source)
XLA Modules:
  0.0 63.8 jit_solution(16313389434707364961)
XLA Ops:
  0.6 60.2 %windows.1 = (bf16[12,2,18432]{2,1,0:T(2,128)(2,1)}, bf16[12,2,18432]{2,1,0:T(2,128)(2,1)}, bf16[16,16,640]{2,1,0:T(8,128)(2,1)}, bf16[8,16,512]{2,1,0:T(8,128)(2,1)}, f32[16,8,128]{2,1,0:T(8,128)}) custom-call(bf16[12,2,18432]{2,1,0:T(2,128)(2,1)} %bitcast.8, bf16[12,2,18432]{2,1,0:T(2,128)(2,1)} %bitcast.9, f32[1,192]{1,0:T(1,128)} %bitcast.11, ...), custom_call_target="tpu_custom_call" | custom-call | tf_op jit(solution)/shard_map/windows/pallas_call | solution.py:840
  60.9 2.9 %finish.1 = (bf16[12,2,18432]{2,1,0:T(2,128)(2,1)}, bf16[12,2,18432]{2,1,0:T(2,128)(2,1)}, f32[192,576]{1,0:T(8,128)}, f32[192,192]{1,0:T(8,128)}, f32[6,2,3312]{2,1,0:T(2,128)}) custom-call(bf16[12,2,18432]{2,1,0:T(2,128)(2,1)} %get-tuple-element.15.x, bf16[12,2,18432]{2,1,0:T(2,128)(2,1)} %get-tuple-element.16.g, ...), custom_call_target="tpu_custom_call" | custom-call | tf_op jit(solution)/shard_map/finish/pallas_call | solution.py:819

commit v8 on v7

--- a/solution.py
+++ b/solution.py
@@ -52,13 +52,13 @@
     return lax.dot_general(a, b, (((0,), (0,)), ((), ())), preferred_element_type=F32)
 
 
-def pick_matrix():
+def pick_matrix(lq):
     row = lax.broadcasted_iota(jnp.int32, (WIN, 1), 0)
     lk = lax.rem(row, WLON)
     block = lax.div(row, WLON)
     kb = lax.rem(block, 2) * 6 + lax.div(block, 2)
     col = lax.broadcasted_iota(jnp.int32, (WIN, ROWPAD), 1)
-    return jnp.where(col == kb * SPAN + 11 - lk, 1.0, 0.0).astype(BF16)
+    return jnp.where(col == kb * SPAN + 11 + lq - lk, 1.0, 0.0).astype(BF16)
 
 
 def pieces_in(frame, tokens, place, unit, count=GROUP):
@@ -128,21 +128,26 @@
         put_head(bias, n % 2, n // 2, total * LOG2E)
 
 
-def bias_out(grads, pick, shifted, rows_scratch):
+def bias_out(grads, natural):
     for n in range(12):
-        full = nn(get_head(grads, n % 2, n // 2).astype(BF16).T, pick)
-        for t in range(3):
-            shifted[t] = full[:, t * 128 : t * 128 + 128]
-        total = jnp.zeros((16, ROWPAD), F32)
-        for lq in range(WLON):
-            rows = [shifted[t, pl.ds(lq, 12, stride=12), :] for t in range(3)]
-            rows = jnp.concatenate(rows, axis=1)
-            rows = jnp.concatenate([rows, jnp.zeros((4, ROWPAD), F32)], axis=0)
-            total = total + (pltpu.roll(rows, lq, 1) if lq else rows)
-        rows_scratch[:, n, :] = total[:12]
-    parts = [rows_scratch[pq * 2 + zq][:, :ROWLEN] for zq in range(2) for pq in range(6)]
-    parts.append(jnp.zeros((16, TABLE - POS), F32))
-    return jnp.concatenate(parts, axis=1)
+        full = get_head(grads, n % 2, n // 2).astype(BF16).T.astype(F32)
+        block = slice(n * WIN, n * WIN + WIN)
+        natural[0, block, :] = full[:, :128]
+        natural[1, block, 0 : WIN - 128] = full[:, 128:]
+    total = jnp.zeros((WIN, ROWPAD), F32)
+    for lq in range(WLON):
+        rows = [natural[0, pl.ds(lq, WIN, stride=WLON), :]]
+        rows.append(natural[1, pl.ds(lq, WIN, stride=WLON), :][:, : WIN - 128])
+        total = total + nn(jnp.concatenate(rows, axis=1).astype(BF16), pick_matrix(lq))
+    for t in range(3):
+        natural[2, t * WIN : t * WIN + WIN, :] = total[:, t * 128 : t * 128 + 128]
+    parts = []
+    for zq in range(2):
+        for pq in range(6):
+            part = [natural[2, pl.ds(t * WIN + pq * 2 + zq, 12, stride=12), :] for t in range(3)]
+            parts.append(jnp.concatenate(part, axis=1)[:, :ROWLEN])
+    parts.append(jnp.zeros((12, TABLE - POS), F32))
+    return jnp.concatenate([jnp.concatenate(parts, axis=1), jnp.zeros((4, TABLE), F32)], axis=0)
 
 
 def head_rows(a):
@@ -362,6 +367,7 @@
     dbias,
     rows_scratch,
     shifted,
+    natural,
     flat,
     wqkv_t,
     wproj_t,
@@ -474,7 +480,7 @@
                 west,
             )
         )
-    pick = pick_matrix()
+    pick = pick_matrix(0)
     bias[:, :, 768:] = jnp.zeros((3, WIN, 128), F32)
     bias_rows(table, flat, rows_scratch)
     bias_in(0, 6, pick, rows_scratch, shifted, bias)
@@ -571,27 +577,6 @@
     lax.fori_loop(0, steps, group, 0)
     weight_sums(raw_q, held_h[...], held_d[...])
 
-    raw = jnp.concatenate([raw_q[...], raw_p[...]], axis=1)
-    for m in range(PARTS):
-        row = []
-        for col in range(m * PTILES, m * PTILES + PTILES):
-            r, c = col // 6 * 16, col % 6 * 128
-            row.append(raw[r : r + 16, c : c + 128] if col < WTILES else jnp.zeros((16, 128), F32))
-        chunk = jnp.concatenate(row, axis=1)
-        mine_w[m] = chunk
-        part_w[m] = chunk.astype(BF16)
-
-    def member(m):
-        return base + lax.rem(m, 2), m // 2
-
-    def w_out(m):
-        return copy_to(part_w.at[m], part_w_in.at[own], w_send.at[m], w_recv.at[own], *member(m))
-
-    def w_in(m):
-        return copy_to(part_w.at[m], part_w_in.at[m], w_send.at[m], w_recv.at[m], *member(m))
-
-    each(0, PARTS, own, lambda m: w_out(m).start())
-
     downs, crosses, backs, tops = [], [], [], []
     for n, frame in enumerate((fx, fg)):
         rows = frame.at[0:3, :, HALO:OWN]
@@ -625,6 +610,27 @@
     for copy in backs:
         copy.start()
 
+    raw = jnp.concatenate([raw_q[...], raw_p[...]], axis=1)
+    for m in range(PARTS):
+        row = []
+        for col in range(m * PTILES, m * PTILES + PTILES):
+            r, c = col // 6 * 16, col % 6 * 128
+            row.append(raw[r : r + 16, c : c + 128] if col < WTILES else jnp.zeros((16, 128), F32))
+        chunk = jnp.concatenate(row, axis=1)
+        mine_w[m] = chunk
+        part_w[m] = chunk.astype(BF16)
+
+    def member(m):
+        return base + lax.rem(m, 2), m // 2
+
+    def w_out(m):
+        return copy_to(part_w.at[m], part_w_in.at[own], w_send.at[m], w_recv.at[own], *member(m))
+
+    def w_in(m):
+        return copy_to(part_w.at[m], part_w_in.at[m], w_send.at[m], w_recv.at[m], *member(m))
+
+    each(0, PARTS, own, lambda m: w_out(m).start())
+
     @pl.when(first)
     def _():
         halves_grad(2, 0, HALF)
@@ -633,7 +639,7 @@
     def _():
         halves_grad(1, 1, 0)
 
-    grads = bias_out(dbias, pick, shifted, rows_scratch)
+    grads = bias_out(dbias, natural)
     for j in range(lons):
         chunk = grads[:, j * TCHUNK : (j + 1) * TCHUNK]
         mine_t[j] = chunk
@@ -857,6 +863,7 @@
             pltpu.VMEM((3, WIN, 896), F32),
             pltpu.VMEM((12, 16, ROWPAD), F32),
             pltpu.VMEM((3, WIN, 128), F32),
+            pltpu.VMEM((3, 12 * WIN, 128), F32),
             pltpu.VMEM((16, 3328), F32),
             pltpu.VMEM((3 * C, C), BF16),
             pltpu.VMEM((C, C), BF16),

time: 64 us -> 63.3 us (0.989)
    pallas_call x1, Pallas kernels: 60.2 us -> 59.6 us  [on_device(): pl.pallas_call(functools.partial(kernel, lats, lons), in_specs=[hbm, hbm]...]
where the time goes in v8:
time: 63.3 us; the launch traced here: 63.1 us
  Pallas kernels  62.5 us (99%)
  between operations  0.64 us (1%)
    pallas_call x1, Pallas kernels, on_device(): pl.pallas_call(functools.partial(kernel, lats, lons), in_specs=[hbm, hbm]...  59.6 us
    pallas_call x1, Pallas kernels, finish(): pl.pallas_call(functools.partial(finish_kernel, lats, lons), in_specs=[hb...  2.91 us

profile of v8, /device:TPU:1, one launch (start us, length us, event | category | flops | bytes accessed | tf_op | source)
XLA Modules:
  0.0 63.1 jit_solution(6095391002456436681)
XLA Ops:
  0.6 59.6 %windows.1 = (bf16[12,2,18432]{2,1,0:T(2,128)(2,1)}, bf16[12,2,18432]{2,1,0:T(2,128)(2,1)}, bf16[16,16,640]{2,1,0:T(8,128)(2,1)}, bf16[8,16,512]{2,1,0:T(8,128)(2,1)}, f32[16,8,128]{2,1,0:T(8,128)}) custom-call(bf16[12,2,18432]{2,1,0:T(2,128)(2,1)} %bitcast.8, bf16[12,2,18432]{2,1,0:T(2,128)(2,1)} %bitcast.9, f32[1,192]{1,0:T(1,128)} %bitcast.11, ...), custom_call_target="tpu_custom_call" | custom-call | tf_op jit(solution)/shard_map/windows/pallas_call | solution.py:846
  60.2 2.9 %finish.1 = (bf16[12,2,18432]{2,1,0:T(2,128)(2,1)}, bf16[12,2,18432]{2,1,0:T(2,128)(2,1)}, f32[192,576]{1,0:T(8,128)}, f32[192,192]{1,0:T(8,128)}, f32[6,2,3312]{2,1,0:T(2,128)}) custom-call(bf16[12,2,18432]{2,1,0:T(2,128)(2,1)} %get-tuple-element.15.x, bf16[12,2,18432]{2,1,0:T(2,128)(2,1)} %get-tuple-element.16.g, ...), custom_call_target="tpu_custom_call" | custom-call | tf_op jit(solution)/shard_map/finish/pallas_call | solution.py:825
